TPU v7x, 32 devices: a whole 2x2x4 slice. The times are simulated.
32 devices in a mesh: seq: 8 (over z, y), fsdp: 4 (over x, core).
Axes of the slice: x: 2, y: 2, z: 4, core: 2. Of those that a mesh axis runs over, the one named last changes fastest.
Arguments:
- inputs: bfloat16 [4, 1024, 3584], P('fsdp', 'seq'), may hold values from -36 to 36
- keys_queries: bfloat16 [4, 1024, 256], P('fsdp', 'seq'), may hold values from -0.29882812 to 0.29882812
- log_decay: float32 [4, 56, 1024], P('fsdp', None, 'seq'), may hold values from -1.5 to 0, as said below
- skip: float32 [56], replicated, may hold values from 0.5 to 1.5
- classifier: bfloat16 [3584, 128], P('fsdp'), may hold values from -0.09375 to 0.09375
Outputs:
- mixed: bfloat16 [4, 1024, 3584], P('fsdp', 'seq')
- logits: float32 [4, 128], P('fsdp')
Inputs may be any that keep to these rules, and one draw needn't show every extreme that they name: `log_decay`: log-decays are negative.
All inputs are finite; a program needn't handle non-finite values.
Results may differ from a plain program's by a relative error of at most 0.0051.
Values may be sent and summed in bfloat16 or wider, within the bound.
No kernel may reach another device: no remote copies, remote signals or barrier semaphores. Data moves between devices by JAX's collectives and lax.ppermute only.
A program may use at most 256 MiB of HBM per device.

v0:
```python
import jax
import jax.numpy as jnp
from jax import lax
from jax.sharding import PartitionSpec as P

N = 128
GROUP = 128


epsilon = 1e-06


def linker(earlier, latter):
    return (earlier[0] + latter[0], jnp.exp(latter[0]) * earlier[1] + latter[1])


def local(inputs, keys_queries, log_decay, skip, classifier):
    copies, positions, channels = inputs.shape
    head_count = log_decay.shape[1]
    head_dim = channels // head_count
    blocks = positions // GROUP
    key_rows = keys_queries[:, :, :N].reshape(copies, blocks, GROUP, N)
    queries = keys_queries[:, :, N:].reshape(copies, blocks, GROUP, N)
    values = inputs.reshape(copies, blocks, GROUP, head_count, head_dim)
    cumulative = jnp.cumsum(log_decay.reshape(copies, head_count, blocks, GROUP), axis=-1)
    block_decay = cumulative[..., -1]
    weighted = (key_rows[:, None] * jnp.exp(block_decay[..., None] - cumulative)[..., None]).astype(
        jnp.bfloat16
    )
    block_state = jnp.einsum(
        "chkun,ckuhp->kchnp", weighted, values, preferred_element_type=jnp.float32
    )

    def advance(running, member):
        return (jnp.exp(member[0])[..., None, None] * running + member[1], running)

    device_state, starts = lax.scan(
        advance, jnp.zeros_like(block_state[0]), (jnp.moveaxis(block_decay, 2, 0), block_state)
    )
    device_decay = jnp.sum(block_decay, axis=-1)
    axis_count = lax.axis_size("seq")
    flattened = device_state.reshape(copies, head_count, 1, N * head_dim)
    decay_copies = jnp.broadcast_to(
        device_decay[:, :, None, None], (copies, head_count, 1, axis_count)
    )
    totals = lax.associative_scan(
        linker,
        (
            lax.all_to_all(decay_copies, "seq", split_axis=3, concat_axis=2, tiled=True),
            lax.all_to_all(flattened, "seq", split_axis=3, concat_axis=2, tiled=True),
        ),
        axis=2,
    )[1]
    shifted = jnp.concatenate([jnp.zeros_like(totals[:, :, :1]), totals[:, :, :-1]], axis=2)
    incoming = lax.all_to_all(shifted, "seq", split_axis=2, concat_axis=3, tiled=True)
    incoming = incoming.reshape(copies, head_count, N, head_dim)
    preceding = jnp.moveaxis(jnp.cumsum(block_decay, axis=-1) - block_decay, 2, 0)
    carried = (jnp.exp(preceding)[..., None, None] * incoming[None] + starts).astype(jnp.bfloat16)
    growth = jnp.exp(cumulative).transpose(0, 2, 3, 1)[..., None]
    carried_out = (
        jnp.einsum("ckqn,kchnp->ckqhp", queries, carried, preferred_element_type=jnp.float32)
        * growth
    )
    causal = jnp.arange(GROUP)[:, None] >= jnp.arange(GROUP)[None, :]
    scores = jnp.einsum("cktn,ckun->cktu", queries, key_rows, preferred_element_type=jnp.float32)
    decay_gap = jnp.where(causal, cumulative[..., :, None] - cumulative[..., None, :], -jnp.inf)
    mixing = (scores[:, None] * jnp.exp(decay_gap)).astype(jnp.bfloat16)
    diagonal = jnp.einsum("chktu,ckuhp->ckthp", mixing, values, preferred_element_type=jnp.float32)
    mixed_full = diagonal + carried_out + skip[:, None] * values.astype(jnp.float32)
    mixed = mixed_full.astype(jnp.bfloat16).reshape(copies, positions, channels)
    partial_sum = jnp.sum(mixed_full, axis=(1, 2)).reshape(copies, channels)
    pooled = lax.psum(partial_sum, "seq") / (positions * lax.axis_size("seq"))
    normed = (
        pooled / jnp.sqrt(jnp.mean(pooled * pooled, axis=-1, keepdims=True) + epsilon)
    ).astype(jnp.bfloat16)
    logits = jnp.dot(
        normed,
        lax.all_gather(classifier, "fsdp", axis=0, tiled=True),
        preferred_element_type=jnp.float32,
    )
    return (mixed, logits)


def solution(mesh):
    return jax.shard_map(
        local,
        mesh=mesh,
        in_specs=(
            P("fsdp", "seq", None),
            P("fsdp", "seq", None),
            P("fsdp", None, "seq"),
            P(),
            P("fsdp", None),
        ),
        out_specs=(P("fsdp", "seq", None), P("fsdp", None)),
        check_vma=False,
    )
```

profile of v0, /device:TPU:0, one launch (start us, length us, event | category | flops | bytes accessed | tf_op | source)
XLA Modules:
  0.0 249.8 jit_solution(8624898215858328479)
XLA Ops:
  0.6 0.0 copy-start.7
  0.6 1.1 reduce_window_sum.17
  1.7 0.2 multiply_reduce_fusion
  1.9 0.6 broadcast_in_dim.18
  2.5 7.3 %all-to-all-start.1 = ((f32[1,56,1,8]{1,2,0,3:T(1,128)}), f32[1,56,1,8]{1,2,0,3:T(1,128)S(1)}, u32[]{:S(2)}, u32[]{:S(2)}) async-start(f32[1,56,1,8]{1,2,0,3:T(1,128)} %broadcast_in_dim.18), calls=%async_computation.1 | async-start | bytes 8192 | tf_op jit(solution)/shard_map/all_to_all | solution.py:49
  9.8 0.1 subtract_exponential_fusion
  9.9 1.6 copy.33
  11.4 0.0 copy-done.7
  11.4 0.0 copy-start.4
  11.5 1.3 fusion.10
  12.7 4.5 %copy.45 = f32[56,128,64]{0,2,1:T(8,128)} copy(f32[56,128,64]{1,2,0:T(8,128)S(1)} %fusion.10) | data formatting | bytes 3670016 | tf_op jit(solution)/shard_map/reshape | solution.py:42
  17.3 0.0 copy-done.4
  17.3 0.5 broadcast.98
  17.8 38.4 %reduce.6 = f32[8192,56]{1,0:T(8,128)} reduce(f32[8192,1,1,56]{3,2,1,0:T(1,128)} %bitcast.64, f32[]{:T(128)} %broadcast.98), dimensions={1,2}, to_apply=%bitcast.53.reduce_sub_computation | reduce | bytes 3670020
  56.1 8.0 %reshape.233 = f32[8,1,57344]{2,1,0:T(1,128)} reshape(f32[8192,56]{1,0:T(8,128)} %reduce.6) | data formatting | bytes 3670016
  64.2 0.0 all-to-all-done.1
  64.2 6.0 %all-to-all-start = ((f32[8,1,57344]{2,1,0:T(1,128)}), f32[8,1,57344]{2,1,0:T(1,128)S(1)}, u32[]{:S(2)}, u32[]{:S(2)}) async-start(f32[8,1,57344]{2,1,0:T(1,128)} %reshape.233), calls=%async_computation | async-start | bytes 3670016 | tf_op jit(solution)/shard_map/all_to_all | solution.py:50
  70.3 41.9 %all-to-all-done = f32[8,1,57344]{2,1,0:T(1,128)S(1)} async-done(((f32[8,1,57344]{2,1,0:T(1,128)}), f32[8,1,57344]{2,1,0:T(1,128)S(1)}, u32[]{:S(2)}, u32[]{:S(2)}) %all-to-all-start) | async-done | bytes 1835040 | tf_op jit(solution)/shard_map/all_to_all | solution.py:50
  112.2 7.0 %reduce.7 = f32[8,57344]{1,0:T(8,128)} reduce(f32[8,1,57344]{2,1,0:T(1,128)S(1)} %all-to-all-done, f32[]{:T(128)} %broadcast.98), dimensions={1}, to_apply=%all_to_all.10.reduce_sub_computation | reduce | bytes 3670020 | tf_op jit(solution)/shard_map/all_to_all | solution.py:50
  119.3 12.9 %reshape.234 = f32[8192,1,1,56]{3,2,1,0:T(1,128)} reshape(f32[8,57344]{1,0:T(8,128)} %reduce.7) | data formatting | bytes 3670016
  132.2 4.0 %fusion.31 = (f32[1,56,4,1024]{1,3,2,0:T(8,128)}, f32[1,56,4,1024]{1,3,2,0:T(8,128)S(1)}) fusion(f32[1,56,8,1024]{1,3,2,0:T(8,128)} %bitcast.61), kind=kLoop, calls=%fused_computation.58 | loop fusion | bytes 3670016 | tf_op jit(solution)/shard_map/slice | solution.py:46
  136.2 0.0 copy-done
  136.2 1.2 slice.96
  137.4 0.8 slice.99
  138.3 2.2 copy.48
  140.4 1.7 copy.49
  142.2 1.3 multiply_add_fusion
  143.5 0.1 slice_add_fusion
  143.6 0.1 slice_add_fusion.1
  143.8 0.1 fusion.33
  143.9 0.1 pad.22
  144.0 0.1 pad.23
  144.1 1.0 add.78
  145.1 4.6 %pad.49 = f32[1,56,8,1024]{3,1,0,2:T(8,128)} pad(f32[1,56,4,1024]{3,1,0,2:T(8,128)} %add.78, f32[]{:T(128)} %constant.16.clone.1), padding=0_0_0x0_0_0x1_0_1x0_0_0 | pad | bytes 2752516
  149.7 0.0 copy-done.3
  149.7 1.3 copy.50
  151.0 1.2 copy.47
  152.2 1.2 fusion.11
  153.5 0.0 copy-start.2
  153.5 1.0 pad_maximum_fusion
  154.5 2.2 pad.31
  156.6 0.0 copy-done.2
  156.7 0.3 slice_add_fusion.2
  156.9 1.5 concatenate.11
  158.4 3.6 %all-to-all-start.2 = ((f32[1,56,8,1024]{3,1,0,2:T(8,128)}), f32[1,56,8,1024]{3,1,0,2:T(8,128)S(1)}, u32[]{:S(2)}, u32[]{:S(2)}) async-start(f32[1,56,8,1024]{3,1,0,2:T(8,128)} %concatenate.11), calls=%async_computation.2 | async-start | bytes 3670016 | tf_op jit(solution)/shard_map/all_to_all | solution.py:55
  162.0 2.6 %copy.42 = f32[1,128,3584]{1,2,0:T(8,128)} copy(bf16[1,128,3584]{2,1,0:T(8,128)(2,1)} %param.5) | data formatting | bytes 2752512 | tf_op jit(solution)/shard_map/convert_element_type | solution.py:69
  164.6 0.1 fusion.16
  164.8 0.0 copy-done.5
  164.8 0.0 copy-start.8
  164.8 2.6 %fusion = f32[56,128,64]{1,2,0:T(8,128)} fusion(bf16[128,56,64]{0,2,1:T(8,128)(2,1)S(1)} %bitcast.68, f32[56,128]{1,0:T(8,128)S(1)} %bitcast.69, f32[128,128]{1,0:T(8,128)S(1)} %fusion.16, pred[128,128]{1,0:T(8,128)(4,1)S(1)} %iota_compare_fusion), kind=kOutput, calls=%fused_computation.2 | convolution fusion | flops 121110528 | bytes 2863104 | tf_op jit(solution)/shard_map/chktu,ckuhp->ckthp/dot_general | solution.py:68
  167.4 0.0 copy-done.8
  167.4 9.7 %all_gather.3 = bf16[3584,128]{1,0:T(8,128)(2,1)} all-gather(bf16[896,128]{1,0:T(8,128)(2,1)S(1)} %copy-done.8), channel_id=1, replica_groups=mesh['seq'=8,'fsdp'=4] {'fsdp'}, dimensions={0}, use_global_device_ids=true | all-gather | bytes 1146880 | tf_op jit(solution)/shard_map/all_gather | solution.py:78
  177.1 27.7 %all-to-all-done.2 = f32[1,56,8,1024]{3,1,0,2:T(8,128)S(1)} async-done(((f32[1,56,8,1024]{3,1,0,2:T(8,128)}), f32[1,56,8,1024]{3,1,0,2:T(8,128)S(1)}, u32[]{:S(2)}, u32[]{:S(2)}) %all-to-all-start.2) | async-done | bytes 1835040 | tf_op jit(solution)/shard_map/all_to_all | solution.py:55
  204.8 0.3 multiply_convert_fusion.4
  205.1 0.5 copy.40
  205.6 0.0 copy-start.1
  205.6 0.0 copy-start.9
  205.6 2.1 convert_element_type.57
  207.7 3.3 %fusion.32 = (f32[56,64]{1,0:T(8,128)S(1)}, bf16[1,1,128,56,64]{2,4,3,1,0:T(8,128)(2,1)S(1)}) fusion(f32[1,1,128,56,64]{2,4,3,1,0:T(8,128)S(1)} %bitcast.65, f32[56]{0:T(128)S(1)} %copy-done.9, f32[128,56]{0,1:T(8,128)S(1)} %exponential_bitcast_fusion, bf16[56,128,64]{2,1,0:T(8,128)(2,1)} %convert_element_type.57, bf16[1,128,256]{2,1,0:T(8,128)(2,1)S(1)} %copy-done.7, ...), kind=kOutput, calls=%fused_computation.59 | convolution fusion | flops 120189440 | bytes 5581312 | tf_op jit(solution)/shard_map/ckqn,kchnp->ckqhp/dot_general | solution.py:61
  211.0 0.1 reshape.224
  211.1 35.3 %psum.7 = f32[1,3584]{1,0:T(1,128)S(1)} all-reduce(f32[1,3584]{1,0:T(1,128)S(1)} %reshape.224), channel_id=1, replica_groups=mesh['seq'=8,'fsdp'=4] {'seq'}, use_global_device_ids=true, to_apply=%region_2.3 | all-reduce | flops 3584 | bytes 28672 | tf_op jit(solution)/shard_map/psum | solution.py:72
  246.4 0.6 multiply_reduce_fusion.1
  247.8 1.3 copy.43
  249.1 0.7 fusion.22
  (23 shorter events, 0.3 us)
Async XLA Ops:
  0.6 10.8 %copy-start.7 = (bf16[1,128,256]{2,1,0:T(8,128)(2,1)S(1)}, bf16[1,128,256]{2,1,0:T(8,128)(2,1)}, u32[]{:S(2)}) copy-start(bf16[1,128,256]{2,1,0:T(8,128)(2,1)} %param.6) | copy-start | bytes 196612
  2.5 61.7 %all-to-all-start.1 = ((f32[1,56,1,8]{1,2,0,3:T(1,128)}), f32[1,56,1,8]{1,2,0,3:T(1,128)S(1)}, u32[]{:S(2)}, u32[]{:S(2)}) async-start(f32[1,56,1,8]{1,2,0,3:T(1,128)} %broadcast_in_dim.18), calls=%async_computation.1 | async-start | bytes 8192 | tf_op jit(solution)/shard_map/all_to_all | solution.py:49
  11.4 5.8 %copy-start.4 = (bf16[1,128,3584]{1,2,0:T(8,128)(2,1)}, bf16[1,128,3584]{1,2,0:T(8,128)(2,1)S(1)}, u32[]{:S(2)}) copy-start(bf16[1,128,3584]{1,2,0:T(8,128)(2,1)S(1)} %copy.33) | copy-start | bytes 2752516
  64.2 48.1 %all-to-all-start = ((f32[8,1,57344]{2,1,0:T(1,128)}), f32[8,1,57344]{2,1,0:T(1,128)S(1)}, u32[]{:S(2)}, u32[]{:S(2)}) async-start(f32[8,1,57344]{2,1,0:T(1,128)} %reshape.233), calls=%async_computation | async-start | bytes 3670016 | tf_op jit(solution)/shard_map/all_to_all | solution.py:50
  132.2 4.0 %copy-start = (f32[8192,1,1,56]{3,2,1,0:T(1,128)S(1)}, f32[8192,1,1,56]{3,2,1,0:T(1,128)}, u32[]{:S(2)}) copy-start(f32[8192,1,1,56]{3,2,1,0:T(1,128)} %reshape.234) | copy-start | bytes 5505028
  145.1 4.6 %copy-start.3 = (f32[1,56,3,1024]{1,3,2,0:T(8,128)S(1)}, f32[1,56,3,1024]{1,3,2,0:T(8,128)}, u32[]{:S(2)}) copy-start(f32[1,56,3,1024]{1,3,2,0:T(8,128)} %slice.96) | copy-start | bytes 2064388
  153.5 3.2 %copy-start.2 = (f32[1,56,8,1024]{3,1,0,2:T(8,128)S(1)}, f32[1,56,8,1024]{3,1,0,2:T(8,128)}, u32[]{:S(2)}) copy-start(f32[1,56,8,1024]{3,1,0,2:T(8,128)} %pad.49) | copy-start | bytes 5505028
  158.4 46.4 %all-to-all-start.2 = ((f32[1,56,8,1024]{3,1,0,2:T(8,128)}), f32[1,56,8,1024]{3,1,0,2:T(8,128)S(1)}, u32[]{:S(2)}, u32[]{:S(2)}) async-start(f32[1,56,8,1024]{3,1,0,2:T(8,128)} %concatenate.11), calls=%async_computation.2 | async-start | bytes 3670016 | tf_op jit(solution)/shard_map/all_to_all | solution.py:55
  162.0 2.7 %copy-start.5 = (bf16[1,128,3584]{1,2,0:T(8,128)(2,1)S(1)}, bf16[1,128,3584]{1,2,0:T(8,128)(2,1)}, u32[]{:S(2)}) copy-start(bf16[1,128,3584]{1,2,0:T(8,128)(2,1)} %copy-done.4) | copy-start | bytes 2752516
  164.8 2.6 %copy-start.8 = (bf16[896,128]{1,0:T(8,128)(2,1)S(1)}, bf16[896,128]{1,0:T(8,128)(2,1)}, u32[]{:S(2)}) copy-start(bf16[896,128]{1,0:T(8,128)(2,1)} %param.9) | copy-start | bytes 688132
  205.6 2.1 copy-start.1
  205.6 2.1 copy-start.9
  211.0 38.0 %copy-start.6 = (bf16[3584,128]{1,0:T(8,128)(2,1)S(1)}, bf16[3584,128]{1,0:T(8,128)(2,1)}, u32[]{:S(2)}) copy-start(bf16[3584,128]{1,0:T(8,128)(2,1)} %all_gather.3) | copy-start | bytes 2752516
where the time goes:
time: 251 us; the launch traced here: 250 us
  waiting for transfers between devices  69.6 us (28%)
  local copies, waits for them, and re-layouts  55.8 us (22%)
  other arithmetic  52.9 us (21%)
  blocking collectives  45.1 us (18%)
  starting transfers between devices  16.9 us (7%)
  matrix products  7.98 us (3%)
    all_to_all x1, waiting for transfers between devices, local(): lax.all_to_all(flattened, 'seq', split_axis=3, concat_axis=2, tiled=True)  41.9 us
    unnamed x1, other arithmetic  38.4 us
    unnamed x30, local copies, waits for them, and re-layouts  35.3 us
    psum x1, blocking collectives, local(): pooled = lax.psum(partial_sum, 'seq') / (positions * lax.axis_size('seq'))  35.3 us
    all_to_all x1, waiting for transfers between devices, local(): lax.all_to_all(shifted, 'seq', split_axis=2, concat_axis=3, tiled=True)  27.7 us
    all_gather x1, blocking collectives, local(): lax.all_gather(classifier, 'fsdp', axis=0, tiled=True)  9.75 us
    all_to_all x1, starting transfers between devices, local(): lax.all_to_all(decay_copies, 'seq', split_axis=3, concat_axis=2, tiled=True)  7.28 us
    all_to_all x1, other arithmetic, local(): lax.all_to_all(flattened, 'seq', split_axis=3, concat_axis=2, tiled=True)  7.03 us
  transfers between devices with their start and end apart: 3, of which 2 were waited for; matrix products, arithmetic and copies ran while one was open for 24% of the time, Pallas kernels for 0%

commit v1 on v0

v1 whole, which is shorter than its diff:
```python
import functools
import jax
import jax.numpy as jnp
from jax import lax
from jax.experimental import pallas as pl
from jax.experimental.pallas import tpu as pltpu
from jax.sharding import PartitionSpec as P

N = 128
GROUP = 128
AUX = 16

epsilon = 1e-06

F32 = jnp.float32
BF16 = jnp.bfloat16
HIGHEST = lax.Precision.HIGHEST
LIMIT = 48 * 1024 * 1024

VMEM = pl.BlockSpec(memory_space=pltpu.VMEM)
SMEM = pl.BlockSpec(memory_space=pltpu.SMEM)


def dot(a, b, contract=((1,), (0,)), precision=None):
    return lax.dot_general(a, b, (contract, ((), ())), preferred_element_type=F32, precision=precision)


def iota(shape, dim):
    return lax.broadcasted_iota(jnp.int32, shape, dim)


def split(x):
    high = x.astype(BF16)
    return high, (x - high.astype(F32)).astype(BF16)


def cumulative_by_position(log_decay):
    upto = (iota((GROUP, GROUP), 1) <= iota((GROUP, GROUP), 0)).astype(F32)
    return dot(upto, log_decay, ((1,), (1,)), HIGHEST)


def cumulative_by_head(log_decay):
    upto = (iota((GROUP, GROUP), 0) <= iota((GROUP, GROUP), 1)).astype(F32)
    return dot(log_decay, upto, precision=HIGHEST)


def spread(x, first_head, lanes, head_dim):
    heads = x.shape[1]
    member = (iota((heads, lanes), 0) == first_head + iota((heads, lanes), 1) // head_dim).astype(BF16)
    high, low = split(x)
    return dot(high, member) + dot(low, member)


def state_kernel(head_dim, place, kq, values, log_decay, *parts):
    lanes = parts[0].shape[1]
    part_heads = lanes // head_dim
    ld = log_decay[...]
    by_position = cumulative_by_position(ld)
    decay_left = jnp.exp(by_position[GROUP - 1 :, :] - by_position)
    by_head = cumulative_by_head(ld)
    block_decay = jnp.exp(jnp.broadcast_to(by_head[:, GROUP - 1 :], by_head.shape))
    keys = jnp.transpose(kq[:, :N])
    for m, part in enumerate(parts):
        owner = place[0] ^ m
        start = pl.multiple_of(owner * lanes, 128)
        wide = spread(decay_left, owner * part_heads, lanes, head_dim)
        weighted = (values[:, pl.ds(start, lanes)].astype(F32) * wide).astype(BF16)
        part[pl.ds(0, N), :] = dot(keys, weighted).astype(BF16)
        chooser = (iota((AUX, ld.shape[0]), 1) == owner * part_heads + iota((AUX, ld.shape[0]), 0)).astype(F32)
        mine = dot(chooser, block_decay, precision=HIGHEST)
        high, low = split(mine)
        part[pl.ds(N, AUX), pl.ds(0, 128)] = high
        part[pl.ds(N, AUX), pl.ds(128, 128)] = low
        part[pl.ds(N, AUX), pl.ds(256, lanes - 256)] = jnp.zeros((AUX, lanes - 256), BF16)


def gather_parts(place, parts, ordered):
    for m, part in enumerate(parts):
        ordered[place[0] ^ m] = part[...]


def part_decay(block, lanes, head_dim):
    aux = block[N:, :]
    factor = aux[:, :128].astype(F32) + aux[:, 128:256].astype(F32)
    per = 128 // head_dim
    pieces = []
    lane = iota((1, 128), 1) // head_dim
    for i in range(lanes // 128):
        piece = factor[i * per : i * per + 1]
        for j in range(1, per):
            piece = jnp.where(lane == j, factor[i * per + j : i * per + j + 1], piece)
        pieces.append(piece)
    return jnp.concatenate(pieces, axis=1)


def total_kernel(head_dim, place, *refs):
    *parts, total, decay, ordered = refs
    lanes = total.shape[1]
    gather_parts(place, parts, ordered)
    running = ordered[0][:N].astype(F32)
    factor = part_decay(ordered[0], lanes, head_dim)
    for j in range(1, len(parts)):
        here = part_decay(ordered[j], lanes, head_dim)
        running = here * running + ordered[j][:N].astype(F32)
        factor = factor * here
    total[...] = running.astype(BF16)
    decay[...] = factor


def starts_kernel(head_dim, place, before, *refs):
    count = (len(refs) - 2) // 2
    parts, outs, ordered, results = refs[:count], refs[count : 2 * count], refs[-2], refs[-1]
    lanes = before.shape[1]
    gather_parts(place, parts, ordered)
    running = before[...].astype(F32)
    for j in range(count):
        results[j] = running.astype(BF16)
        if j < count - 1:
            running = part_decay(ordered[j], lanes, head_dim) * running + ordered[j][:N].astype(F32)
    for m, out in enumerate(outs):
        out[...] = results[place[0] ^ m]


def block_kernel(head_dim, kq, values, log_decay, skip, out):
    ld = log_decay[...]
    by_position = cumulative_by_position(ld)
    by_head = cumulative_by_head(ld)
    scores = dot(kq[:, N:], kq[:, :N], ((1,), (1,)))
    causal = iota((GROUP, GROUP), 0) >= iota((GROUP, GROUP), 1)
    per = 128 // head_dim
    lane = iota((GROUP, 128), 1) // head_dim
    lane_row = iota((1, 128), 1) // head_dim
    for i in range(values.shape[1] // 128):
        value = values[:, i * 128 : (i + 1) * 128]
        mixes, tops = [], []
        direct = jnp.zeros((1, 128), F32)
        for j in range(per):
            h = i * per + j
            gap = by_position[:, h : h + 1] - by_head[h : h + 1, :]
            mixes.append((scores * jnp.exp(jnp.where(causal, gap, -jnp.inf))).astype(BF16))
            tops.append(jnp.where(lane == j, value, jnp.zeros_like(value)))
            direct = jnp.where(lane_row == j, skip[h], direct)
        mixed = dot(jnp.concatenate(mixes, axis=1), jnp.concatenate(tops, axis=0))
        out[:, i * 128 : (i + 1) * 128] = mixed + direct * value.astype(F32)


def output_kernel(head_dim, place, kq, log_decay, local, *refs):
    *carried, mixed, pooled = refs
    lanes = carried[0].shape[1]
    part_heads = lanes // head_dim
    growth = jnp.exp(cumulative_by_position(log_decay[...]))
    queries = kq[:, N:]
    for m, state in enumerate(carried):
        owner = place[0] ^ m
        at = pl.ds(pl.multiple_of(owner * lanes, 128), lanes)
        wide = spread(growth, owner * part_heads, lanes, head_dim)
        full = local[:, at] + wide * dot(queries, state[...])
        mixed[:, at] = full.astype(BF16)
        pooled[:, at] = jnp.sum(full, axis=0, keepdims=True)


def call(kernel, outs, in_specs, scratch=(), flops=0, moved=0):
    return pl.pallas_call(
        kernel,
        out_shape=outs,
        in_specs=in_specs,
        out_specs=jax.tree.map(lambda _: VMEM, outs),
        scratch_shapes=scratch,
        cost_estimate=pl.CostEstimate(flops=flops, bytes_accessed=moved, transcendentals=0),
        compiler_params=pltpu.CompilerParams(vmem_limit_bytes=LIMIT),
    )


def local(inputs, keys_queries, log_decay, skip, classifier):
    _, positions, channels = inputs.shape
    heads = log_decay.shape[1]
    head_dim = channels // heads
    size = lax.axis_size("seq")
    group = 4
    lanes = channels // group
    index = lax.axis_index("seq")
    place = (index % group).astype(jnp.int32).reshape(1)
    values, kq, ld = inputs[0], keys_queries[0], log_decay[0]
    part = jax.ShapeDtypeStruct((N + AUX, lanes), BF16)
    state = jax.ShapeDtypeStruct((N, lanes), BF16)

    def swap(x, m):
        return lax.ppermute(x, "seq", [(i, i ^ m) for i in range(size)])

    def shift(x, by):
        return lax.ppermute(x, "seq", [(i, i + by) for i in range(size - by)])

    parts = call(
        functools.partial(state_kernel, head_dim),
        [part] * group,
        [SMEM] + [VMEM] * 3,
        flops=2 * positions * N * channels,
        moved=4 * positions * channels,
    )(place, kq, values, ld)
    parts = [parts[0]] + [swap(parts[m], m) for m in range(1, group)]

    from_block = call(
        functools.partial(block_kernel, head_dim),
        jax.ShapeDtypeStruct((positions, channels), F32),
        [VMEM] * 3 + [SMEM],
        flops=8 * positions * N * channels,
        moved=6 * positions * channels,
    )(kq, values, ld, skip)
    gathered = lax.all_gather(classifier, "fsdp", axis=0, tiled=True)

    total, decay = call(
        functools.partial(total_kernel, head_dim),
        [state, jax.ShapeDtypeStruct((1, lanes), F32)],
        [SMEM] + [VMEM] * group,
        [pltpu.VMEM((group, N + AUX, lanes), BF16)],
    )(place, *parts)
    before = shift(total, group)
    if size > 2 * group:
        before, decay = before.astype(F32), shift(decay, group)
        reach = 1
        while reach < size // group - 1:
            before = before + decay * shift(before, group * reach)
            decay = decay * shift(decay, group * reach)
            reach *= 2
        before = before.astype(BF16)
    starts = call(
        functools.partial(starts_kernel, head_dim),
        [state] * group,
        [SMEM] + [VMEM] * (group + 1),
        [pltpu.VMEM((group, N + AUX, lanes), BF16), pltpu.VMEM((group, N, lanes), BF16)],
    )(place, before, *parts)
    starts = [starts[0]] + [swap(starts[m], m) for m in range(1, group)]
    mixed, pooled = call(
        functools.partial(output_kernel, head_dim),
        [jax.ShapeDtypeStruct((positions, channels), BF16), jax.ShapeDtypeStruct((1, channels), F32)],
        [SMEM] + [VMEM] * (3 + group),
    )(place, kq, ld, from_block, *starts)

    reach = 1
    while reach < size:
        pooled = pooled + swap(pooled, reach)
        reach *= 2
    pooled = pooled / (positions * size)
    normed = (pooled / jnp.sqrt(jnp.mean(pooled * pooled, axis=-1, keepdims=True) + epsilon)).astype(BF16)
    logits = jnp.dot(normed, gathered, preferred_element_type=F32)
    return mixed[None], logits


def solution(mesh):
    return jax.shard_map(
        local,
        mesh=mesh,
        in_specs=(
            P("fsdp", "seq", None),
            P("fsdp", "seq", None),
            P("fsdp", None, "seq"),
            P(),
            P("fsdp", None),
        ),
        out_specs=(P("fsdp", "seq", None), P("fsdp", None)),
        check_vma=False,
    )
```

time: 251 us -> 73.8 us (0.29)
  local copies, waits for them, and re-layouts: 55.8 us -> 2.78 us
  other arithmetic: 52.9 us -> 0.66 us
  waiting for transfers between devices: 69.6 us -> 27.4 us
  blocking collectives: 45.1 us -> 9.29 us
  Pallas kernels: 0 us -> 7.34 us
  matrix products: 7.98 us -> 0.75 us
  starting transfers between devices: 16.9 us -> 23.9 us
    all_to_all x3 -> x0, waiting for transfers between devices: 69.6 us -> none  [the longest x1 41.9 us: local(): lax.all_to_all(flattened, 'seq', split_axis=3, concat_axis=2, tiled=True)]
    unnamed x1 -> x0, other arithmetic: 38.4 us -> none
    psum x1 -> x0, blocking collectives: 35.3 us -> none  [local(): pooled = lax.psum(partial_sum, 'seq') / (positions * lax.axis_size('seq'))]
    unnamed x30 -> x14, local copies, waits for them, and re-layouts: 35.3 us -> 2.78 us
    ppermute x0 -> x10, waiting for transfers between devices: none -> 27.4 us  [the longest x9 23.7 us: swap(): return lax.ppermute(x, 'seq', [(i, i ^ m) for i in range(size)])]
    ppermute x0 -> x10, starting transfers between devices: none -> 23.9 us  [the longest x9 19.3 us: swap(): return lax.ppermute(x, 'seq', [(i, i ^ m) for i in range(size)])]
    all_to_all x3 -> x0, starting transfers between devices: 16.9 us -> none  [the longest x1 7.28 us: local(): lax.all_to_all(decay_copies, 'seq', split_axis=3, concat_axis=2, tiled=True)]
    slice x9 -> x0, local copies, waits for them, and re-layouts: 8.34 us -> none  [the longest x8 6.19 us: local(): lax.associative_scan(linker, (lax.all_to_all(decay_copies, 'seq', split_a...]
  transfers between devices with their start and end apart: 3 -> 10, of which waited for: 2 -> 8; matrix products, arithmetic and copies ran while one was open for 24% -> 0% of each run, Pallas kernels for 0% -> 3%
where the time goes in v1:
time: 73.8 us; the launch traced here: 73.6 us
  waiting for transfers between devices  27.4 us (37%)
  starting transfers between devices  23.9 us (32%)
  blocking collectives  9.29 us (13%)
  Pallas kernels  7.34 us (10%)
  local copies, waits for them, and re-layouts  2.78 us (4%)
  between operations  1.42 us (2%)
  matrix products  0.75 us (1%)
    ppermute x9, waiting for transfers between devices, swap(): return lax.ppermute(x, 'seq', [(i, i ^ m) for i in range(size)])  23.7 us
    ppermute x9, starting transfers between devices, swap(): return lax.ppermute(x, 'seq', [(i, i ^ m) for i in range(size)])  19.3 us
    all_gather x1, blocking collectives, local(): gathered = lax.all_gather(classifier, 'fsdp', axis=0, tiled=True)  9.29 us
    ppermute x1, starting transfers between devices, shift(): return lax.ppermute(x, 'seq', [(i, i + by) for i in range(size - by)])  4.64 us
    ppermute x1, waiting for transfers between devices, shift(): return lax.ppermute(x, 'seq', [(i, i + by) for i in range(size - by)])  3.68 us
    unnamed x14, local copies, waits for them, and re-layouts  2.78 us
    pallas_call x1, Pallas kernels, local(): call(functools.partial(block_kernel, head_dim), jax.ShapeDtypeStruct((pos...  2.19 us
    pallas_call x1, Pallas kernels, local(): call(functools.partial(output_kernel, head_dim), [jax.ShapeDtypeStruct((p...  2.06 us
  transfers between devices with their start and end apart: 10, of which 8 were waited for; matrix products, arithmetic and copies ran while one was open for 0% of the time, Pallas kernels for 3%

profile of v1, /device:TPU:0, one launch (start us, length us, event | category | flops | bytes accessed | tf_op | source)
XLA Modules:
  0.0 73.6 jit_solution(15291467161070841354)
XLA Ops:
  0.6 0.0 copy-start.5
  0.7 0.0 copy-start
  0.7 1.2 %copy-done = bf16[1,128,3584]{2,1,0:T(8,128)(2,1)S(1)} copy-done((bf16[1,128,3584]{2,1,0:T(8,128)(2,1)S(1)}, bf16[1,128,3584]{2,1,0:T(8,128)(2,1)}, u32[]{:S(2)}) %copy-start) | copy-done | bytes 917528
  1.8 0.0 copy-start.2
  1.8 0.8 %copy-done.2 = bf16[1,128,256]{2,1,0:T(8,128)(2,1)S(1)} copy-done((bf16[1,128,256]{2,1,0:T(8,128)(2,1)S(1)}, bf16[1,128,256]{2,1,0:T(8,128)(2,1)}, u32[]{:S(2)}) %copy-start.2) | copy-done | bytes 65560
  2.7 0.0 copy-start.4
  2.7 0.7 %copy-done.4 = f32[1,56,128]{2,1,0:T(8,128)S(1)} copy-done((f32[1,56,128]{2,1,0:T(8,128)S(1)}, f32[1,56,128]{2,1,0:T(8,128)}, u32[]{:S(2)}) %copy-start.4) | copy-done | bytes 28696
  3.4 0.0 copy-start.1
  3.4 0.0 copy-start.3
  3.4 1.6 %shard_map.69 = (bf16[144,896]{1,0:T(8,128)(2,1)S(1)}, bf16[144,896]{1,0:T(8,128)(2,1)S(1)}, bf16[144,896]{1,0:T(8,128)(2,1)S(1)}, bf16[144,896]{1,0:T(8,128)(2,1)S(1)}) custom-call(s32[1]{0:T(128)} %bitcast.place, bf16[128,256]{1,0:T(8,128)(2,1)S(1)} %bitcast.12, bf16[128,3584]{1,0:T(8,128)(2,1)S(1)} %bitcast.10, f32[56,128]{1,0:T(8,128)S(1)} %bitcast.15), custom_call_target="tpu_custom_call" | custom-call | flops 117440512 | bytes 1835008 | tf_op jit(solution)/shard_map/pallas_call | solution.py:193
  5.1 3.0 %collective-permute-start = (bf16[144,896]{1,0:T(8,128)(2,1)S(1)}, bf16[144,896]{1,0:T(8,128)(2,1)S(1)}, u32[]{:S(2)}, u32[]{:S(2)}) collective-permute-start(bf16[144,896]{1,0:T(8,128)(2,1)S(1)} %get-tuple-element.14), channel_id=1, source_target_pairs={{0,4},{4,0},{8,12},{12,8},{16,20},{20,16},{24,28},{28,24},{1,5},{5... | collective-permute-start | bytes 774152 | tf_op jit(solution)/shard_map/ppermute | solution.py:188
  8.1 1.6 %collective-permute-start.1 = (bf16[144,896]{1,0:T(8,128)(2,1)S(1)}, bf16[144,896]{1,0:T(8,128)(2,1)S(1)}, u32[]{:S(2)}, u32[]{:S(2)}) collective-permute-start(bf16[144,896]{1,0:T(8,128)(2,1)S(1)} %get-tuple-element.15), channel_id=1, source_target_pairs={{0,8},{4,12},{8,0},{12,4},{16,24},{20,28},{24,16},{28,20},{1,9},{5... | collective-permute-start | bytes 774152 | tf_op jit(solution)/shard_map/ppermute | solution.py:188
  9.6 0.0 collective-permute-start.2
  9.6 4.6 %collective-permute-done.refs_1_ = bf16[144,896]{1,0:T(8,128)(2,1)S(1)} collective-permute-done((bf16[144,896]{1,0:T(8,128)(2,1)S(1)}, bf16[144,896]{1,0:T(8,128)(2,1)S(1)}, u32[]{:S(2)}, u32[]{:S(2)}) %collective-permute-start) | collective-permute-done | bytes 258080 | tf_op jit(solution)/shard_map/ppermute | solution.py:188
  14.3 2.9 %collective-permute-done.1.refs_2_ = bf16[144,896]{1,0:T(8,128)(2,1)S(1)} collective-permute-done((bf16[144,896]{1,0:T(8,128)(2,1)S(1)}, bf16[144,896]{1,0:T(8,128)(2,1)S(1)}, u32[]{:S(2)}, u32[]{:S(2)}) %collective-permute-start.1) | collective-permute-done | bytes 258080 | tf_op jit(solution)/shard_map/ppermute | solution.py:188
  17.2 3.9 %collective-permute-done.2.refs_3_ = bf16[144,896]{1,0:T(8,128)(2,1)S(1)} collective-permute-done((bf16[144,896]{1,0:T(8,128)(2,1)S(1)}, bf16[144,896]{1,0:T(8,128)(2,1)S(1)}, u32[]{:S(2)}, u32[]{:S(2)}) %collective-permute-start.2) | collective-permute-done | bytes 258080 | tf_op jit(solution)/shard_map/ppermute | solution.py:188
  21.1 1.0 %shard_map.70 = (bf16[128,896]{1,0:T(8,128)(2,1)S(1)}, f32[1,896]{1,0:T(1,128)}) custom-call(s32[1]{0:T(128)} %bitcast.place, bf16[144,896]{1,0:T(8,128)(2,1)S(1)} %get-tuple-element.13.refs_0_, bf16[144,896]{1,0:T(8,128)(2,1)S(1)} %collective-permute-done.refs_1_, bf16[144,896]{1,0:T(8,128)(2,1)S(1)} %collective-permute-done.1.refs_2_, ...), custom_call_target="tpu_custom_call" | custom-call | tf_op jit(solution)/shard_map/pallas_call | solution.py:211
  22.0 4.6 %collective-permute-start.3 = (bf16[128,896]{1,0:T(8,128)(2,1)S(1)}, bf16[128,896]{1,0:T(8,128)(2,1)S(1)}, u32[]{:S(2)}, u32[]{:S(2)}) collective-permute-start(bf16[128,896]{1,0:T(8,128)(2,1)S(1)} %get-tuple-element.17), channel_id=1, source_target_pairs={{0,16},{4,20},{8,24},{12,28},{1,17},{5,21},{9,25},{13,29},{2,18},{... | collective-permute-start | bytes 688136 | tf_op jit(solution)/shard_map/ppermute | solution.py:191
  26.7 3.7 %collective-permute-done.3.before = bf16[128,896]{1,0:T(8,128)(2,1)S(1)} collective-permute-done((bf16[128,896]{1,0:T(8,128)(2,1)S(1)}, bf16[128,896]{1,0:T(8,128)(2,1)S(1)}, u32[]{:S(2)}, u32[]{:S(2)}) %collective-permute-start.3) | collective-permute-done | bytes 229408 | tf_op jit(solution)/shard_map/ppermute | solution.py:191
  30.4 0.5 shard_map.71
  30.9 1.6 %collective-permute-start.4 = (bf16[128,896]{1,0:T(8,128)(2,1)S(1)}, bf16[128,896]{1,0:T(8,128)(2,1)S(1)}, u32[]{:S(2)}, u32[]{:S(2)}) collective-permute-start(bf16[128,896]{1,0:T(8,128)(2,1)S(1)} %get-tuple-element.19), channel_id=1, source_target_pairs={{0,4},{4,0},{8,12},{12,8},{16,20},{20,16},{24,28},{28,24},{1,5},{5... | collective-permute-start | bytes 688136 | tf_op jit(solution)/shard_map/ppermute | solution.py:188
  32.4 6.3 %collective-permute-start.5 = (bf16[128,896]{1,0:T(8,128)(2,1)S(1)}, bf16[128,896]{1,0:T(8,128)(2,1)S(1)}, u32[]{:S(2)}, u32[]{:S(2)}) collective-permute-start(bf16[128,896]{1,0:T(8,128)(2,1)S(1)} %get-tuple-element.20), channel_id=1, source_target_pairs={{0,8},{4,12},{8,0},{12,4},{16,24},{20,28},{24,16},{28,20},{1,9},{5... | collective-permute-start | bytes 688136 | tf_op jit(solution)/shard_map/ppermute | solution.py:188
  38.8 0.0 collective-permute-start.6
  38.8 0.0 copy-done.5
  38.8 0.0 copy-done.1
  38.8 0.0 copy-done.3
  38.8 2.2 %shard_map.68.local = f32[128,3584]{1,0:T(8,128)S(1)} custom-call(bf16[128,256]{1,0:T(8,128)(2,1)S(1)} %bitcast.13, bf16[128,3584]{1,0:T(8,128)(2,1)S(1)} %bitcast.11, f32[56,128]{1,0:T(8,128)S(1)} %bitcast.16, f32[56]{0:T(128)S(1)} %copy-done.5), custom_call_target="tpu_custom_call" | custom-call | flops 469762048 | bytes 2752512 | tf_op jit(solution)/shard_map/pallas_call | solution.py:202
  41.0 0.0 copy-start.6
  41.0 0.0 collective-permute-done.4.refs_1_
  41.0 4.2 %collective-permute-done.5.refs_2_ = bf16[128,896]{1,0:T(8,128)(2,1)S(1)} collective-permute-done((bf16[128,896]{1,0:T(8,128)(2,1)S(1)}, bf16[128,896]{1,0:T(8,128)(2,1)S(1)}, u32[]{:S(2)}, u32[]{:S(2)}) %collective-permute-start.5) | collective-permute-done | bytes 229408 | tf_op jit(solution)/shard_map/ppermute | solution.py:188
  45.2 3.9 %collective-permute-done.6.refs_3_ = bf16[128,896]{1,0:T(8,128)(2,1)S(1)} collective-permute-done((bf16[128,896]{1,0:T(8,128)(2,1)S(1)}, bf16[128,896]{1,0:T(8,128)(2,1)S(1)}, u32[]{:S(2)}, u32[]{:S(2)}) %collective-permute-start.6) | collective-permute-done | bytes 229408 | tf_op jit(solution)/shard_map/ppermute | solution.py:188
  49.1 2.1 %shard_map.72 = (bf16[128,3584]{1,0:T(8,128)(2,1)}, f32[1,3584]{1,0:T(1,128)S(1)}) custom-call(s32[1]{0:T(128)} %bitcast.place, bf16[128,256]{1,0:T(8,128)(2,1)S(1)} %bitcast.14, f32[56,128]{1,0:T(8,128)S(1)} %bitcast.17, f32[128,3584]{1,0:T(8,128)S(1)} %shard_map.68.local, bf16[128,896]{1,0:T(8,128)(2,1)S(1)} %get-tuple-element.18.refs_0_, ...), custom_call_target="tpu_custom_call" | custom-call | tf_op jit(solution)/shard_map/pallas_call | solution.py:233
  51.2 1.5 %collective-permute-start.7 = (f32[1,3584]{1,0:T(1,128)S(1)}, f32[1,3584]{1,0:T(1,128)S(1)}, u32[]{:S(2)}, u32[]{:S(2)}) collective-permute-start(f32[1,3584]{1,0:T(1,128)S(1)} %get-tuple-element.23), channel_id=1, source_target_pairs={{0,4},{4,0},{8,12},{12,8},{16,20},{20,16},{24,28},{28,24},{1,5},{5... | collective-permute-start | bytes 43016 | tf_op jit(solution)/shard_map/ppermute | solution.py:188
  52.7 2.2 %collective-permute-done.7 = f32[1,3584]{1,0:T(1,128)S(1)} collective-permute-done((f32[1,3584]{1,0:T(1,128)S(1)}, f32[1,3584]{1,0:T(1,128)S(1)}, u32[]{:S(2)}, u32[]{:S(2)}) %collective-permute-start.7) | collective-permute-done | bytes 14368 | tf_op jit(solution)/shard_map/ppermute | solution.py:188
  54.9 1.8 %collective-permute-start.8 = (f32[1,3584]{1,0:T(1,128)S(1)}, f32[1,3584]{1,0:T(1,128)S(1)}, u32[]{:S(2)}, u32[]{:S(2)}) collective-permute-start(f32[1,3584]{1,0:T(1,128)S(1)} %add.18), channel_id=1, source_target_pairs={{0,8},{4,12},{8,0},{12,4},{16,24},{20,28},{24,16},{28,20},{1,9},{5... | collective-permute-start | bytes 43016 | tf_op jit(solution)/shard_map/ppermute | solution.py:188
  56.7 2.0 %collective-permute-done.8 = f32[1,3584]{1,0:T(1,128)S(1)} collective-permute-done((f32[1,3584]{1,0:T(1,128)S(1)}, f32[1,3584]{1,0:T(1,128)S(1)}, u32[]{:S(2)}, u32[]{:S(2)}) %collective-permute-start.8) | collective-permute-done | bytes 14368 | tf_op jit(solution)/shard_map/ppermute | solution.py:188
  58.7 3.4 %collective-permute-start.9 = (f32[1,3584]{1,0:T(1,128)S(1)}, f32[1,3584]{1,0:T(1,128)S(1)}, u32[]{:S(2)}, u32[]{:S(2)}) collective-permute-start(f32[1,3584]{1,0:T(1,128)S(1)} %add.19), channel_id=1, source_target_pairs={{0,16},{4,20},{8,24},{12,28},{16,0},{20,4},{24,8},{28,12},{1,17},{... | collective-permute-start | bytes 43016 | tf_op jit(solution)/shard_map/ppermute | solution.py:188
  62.2 0.0 copy-done.6
  62.2 9.3 %all_gather.3 = bf16[3584,128]{1,0:T(8,128)(2,1)S(1)} all-gather(bf16[896,128]{1,0:T(8,128)(2,1)S(1)} %copy-done.6), channel_id=1, replica_groups=mesh['seq'=8,'fsdp'=4] {'fsdp'}, dimensions={0}, use_global_device_ids=true | all-gather | bytes 1146880 | tf_op jit(solution)/shard_map/all_gather | solution.py:209
  71.5 0.0 collective-permute-done.9
  71.5 0.6 multiply_reduce_fusion
  72.8 0.7 %fusion = f32[1,128]{1,0:T(1,128)} fusion(bf16[3584,128]{1,0:T(8,128)(2,1)S(1)} %all_gather.3, f32[]{:T(128)S(6)} %sqrt.4, f32[1,3584]{1,0:T(1,128)S(1)} %add.19, f32[1,3584]{1,0:T(1,128)S(1)} %collective-permute-done.9), kind=kOutput, calls=%fused_computation | convolution fusion | flops 931840 | bytes 946692 | tf_op jit(solution)/shard_map/dot_general | solution.py:245
  (2 shorter events, 0.0 us)
Async XLA Ops:
  0.6 38.1 %copy-start.5 = (f32[56]{0:T(128)S(1)}, f32[56]{0:T(128)}, u32[]{:S(2)}) copy-start(f32[56]{0:T(128)} %skip.1) | copy-start | bytes 676
  0.7 1.2 %copy-start = (bf16[1,128,3584]{2,1,0:T(8,128)(2,1)S(1)}, bf16[1,128,3584]{2,1,0:T(8,128)(2,1)}, u32[]{:S(2)}) copy-start(bf16[1,128,3584]{2,1,0:T(8,128)(2,1)} %param.5) | copy-start | bytes 2752516
  1.8 0.8 %copy-start.2 = (bf16[1,128,256]{2,1,0:T(8,128)(2,1)S(1)}, bf16[1,128,256]{2,1,0:T(8,128)(2,1)}, u32[]{:S(2)}) copy-start(bf16[1,128,256]{2,1,0:T(8,128)(2,1)} %param.6) | copy-start | bytes 196612
  2.7 0.7 %copy-start.4 = (f32[1,56,128]{2,1,0:T(8,128)S(1)}, f32[1,56,128]{2,1,0:T(8,128)}, u32[]{:S(2)}) copy-start(f32[1,56,128]{2,1,0:T(8,128)} %param.7) | copy-start | bytes 86020
  3.4 35.4 %copy-start.1 = (bf16[1,128,3584]{2,1,0:T(8,128)(2,1)S(1)}, bf16[1,128,3584]{2,1,0:T(8,128)(2,1)}, u32[]{:S(2)}) copy-start(bf16[1,128,3584]{2,1,0:T(8,128)(2,1)} %param.5) | copy-start | bytes 2752516
  3.4 35.4 %copy-start.3 = (bf16[1,128,256]{2,1,0:T(8,128)(2,1)S(1)}, bf16[1,128,256]{2,1,0:T(8,128)(2,1)}, u32[]{:S(2)}) copy-start(bf16[1,128,256]{2,1,0:T(8,128)(2,1)} %param.6) | copy-start | bytes 196612
  5.1 9.2 %collective-permute-start = (bf16[144,896]{1,0:T(8,128)(2,1)S(1)}, bf16[144,896]{1,0:T(8,128)(2,1)S(1)}, u32[]{:S(2)}, u32[]{:S(2)}) collective-permute-start(bf16[144,896]{1,0:T(8,128)(2,1)S(1)} %get-tuple-element.14), channel_id=1, source_target_pairs={{0,4},{4,0},{8,12},{12,8},{16,20},{20,16},{24,28},{28,24},{1,5},{5... | collective-permute-start | bytes 774152 | tf_op jit(solution)/shard_map/ppermute | solution.py:188
  8.1 9.1 %collective-permute-start.1 = (bf16[144,896]{1,0:T(8,128)(2,1)S(1)}, bf16[144,896]{1,0:T(8,128)(2,1)S(1)}, u32[]{:S(2)}, u32[]{:S(2)}) collective-permute-start(bf16[144,896]{1,0:T(8,128)(2,1)S(1)} %get-tuple-element.15), channel_id=1, source_target_pairs={{0,8},{4,12},{8,0},{12,4},{16,24},{20,28},{24,16},{28,20},{1,9},{5... | collective-permute-start | bytes 774152 | tf_op jit(solution)/shard_map/ppermute | solution.py:188
  9.6 11.4 %collective-permute-start.2 = (bf16[144,896]{1,0:T(8,128)(2,1)S(1)}, bf16[144,896]{1,0:T(8,128)(2,1)S(1)}, u32[]{:S(2)}, u32[]{:S(2)}) collective-permute-start(bf16[144,896]{1,0:T(8,128)(2,1)S(1)} %get-tuple-element.16), channel_id=1, source_target_pairs={{0,12},{4,8},{8,4},{12,0},{16,28},{20,24},{24,20},{28,16},{1,13},{... | collective-permute-start | bytes 774152 | tf_op jit(solution)/shard_map/ppermute | solution.py:188
  22.0 8.3 %collective-permute-start.3 = (bf16[128,896]{1,0:T(8,128)(2,1)S(1)}, bf16[128,896]{1,0:T(8,128)(2,1)S(1)}, u32[]{:S(2)}, u32[]{:S(2)}) collective-permute-start(bf16[128,896]{1,0:T(8,128)(2,1)S(1)} %get-tuple-element.17), channel_id=1, source_target_pairs={{0,16},{4,20},{8,24},{12,28},{1,17},{5,21},{9,25},{13,29},{2,18},{... | collective-permute-start | bytes 688136 | tf_op jit(solution)/shard_map/ppermute | solution.py:191
  30.9 10.1 %collective-permute-start.4 = (bf16[128,896]{1,0:T(8,128)(2,1)S(1)}, bf16[128,896]{1,0:T(8,128)(2,1)S(1)}, u32[]{:S(2)}, u32[]{:S(2)}) collective-permute-start(bf16[128,896]{1,0:T(8,128)(2,1)S(1)} %get-tuple-element.19), channel_id=1, source_target_pairs={{0,4},{4,0},{8,12},{12,8},{16,20},{20,16},{24,28},{28,24},{1,5},{5... | collective-permute-start | bytes 688136 | tf_op jit(solution)/shard_map/ppermute | solution.py:188
  32.4 12.8 %collective-permute-start.5 = (bf16[128,896]{1,0:T(8,128)(2,1)S(1)}, bf16[128,896]{1,0:T(8,128)(2,1)S(1)}, u32[]{:S(2)}, u32[]{:S(2)}) collective-permute-start(bf16[128,896]{1,0:T(8,128)(2,1)S(1)} %get-tuple-element.20), channel_id=1, source_target_pairs={{0,8},{4,12},{8,0},{12,4},{16,24},{20,28},{24,16},{28,20},{1,9},{5... | collective-permute-start | bytes 688136 | tf_op jit(solution)/shard_map/ppermute | solution.py:188
  38.8 10.4 %collective-permute-start.6 = (bf16[128,896]{1,0:T(8,128)(2,1)S(1)}, bf16[128,896]{1,0:T(8,128)(2,1)S(1)}, u32[]{:S(2)}, u32[]{:S(2)}) collective-permute-start(bf16[128,896]{1,0:T(8,128)(2,1)S(1)} %get-tuple-element.21), channel_id=1, source_target_pairs={{0,12},{4,8},{8,4},{12,0},{16,28},{20,24},{24,20},{28,16},{1,13},{... | collective-permute-start | bytes 688136 | tf_op jit(solution)/shard_map/ppermute | solution.py:188
  41.0 21.2 %copy-start.6 = (bf16[896,128]{1,0:T(8,128)(2,1)S(1)}, bf16[896,128]{1,0:T(8,128)(2,1)}, u32[]{:S(2)}) copy-start(bf16[896,128]{1,0:T(8,128)(2,1)} %param.9) | copy-start | bytes 688132
  51.2 3.7 %collective-permute-start.7 = (f32[1,3584]{1,0:T(1,128)S(1)}, f32[1,3584]{1,0:T(1,128)S(1)}, u32[]{:S(2)}, u32[]{:S(2)}) collective-permute-start(f32[1,3584]{1,0:T(1,128)S(1)} %get-tuple-element.23), channel_id=1, source_target_pairs={{0,4},{4,0},{8,12},{12,8},{16,20},{20,16},{24,28},{28,24},{1,5},{5... | collective-permute-start | bytes 43016 | tf_op jit(solution)/shard_map/ppermute | solution.py:188
  54.9 3.8 %collective-permute-start.8 = (f32[1,3584]{1,0:T(1,128)S(1)}, f32[1,3584]{1,0:T(1,128)S(1)}, u32[]{:S(2)}, u32[]{:S(2)}) collective-permute-start(f32[1,3584]{1,0:T(1,128)S(1)} %add.18), channel_id=1, source_target_pairs={{0,8},{4,12},{8,0},{12,4},{16,24},{20,28},{24,16},{28,20},{1,9},{5... | collective-permute-start | bytes 43016 | tf_op jit(solution)/shard_map/ppermute | solution.py:188
  58.7 12.7 %collective-permute-start.9 = (f32[1,3584]{1,0:T(1,128)S(1)}, f32[1,3584]{1,0:T(1,128)S(1)}, u32[]{:S(2)}, u32[]{:S(2)}) collective-permute-start(f32[1,3584]{1,0:T(1,128)S(1)} %add.19), channel_id=1, source_target_pairs={{0,16},{4,20},{8,24},{12,28},{16,0},{20,4},{24,8},{28,12},{1,17},{... | collective-permute-start | bytes 43016 | tf_op jit(solution)/shard_map/ppermute | solution.py:188

commit v2 on v1

v2 whole, which is shorter than its diff:
```python
import functools
import jax
import jax.numpy as jnp
from jax import lax
from jax.experimental import pallas as pl
from jax.experimental.pallas import tpu as pltpu
from jax.sharding import PartitionSpec as P

N = 128
GROUP = 128

epsilon = 1e-06

F32 = jnp.float32
BF16 = jnp.bfloat16
HIGHEST = lax.Precision.HIGHEST
LIMIT = 48 * 1024 * 1024

VMEM = pl.BlockSpec(memory_space=pltpu.VMEM)
HBM = pl.BlockSpec(memory_space=pltpu.HBM)
SMEM = pl.BlockSpec(memory_space=pltpu.SMEM)


def dot(a, b, contract=((1,), (0,)), precision=None):
    return lax.dot_general(a, b, (contract, ((), ())), preferred_element_type=F32, precision=precision)


def iota(shape, dim):
    return lax.broadcasted_iota(jnp.int32, shape, dim)


def split(x):
    high = x.astype(BF16)
    return high, (x - high.astype(F32)).astype(BF16)


def cumulative_by_position(log_decay):
    upto = (iota((GROUP, GROUP), 1) <= iota((GROUP, GROUP), 0)).astype(F32)
    return dot(upto, log_decay, ((1,), (1,)), HIGHEST)


def cumulative_by_head(log_decay):
    upto = (iota((GROUP, GROUP), 0) <= iota((GROUP, GROUP), 1)).astype(F32)
    return dot(log_decay, upto, precision=HIGHEST)


def spread(x, first_head, lanes, head_dim):
    heads = x.shape[1]
    member = (iota((heads, lanes), 0) == first_head + iota((heads, lanes), 1) // head_dim).astype(BF16)
    return dot(jnp.concatenate(split(x), axis=1), jnp.concatenate([member, member], axis=0))


def state_kernel(head_dim, place, kq_from, values_from, log_decay_from, *refs):
    *parts, kq, values, log_decay, sem = refs
    copies = [
        pltpu.make_async_copy(source, target, sem.at[i])
        for i, (source, target) in enumerate(
            [(log_decay_from, log_decay), (kq_from, kq), (values_from, values)]
        )
    ]
    for copy in copies:
        copy.start()
    lanes = parts[0].shape[1]
    part_heads = lanes // head_dim
    copies[0].wait()
    by_position = cumulative_by_position(log_decay[...])
    decay_left = jnp.exp(by_position[GROUP - 1 :, :] - by_position)
    copies[1].wait()
    keys = jnp.transpose(kq[:, :N])
    wides = [spread(decay_left, (place[0] ^ m) * part_heads, lanes, head_dim) for m in range(len(parts))]
    copies[2].wait()
    for m, part in enumerate(parts):
        start = pl.multiple_of((place[0] ^ m) * lanes, 128)
        weighted = (values[:, pl.ds(start, lanes)].astype(F32) * wides[m]).astype(BF16)
        part[...] = dot(keys, weighted).astype(BF16)


def note_rows(lanes, head_dim):
    sums = -(-(lanes // 128) // 8) * 8
    heads = -(-(lanes // head_dim) // 8) * 8
    return sums, heads, sums + 2 * heads


def block_kernel(head_dim, place, kq, values, log_decay, skip, out, wide_growth, *refs):
    *notes, own_sums = refs
    ld = log_decay[...]
    channels = values.shape[1]
    lanes = channels // len(notes)
    part_heads = lanes // head_dim
    by_position = cumulative_by_position(ld)
    by_head = cumulative_by_head(ld)
    queries = kq[:, N:]
    scores = dot(queries, kq[:, :N], ((1,), (1,)))
    causal = iota((GROUP, GROUP), 0) >= iota((GROUP, GROUP), 1)
    per = 128 // head_dim
    lane = iota((GROUP, 128), 1) // head_dim
    lane_row = iota((1, 128), 1) // head_dim
    sums_rows, heads_rows, _ = note_rows(lanes, head_dim)
    own_sums[...] = jnp.zeros_like(own_sums)
    for i in range(channels // 128):
        at = slice(i * 128, (i + 1) * 128)
        value = values[:, at]
        mixes, tops = [], []
        direct = jnp.zeros((1, 128), F32)
        growth = None
        for j in range(per):
            h = i * per + j
            here = jnp.broadcast_to(by_position[:, h : h + 1], (GROUP, 128))
            gap = here - by_head[h : h + 1, :]
            mixes.append((scores * jnp.exp(jnp.where(causal, gap, -jnp.inf))).astype(BF16))
            tops.append(jnp.where(lane == j, value, jnp.zeros_like(value)))
            direct = jnp.where(lane_row == j, skip[h], direct)
            growth = here if growth is None else jnp.where(lane == j, here, growth)
        mixed = dot(jnp.concatenate(mixes, axis=1), jnp.concatenate(tops, axis=0))
        mixed = mixed + direct * value.astype(F32)
        out[:, at] = mixed
        wide_growth[:, at] = jnp.exp(growth)
        part, row = divmod(i, lanes // 128)
        own_sums[part, row : row + 1, :] = jnp.sum(mixed, axis=0, keepdims=True)

    high, low = split(jnp.exp(by_head))
    grown = dot(high, queries) + dot(low, queries)
    factor = jnp.exp(jnp.broadcast_to(by_head[:, GROUP - 1 :], by_head.shape))
    both = jnp.concatenate([grown, factor], axis=1)
    for m, note in enumerate(notes):
        first = (place[0] ^ m) * part_heads
        own = (iota((heads_rows, ld.shape[0]), 1) == first + iota((heads_rows, ld.shape[0]), 0)).astype(F32)
        mine = dot(own, both, precision=HIGHEST)
        note[pl.ds(0, sums_rows), :] = own_sums[place[0] ^ m]
        note[pl.ds(sums_rows, heads_rows), :] = mine[:, :128]
        note[pl.ds(sums_rows + heads_rows, heads_rows), :] = mine[:, 128:]


def wide_factor(factor, lanes, head_dim):
    per = 128 // head_dim
    pieces = []
    lane = iota((1, 128), 1) // head_dim
    for i in range(lanes // 128):
        piece = factor[i * per : i * per + 1]
        for j in range(1, per):
            piece = jnp.where(lane == j, factor[i * per + j : i * per + j + 1], piece)
        pieces.append(piece)
    return jnp.concatenate(pieces, axis=1)


def part_decay(note, lanes, head_dim):
    sums_rows, heads_rows, rows = note_rows(lanes, head_dim)
    return wide_factor(note[sums_rows + heads_rows : rows, :], lanes, head_dim)


def gather_parts(place, parts, notes, ordered, ordered_notes):
    for m, (part, note) in enumerate(zip(parts, notes)):
        ordered[place[0] ^ m] = part[...]
        ordered_notes[place[0] ^ m] = note[...]


def total_kernel(head_dim, count, place, *refs):
    parts, notes = refs[:count], refs[count : 2 * count]
    total, *decay, ordered_notes, scales = refs[2 * count :]
    lanes = total.shape[1]
    sums_rows, heads_rows, _ = note_rows(lanes, head_dim)
    at = pl.ds(sums_rows + heads_rows, heads_rows)
    for m, note in enumerate(notes):
        ordered_notes[place[0] ^ m] = note[at, :]
    factor = jnp.ones((heads_rows, 128), F32)
    for j in reversed(range(count)):
        scales[j] = wide_factor(factor, lanes, head_dim)
        factor = factor * ordered_notes[j]
    running = scales[place[0]] * parts[0][...].astype(F32)
    for m in range(1, count):
        running = running + scales[place[0] ^ m] * parts[m][...].astype(F32)
    total[...] = running.astype(BF16)
    for out in decay:
        out[...] = wide_factor(factor, lanes, head_dim)


def starts_kernel(head_dim, count, place, before, _, *refs):
    parts, notes, outs = refs[:count], refs[count : 2 * count], refs[2 * count : 3 * count]
    ordered, ordered_notes, results = refs[3 * count :]
    lanes = before.shape[1]
    gather_parts(place, parts, notes, ordered, ordered_notes)
    running = jnp.where(place[1] == 0, 0.0, before[...].astype(F32))
    for j in range(count):
        results[j] = running.astype(BF16)
        if j < count - 1:
            running = part_decay(ordered_notes[j], lanes, head_dim) * running + ordered[j].astype(F32)
    for m, out in enumerate(outs):
        out[...] = results[place[0] ^ m]


def base_kernel(head_dim, count, place, *refs):
    parts, notes = refs[:count], refs[count : 2 * count]
    base, ordered, ordered_notes = refs[2 * count :]
    lanes = parts[0].shape[1]
    sums_rows, heads_rows, rows = note_rows(lanes, head_dim)
    gather_parts(place, parts, notes, ordered, ordered_notes)
    sums = ordered_notes[0, pl.ds(0, sums_rows), :]
    weight = ordered_notes[0, pl.ds(sums_rows, heads_rows), :]
    factor = ordered_notes[0, pl.ds(sums_rows + heads_rows, heads_rows), :]
    running = ordered[0].astype(F32)
    carried = jnp.zeros((heads_rows, lanes), F32)
    for j in range(1, count):
        query_sums = ordered_notes[j, pl.ds(sums_rows, heads_rows), :]
        sums = sums + ordered_notes[j, pl.ds(0, sums_rows), :]
        weight = weight + factor * query_sums
        factor = factor * ordered_notes[j, pl.ds(sums_rows + heads_rows, heads_rows), :]
        carried = carried + heads_dot(query_sums, running.astype(BF16))
        running = part_decay(ordered_notes[j], lanes, head_dim) * running + ordered[j].astype(F32)
    carried = own_heads(carried, head_dim)
    for i in range(lanes // 128):
        base[i : i + 1, :] = sums[i : i + 1] + carried[:, i * 128 : (i + 1) * 128]
    for i in range(lanes // 128, sums_rows):
        base[i : i + 1, :] = jnp.zeros((1, 128), F32)
    base[pl.ds(sums_rows, heads_rows), :] = weight


def heads_dot(query_sums, state):
    rows = query_sums.shape[0]
    both = dot(jnp.concatenate(split(query_sums), axis=0), state)
    return both[:rows] + both[rows:]


def own_heads(x, head_dim):
    mine = iota(x.shape, 0) == iota(x.shape, 1) // head_dim
    return jnp.sum(jnp.where(mine, x, 0.0), axis=0, keepdims=True)


def share_of(pooled, classifier, out):
    high, low = split(pooled)
    weights = classifier[...]
    out[0:1, :] = dot(high, weights) + dot(low, weights)
    out[1:2, :] = jnp.broadcast_to(jnp.sum(pooled * pooled, axis=1, keepdims=True), (1, weights.shape[1]))
    out[2:, :] = jnp.zeros((out.shape[0] - 2, weights.shape[1]), F32)


def pooled_kernel(head_dim, positions, place, mine, other, total, before, classifier, out):
    lanes = total.shape[1]
    sums_rows, heads_rows, _ = note_rows(lanes, head_dim)
    first = place[1] == 0
    at = pl.ds(sums_rows, heads_rows)
    weight = jnp.where(first, other[at, :], mine[at, :])
    state = jnp.where(first, total[...].astype(F32), before[...].astype(F32)).astype(BF16)
    carried = own_heads(heads_dot(weight, state), head_dim)
    rows = mine[pl.ds(0, sums_rows), :] + other[pl.ds(0, sums_rows), :]
    sums = carried + jnp.concatenate([rows[i : i + 1] for i in range(lanes // 128)], axis=1)
    share_of(sums / positions, classifier, out)


def sums_kernel(head_dim, count, *refs):
    notes, states, sums = refs[:count], refs[count : 2 * count], refs[-1]
    lanes = sums.shape[1]
    sums_rows, heads_rows, _ = note_rows(lanes, head_dim)
    carried = jnp.zeros((heads_rows, lanes), F32)
    for note, state in zip(notes, states):
        carried = carried + heads_dot(note[pl.ds(sums_rows, heads_rows), :], state[...])
    carried = own_heads(carried, head_dim)
    rows = notes[0][pl.ds(0, sums_rows), :]
    for note in notes[1:]:
        rows = rows + note[pl.ds(0, sums_rows), :]
    own = jnp.concatenate([rows[i : i + 1] for i in range(lanes // 128)], axis=1)
    sums[...] = carried + own


def logits_kernel(positions, sums, classifier, out):
    share_of(sums[...] / positions, classifier, out)


def scale_kernel(channels, *refs):
    *shares, _, logits = refs
    whole = shares[0][...]
    for share in shares[1:]:
        whole = whole + share[...]
    logits[...] = whole[0:1] / jnp.sqrt(whole[1:2] / channels + epsilon)


def output_kernel(ms, aliased, place, kq, local, wide_growth, *refs):
    carried, refs = refs[: len(ms)], refs[len(ms) + aliased :]
    mixed, done, made, sem = refs
    lanes = carried[0].shape[1]
    queries = kq[:, N:]
    copies = []
    for i, (m, state) in enumerate(zip(ms, carried)):
        at = pl.ds(pl.multiple_of((place[0] ^ m) * lanes, 128), lanes)
        made[i] = (local[:, at] + wide_growth[:, at] * dot(queries, state[...])).astype(BF16)
        copies.append(pltpu.make_async_copy(made.at[i], mixed.at[:, at], sem.at[i]))
        copies[-1].start()
    for copy in copies:
        copy.wait()
    done[...] = jnp.zeros_like(done)


def call(kernel, outs, in_specs, scratch=(), flops=0, moved=0, out_specs=None, aliases=None):
    return pl.pallas_call(
        kernel,
        out_shape=outs,
        in_specs=in_specs,
        out_specs=out_specs or jax.tree.map(lambda _: VMEM, outs),
        scratch_shapes=scratch,
        input_output_aliases=aliases or {},
        cost_estimate=pl.CostEstimate(flops=flops, bytes_accessed=moved, transcendentals=0),
        compiler_params=pltpu.CompilerParams(vmem_limit_bytes=LIMIT),
    )


def local(inputs, keys_queries, log_decay, skip, classifier):
    _, positions, channels = inputs.shape
    heads = log_decay.shape[1]
    head_dim = channels // heads
    size, wide = lax.axis_size("seq"), lax.axis_size("fsdp")
    group = wide
    lanes = channels // group
    index = lax.axis_index("seq")
    place = jnp.stack([index % group, index // group]).astype(jnp.int32)
    values, kq, ld = inputs[0], keys_queries[0], log_decay[0]
    state = jax.ShapeDtypeStruct((N, lanes), BF16)
    note = jax.ShapeDtypeStruct((note_rows(lanes, head_dim)[2], 128), F32)
    row = jax.ShapeDtypeStruct((1, lanes), F32)
    full = jax.ShapeDtypeStruct((positions, channels), F32)
    gathered = [pltpu.VMEM((group, *state.shape), BF16), pltpu.VMEM((group, *note.shape), F32)]

    def swap(x, m):
        return lax.ppermute(x, "seq", [(i, i ^ m) for i in range(size)])

    def swap_all(xs):
        return [xs[0]] + [swap(xs[m], m) for m in range(1, group)]

    def shift(x, by):
        return lax.ppermute(x, "seq", [(i, i + by) for i in range(size - by)])

    *parts, kq, values, ld = call(
        functools.partial(state_kernel, head_dim),
        [state] * group + [jax.ShapeDtypeStruct(x.shape, x.dtype) for x in (kq, values, ld)],
        [SMEM] + [HBM] * 3,
        [pltpu.SemaphoreType.DMA((3,))],
        flops=2 * positions * N * channels,
        moved=4 * positions * channels,
    )(place, kq, values, ld)
    parts = swap_all(parts)

    from_block, wide_growth, *notes = call(
        functools.partial(block_kernel, head_dim),
        [full, full] + [note] * group,
        [SMEM] + [VMEM] * 3 + [SMEM],
        [pltpu.VMEM((group, note_rows(lanes, head_dim)[0], 128), F32)],
        flops=8 * positions * N * channels,
        moved=6 * positions * channels,
    )(place, kq, values, ld, skip)
    notes = swap_all(notes)

    pair = size == 2 * group
    total, *decay = call(
        functools.partial(total_kernel, head_dim, group),
        [state] if pair else [state, row],
        [SMEM] + [VMEM] * (2 * group),
        [pltpu.VMEM((group, note_rows(lanes, head_dim)[1], 128), F32), pltpu.VMEM((group, *row.shape), F32)],
    )(place, *parts, *notes)
    rows, _ = lax.optimization_barrier((classifier, total))
    rows = lax.ppermute(
        rows,
        ("seq", "fsdp"),
        [((s - s % group + f) * wide + s % group, s * wide + f) for s in range(size) for f in range(wide)],
    )
    if pair:
        before = swap(total, group)
        base = call(
            functools.partial(base_kernel, head_dim, group),
            jax.ShapeDtypeStruct((sum(note_rows(lanes, head_dim)[:2]), 128), F32),
            [SMEM] + [VMEM] * (2 * group),
            gathered,
        )(place, *parts, *notes)
        other = swap(base, group)
    else:
        before, decay = shift(total, group).astype(F32), shift(decay[0], group)
        reach = 1
        while reach < size // group - 1:
            before = before + decay * shift(before, group * reach)
            decay = decay * shift(decay, group * reach)
            reach *= 2
        before = before.astype(BF16)
        other = decay
    starts = call(
        functools.partial(starts_kernel, head_dim, group),
        [state] * group,
        [SMEM] + [VMEM] * (2 * group + 2),
        [*gathered, pltpu.VMEM((group, *state.shape), BF16)],
    )(place, before, other, *parts, *notes)
    carried = swap_all(starts)

    out = jax.ShapeDtypeStruct((8, classifier.shape[1]), F32)
    if pair:
        share = call(
            functools.partial(pooled_kernel, head_dim, positions * size), out, [SMEM] + [VMEM] * 5
        )(place, base, other, total, before, rows)
    else:
        sums = call(functools.partial(sums_kernel, head_dim, group), row, [VMEM] * (2 * group))(*notes, *starts)
        reach = group
        while reach < size:
            sums = sums + swap(sums, reach)
            reach *= 2
        share = call(functools.partial(logits_kernel, positions * size), out, [VMEM] * 2)(sums, rows)
    shares = swap_all([share] * group)

    mixed = jax.ShapeDtypeStruct((positions, channels), BF16)
    for ms in (tuple(range(group - 1)), (group - 1,)):
        made = () if isinstance(mixed, jax.ShapeDtypeStruct) else (mixed,)
        mixed, done = call(
            functools.partial(output_kernel, ms, len(made)),
            [jax.ShapeDtypeStruct((positions, channels), BF16), jax.ShapeDtypeStruct((8, 128), F32)],
            [SMEM] + [VMEM] * (3 + len(ms)) + [HBM] * len(made),
            [pltpu.VMEM((len(ms), positions, lanes), BF16), pltpu.SemaphoreType.DMA((len(ms),))],
            out_specs=[HBM, VMEM],
            aliases={4 + len(ms): 0} if made else None,
        )(place, kq, from_block, wide_growth, *[carried[m] for m in ms], *made)
    logits = call(
        functools.partial(scale_kernel, channels),
        jax.ShapeDtypeStruct((1, classifier.shape[1]), F32),
        [VMEM] * (group + 1),
    )(*shares, done)
    return mixed[None], logits


def solution(mesh):
    return jax.shard_map(
        local,
        mesh=mesh,
        in_specs=(
            P("fsdp", "seq", None),
            P("fsdp", "seq", None),
            P("fsdp", None, "seq"),
            P(),
            P("fsdp", None),
        ),
        out_specs=(P("fsdp", "seq", None), P("fsdp", None)),
        check_vma=False,
    )
```

time: 73.8 us -> 53 us (0.72)
  the two profiles are of different devices: /device:TPU:0 before, /device:TPU:18 now
where the time goes in v2:
time: 53 us; the launch traced here: 52.7 us
  starting transfers between devices  27.8 us (52%)
  Pallas kernels  12.6 us (24%)
  waiting for transfers between devices  7.99 us (15%)
  local copies, waits for them, and re-layouts  3.42 us (6%)
  between operations  0.78 us (1%)
    ppermute x14, starting transfers between devices, swap(): return lax.ppermute(x, 'seq', [(i, i ^ m) for i in range(size)])  24.4 us
    ppermute x14, waiting for transfers between devices, swap(): return lax.ppermute(x, 'seq', [(i, i ^ m) for i in range(size)])  7.31 us
    pallas_call x2, Pallas kernels, local(): call(functools.partial(output_kernel, ms, len(made)), [jax.ShapeDtypeStru...  3.69 us
    ppermute x1, starting transfers between devices, local(): lax.ppermute(rows, ('seq', 'fsdp'), [((s - s % group + f) * wide + s % gr...  3.45 us
    unnamed x10, local copies, waits for them, and re-layouts  3.42 us
    pallas_call x1, Pallas kernels, local(): call(functools.partial(block_kernel, head_dim), [full, full] + [note] * g...  2.61 us
    pallas_call x1, Pallas kernels, local(): call(functools.partial(state_kernel, head_dim), [state] * group + [jax.Sh...  2.1 us
  transfers between devices with their start and end apart: 15, of which 4 were waited for; matrix products, arithmetic and copies ran while one was open for 0% of the time, Pallas kernels for 17%

profile of v2, /device:TPU:18, one launch (start us, length us, event | category | flops | bytes accessed | tf_op | source)
XLA Modules:
  0.0 52.7 jit_solution(3373622293753705516)
XLA Ops:
  0.6 0.1 pad_add_fusion.place
  0.7 0.0 copy-start
  0.7 1.2 %copy-done = bf16[1,128,3584]{2,1,0:T(8,128)(2,1)S(1)} copy-done((bf16[1,128,3584]{2,1,0:T(8,128)(2,1)S(1)}, bf16[1,128,3584]{2,1,0:T(8,128)(2,1)}, u32[]{:S(2)}) %copy-start) | copy-done | bytes 917528
  1.9 0.0 copy-start.1
  1.9 0.8 %copy-done.1 = bf16[1,128,256]{2,1,0:T(8,128)(2,1)S(1)} copy-done((bf16[1,128,256]{2,1,0:T(8,128)(2,1)S(1)}, bf16[1,128,256]{2,1,0:T(8,128)(2,1)}, u32[]{:S(2)}) %copy-start.1) | copy-done | bytes 65560
  2.7 0.0 copy-start.2
  2.7 0.7 %copy-done.2 = f32[1,56,128]{2,1,0:T(8,128)S(1)} copy-done((f32[1,56,128]{2,1,0:T(8,128)S(1)}, f32[1,56,128]{2,1,0:T(8,128)}, u32[]{:S(2)}) %copy-start.2) | copy-done | bytes 28696
  3.5 2.1 %shard_map.68 = (bf16[128,896]{1,0:T(8,128)(2,1)S(1)}, bf16[128,896]{1,0:T(8,128)(2,1)S(1)}, bf16[128,896]{1,0:T(8,128)(2,1)S(1)}, bf16[128,896]{1,0:T(8,128)(2,...) custom-call(s32[2]{0:T(128)S(1)} %pad_add_fusion.place, ...), custom_call_target="tpu_custom_call" | custom-call | flops 117440512 | bytes 1835008 | tf_op jit(solution)/shard_map/pallas_call | solution.py:330
  5.6 1.6 %collective-permute-start = (bf16[128,896]{1,0:T(8,128)(2,1)S(1)}, bf16[128,896]{1,0:T(8,128)(2,1)S(1)}, u32[]{:S(2)}, u32[]{:S(2)}) collective-permute-start(bf16[128,896]{1,0:T(8,128)(2,1)S(1)} %get-tuple-element.29), channel_id=1, source_target_pairs={{0,4},{4,0},{8,12},{12,8},{16,20},{20,16},{24,28},{28,24},{1,5},{5... | collective-permute-start | bytes 688136 | tf_op jit(solution)/shard_map/ppermute | solution.py:322
  7.2 1.6 %collective-permute-start.1 = (bf16[128,896]{1,0:T(8,128)(2,1)S(1)}, bf16[128,896]{1,0:T(8,128)(2,1)S(1)}, u32[]{:S(2)}, u32[]{:S(2)}) collective-permute-start(bf16[128,896]{1,0:T(8,128)(2,1)S(1)} %get-tuple-element.30), channel_id=1, source_target_pairs={{0,8},{4,12},{8,0},{12,4},{16,24},{20,28},{24,16},{28,20},{1,9},{5... | collective-permute-start | bytes 688136 | tf_op jit(solution)/shard_map/ppermute | solution.py:322
  8.8 0.4 collective-permute-start.2
  9.2 0.0 copy-start.3
  9.2 0.7 %copy-done.3 = f32[56]{0:T(128)S(1)} copy-done((f32[56]{0:T(128)S(1)}, f32[56]{0:T(128)}, u32[]{:S(2)}) %copy-start.3) | copy-done | bytes 248
  9.8 0.0 copy-start.4
  9.8 2.6 %shard_map.69 = (f32[128,3584]{1,0:T(8,128)S(1)}, f32[128,3584]{1,0:T(8,128)S(1)}, f32[40,128]{1,0:T(8,128)S(1)}, f32[40,128]{1,0:T(8,128)S(1)}, f32[40,128]{1,0:T(8,128)S(1)}, /*index=5*/f32[40,128]{1,0:T(8,128)S(1)}) custom-call(s32[2]{0:T(128)S(1)} %pad_add_fusion.place, bf16[128,256]{1,0:T(8,128)(2,1)S(1)} %get-tuple-element.23.kq, ...), custom_call_target="tpu_custom_call" | custom-call | flops 469762048 | bytes 2752512 | tf_op jit(solution)/shard_map/pallas_call | solution.py:340
  12.4 1.6 %collective-permute-start.3 = (f32[40,128]{1,0:T(8,128)S(1)}, f32[40,128]{1,0:T(8,128)S(1)}, u32[]{:S(2)}, u32[]{:S(2)}) collective-permute-start(f32[40,128]{1,0:T(8,128)S(1)} %get-tuple-element.33), channel_id=1, source_target_pairs={{0,4},{4,0},{8,12},{12,8},{16,20},{20,16},{24,28},{28,24},{1,5},{5... | collective-permute-start | bytes 61448 | tf_op jit(solution)/shard_map/ppermute | solution.py:322
  14.0 1.6 %collective-permute-start.4 = (f32[40,128]{1,0:T(8,128)S(1)}, f32[40,128]{1,0:T(8,128)S(1)}, u32[]{:S(2)}, u32[]{:S(2)}) collective-permute-start(f32[40,128]{1,0:T(8,128)S(1)} %get-tuple-element.34), channel_id=1, source_target_pairs={{0,8},{4,12},{8,0},{12,4},{16,24},{20,28},{24,16},{28,20},{1,9},{5... | collective-permute-start | bytes 61448 | tf_op jit(solution)/shard_map/ppermute | solution.py:322
  15.6 2.5 %collective-permute-done.3.refs_5_ = f32[40,128]{1,0:T(8,128)S(1)} collective-permute-done((f32[40,128]{1,0:T(8,128)S(1)}, f32[40,128]{1,0:T(8,128)S(1)}, u32[]{:S(2)}, u32[]{:S(2)}) %collective-permute-start.3) | collective-permute-done | bytes 20512 | tf_op jit(solution)/shard_map/ppermute | solution.py:322
  18.1 2.5 %collective-permute-start.5 = (f32[40,128]{1,0:T(8,128)S(1)}, f32[40,128]{1,0:T(8,128)S(1)}, u32[]{:S(2)}, u32[]{:S(2)}) collective-permute-start(f32[40,128]{1,0:T(8,128)S(1)} %get-tuple-element.35), channel_id=1, source_target_pairs={{0,12},{4,8},{8,4},{12,0},{16,28},{20,24},{24,20},{28,16},{1,13},{... | collective-permute-start | bytes 61448 | tf_op jit(solution)/shard_map/ppermute | solution.py:322
  20.6 0.0 collective-permute-done.4.refs_6_
  20.6 2.1 %collective-permute-done.5.refs_7_ = f32[40,128]{1,0:T(8,128)S(1)} collective-permute-done((f32[40,128]{1,0:T(8,128)S(1)}, f32[40,128]{1,0:T(8,128)S(1)}, u32[]{:S(2)}, u32[]{:S(2)}) %collective-permute-start.5) | collective-permute-done | bytes 20512 | tf_op jit(solution)/shard_map/ppermute | solution.py:322
  22.7 0.0 collective-permute-done.refs_1_
  22.7 0.0 collective-permute-done.1.refs_2_
  22.8 0.0 collective-permute-done.2.refs_3_
  22.8 0.9 %shard_map.70.total = bf16[128,896]{1,0:T(8,128)(2,1)S(1)} custom-call(s32[2]{0:T(128)S(1)} %pad_add_fusion.place, bf16[128,896]{1,0:T(8,128)(2,1)S(1)} %get-tuple-element.28.refs_0_, bf16[128,896]{1,0:T(8,128)(2,1)S(1)} %collective-permute-done.refs_1_, bf16[128,896]{1,0:T(8,128)(2,1)S(1)} %collective-permute-done.1.refs_2_, ...), custom_call_target="tpu_custom_call" | custom-call | tf_op jit(solution)/shard_map/pallas_call | solution.py:351
  23.6 0.4 collective-permute-start.6
  24.0 0.9 %shard_map.71.mine = f32[24,128]{1,0:T(8,128)S(1)} custom-call(s32[2]{0:T(128)S(1)} %pad_add_fusion.place, bf16[128,896]{1,0:T(8,128)(2,1)S(1)} %get-tuple-element.28.refs_0_, bf16[128,896]{1,0:T(8,128)(2,1)S(1)} %collective-permute-done.refs_1_, bf16[128,896]{1,0:T(8,128)(2,1)S(1)} %collective-permute-done.1.refs_2_, ...), custom_call_target="tpu_custom_call" | custom-call | tf_op jit(solution)/shard_map/pallas_call | solution.py:365
  24.9 2.6 %collective-permute-start.7 = (f32[24,128]{1,0:T(8,128)S(1)}, f32[24,128]{1,0:T(8,128)S(1)}, u32[]{:S(2)}, u32[]{:S(2)}) collective-permute-start(f32[24,128]{1,0:T(8,128)S(1)} %shard_map.71.mine), channel_id=1, source_target_pairs={{0,16},{4,20},{8,24},{12,28},{16,0},{20,4},{24,8},{28,12},{1,17},{... | collective-permute-start | bytes 36872 | tf_op jit(solution)/shard_map/ppermute | solution.py:322
  27.6 0.0 copy-done.4
  27.6 3.4 %collective-permute-start.11 = (bf16[896,128]{1,0:T(8,128)(2,1)S(1)}, bf16[896,128]{1,0:T(8,128)(2,1)S(1)}, u32[]{:S(2)}, u32[]{:S(2)}) collective-permute-start(bf16[896,128]{1,0:T(8,128)(2,1)S(1)} %copy-done.4), channel_id=1, source_target_pairs={{0,0},{4,1},{8,2},{12,3},{1,4},{5,5},{9,6},{13,7},{2,8},{6,9},{10,... | collective-permute-start | bytes 688136 | tf_op jit(solution)/shard_map/ppermute | solution.py:358
  31.1 0.0 collective-permute-done.7._.other
  31.1 0.0 collective-permute-done.6.before
  31.1 1.0 %shard_map.72 = (bf16[128,896]{1,0:T(8,128)(2,1)S(1)}, bf16[128,896]{1,0:T(8,128)(2,1)S(1)}, bf16[128,896]{1,0:T(8,128)(2,1)S(1)}, bf16[128,896]{1,0:T(8,128)(2,1)S(1)}) custom-call(s32[2]{0:T(128)S(1)} %pad_add_fusion.place, bf16[128,896]{1,0:T(8,128)(2,1)S(1)} %collective-permute-done.6.before, f32[24,128]{1,0:T(8,128)S(1)} %collective-permute-done.7._.other, ...), custom_call_target="tpu_custom_call" | custom-call | tf_op jit(solution)/shard_map/pallas_call | solution.py:381
  32.1 2.9 %collective-permute-start.9 = (bf16[128,896]{1,0:T(8,128)(2,1)S(1)}, bf16[128,896]{1,0:T(8,128)(2,1)S(1)}, u32[]{:S(2)}, u32[]{:S(2)}) collective-permute-start(bf16[128,896]{1,0:T(8,128)(2,1)S(1)} %get-tuple-element.38), channel_id=1, source_target_pairs={{0,4},{4,0},{8,12},{12,8},{16,20},{20,16},{24,28},{28,24},{1,5},{5... | collective-permute-start | bytes 688136 | tf_op jit(solution)/shard_map/ppermute | solution.py:322
  35.0 2.7 %collective-permute-start.10 = (bf16[128,896]{1,0:T(8,128)(2,1)S(1)}, bf16[128,896]{1,0:T(8,128)(2,1)S(1)}, u32[]{:S(2)}, u32[]{:S(2)}) collective-permute-start(bf16[128,896]{1,0:T(8,128)(2,1)S(1)} %get-tuple-element.39), channel_id=1, source_target_pairs={{0,8},{4,12},{8,0},{12,4},{16,24},{20,28},{24,16},{28,20},{1,9},{5... | collective-permute-start | bytes 688136 | tf_op jit(solution)/shard_map/ppermute | solution.py:322
  37.7 0.0 collective-permute-start.8
  37.7 0.7 %collective-permute-done.11.classifier = bf16[896,128]{1,0:T(8,128)(2,1)S(1)} collective-permute-done((bf16[896,128]{1,0:T(8,128)(2,1)S(1)}, bf16[896,128]{1,0:T(8,128)(2,1)S(1)}, u32[]{:S(2)}, u32[]{:S(2)}) %collective-permute-start.11) | collective-permute-done | bytes 229408 | tf_op jit(solution)/shard_map/ppermute | solution.py:358
  38.4 0.9 %shard_map.75.refs_0_ = f32[8,128]{1,0:T(8,128)S(1)} custom-call(s32[2]{0:T(128)S(1)} %pad_add_fusion.place, f32[24,128]{1,0:T(8,128)S(1)} %shard_map.71.mine, f32[24,128]{1,0:T(8,128)S(1)} %collective-permute-done.7._.other, bf16[128,896]{1,0:T(8,128)(2,1)S(1)} %shard_map.70.total, bf16[128,896]{1,0:T(8,128)(2,1)S(1)} %collective-permute-done.6.before, ...), custom_call_target="tpu_custom_call" | custom-call | tf_op jit(solution)/shard_map/pallas_call | solution.py:391
  39.3 2.3 %collective-permute-start.14 = (f32[8,128]{1,0:T(8,128)S(1)}, f32[8,128]{1,0:T(8,128)S(1)}, u32[]{:S(2)}, u32[]{:S(2)}) collective-permute-start(f32[8,128]{1,0:T(8,128)S(1)} %shard_map.75.refs_0_), channel_id=1, source_target_pairs={{0,12},{4,8},{8,4},{12,0},{16,28},{20,24},{24,20},{28,16},{1,13},{... | collective-permute-start | bytes 12296 | tf_op jit(solution)/shard_map/ppermute | solution.py:322
  41.6 1.7 %collective-permute-start.13 = (f32[8,128]{1,0:T(8,128)S(1)}, f32[8,128]{1,0:T(8,128)S(1)}, u32[]{:S(2)}, u32[]{:S(2)}) collective-permute-start(f32[8,128]{1,0:T(8,128)S(1)} %shard_map.75.refs_0_), channel_id=1, source_target_pairs={{0,8},{4,12},{8,0},{12,4},{16,24},{20,28},{24,16},{28,20},{1,9},{5... | collective-permute-start | bytes 12296 | tf_op jit(solution)/shard_map/ppermute | solution.py:322
  43.3 2.6 %collective-permute-done.9.refs_1_ = bf16[128,896]{1,0:T(8,128)(2,1)S(1)} collective-permute-done((bf16[128,896]{1,0:T(8,128)(2,1)S(1)}, bf16[128,896]{1,0:T(8,128)(2,1)S(1)}, u32[]{:S(2)}, u32[]{:S(2)}) %collective-permute-start.9) | collective-permute-done | bytes 229408 | tf_op jit(solution)/shard_map/ppermute | solution.py:322
  45.9 2.5 %collective-permute-start.12 = (f32[8,128]{1,0:T(8,128)S(1)}, f32[8,128]{1,0:T(8,128)S(1)}, u32[]{:S(2)}, u32[]{:S(2)}) collective-permute-start(f32[8,128]{1,0:T(8,128)S(1)} %shard_map.75.refs_0_), channel_id=1, source_target_pairs={{0,4},{4,0},{8,12},{12,8},{16,20},{20,16},{24,28},{28,24},{1,5},{5... | collective-permute-start | bytes 12296 | tf_op jit(solution)/shard_map/ppermute | solution.py:322
  48.4 0.0 collective-permute-done.10.refs_2_
  48.4 2.2 %shard_map.73 = (bf16[128,3584]{1,0:T(8,128)(2,1)}, f32[8,128]{1,0:T(8,128)}) custom-call(s32[2]{0:T(128)S(1)} %pad_add_fusion.place, bf16[128,256]{1,0:T(8,128)(2,1)S(1)} %get-tuple-element.23.kq, f32[128,3584]{1,0:T(8,128)S(1)} %get-tuple-element.26.local, f32[128,3584]{1,0:T(8,128)S(1)} %get-tuple-element.27.wide_growth, ...), custom_call_target="tpu_custom_call" | custom-call | tf_op jit(solution)/shard_map/pallas_call | solution.py:406
  50.7 0.0 collective-permute-done.8.refs_0_
  50.7 1.5 %shard_map.74 = (bf16[128,3584]{1,0:T(8,128)(2,1)}, f32[8,128]{1,0:T(8,128)S(1)}) custom-call(s32[2]{0:T(128)S(1)} %pad_add_fusion.place, bf16[128,256]{1,0:T(8,128)(2,1)S(1)} %get-tuple-element.23.kq, f32[128,3584]{1,0:T(8,128)S(1)} %get-tuple-element.26.local, f32[128,3584]{1,0:T(8,128)S(1)} %get-tuple-element.27.wide_growth, ...), custom_call_target="tpu_custom_call", output_to_operand_aliasing={{0}: (5, {})} | custom-call | tf_op jit(solution)/shard_map/pallas_call | solution.py:406
  52.1 0.0 collective-permute-done.14.refs_3_
  52.1 0.0 collective-permute-done.13.refs_2_
  52.2 0.0 collective-permute-done.12.refs_1_
  52.2 0.5 %shard_map.76 = f32[1,128]{1,0:T(1,128)} custom-call(f32[8,128]{1,0:T(8,128)S(1)} %shard_map.75.refs_0_, f32[8,128]{1,0:T(8,128)S(1)} %collective-permute-done.12.refs_1_, f32[8,128]{1,0:T(8,128)S(1)} %collective-permute-done.13.refs_2_, f32[8,128]{1,0:T(8,128)S(1)} %collective-permute-done.14.refs_3_, f32[8,128]{1,0:T(8,128)S(1)} %get-tuple-element.43.refs_4_), custom_call_target="tpu_custom_call" | custom-call | tf_op jit(solution)/shard_map/pallas_call | solution.py:414
Async XLA Ops:
  0.7 1.2 %copy-start = (bf16[1,128,3584]{2,1,0:T(8,128)(2,1)S(1)}, bf16[1,128,3584]{2,1,0:T(8,128)(2,1)}, u32[]{:S(2)}) copy-start(bf16[1,128,3584]{2,1,0:T(8,128)(2,1)} %param.5) | copy-start | bytes 2752516
  1.9 0.8 %copy-start.1 = (bf16[1,128,256]{2,1,0:T(8,128)(2,1)S(1)}, bf16[1,128,256]{2,1,0:T(8,128)(2,1)}, u32[]{:S(2)}) copy-start(bf16[1,128,256]{2,1,0:T(8,128)(2,1)} %param.6) | copy-start | bytes 196612
  2.7 0.7 %copy-start.2 = (f32[1,56,128]{2,1,0:T(8,128)S(1)}, f32[1,56,128]{2,1,0:T(8,128)}, u32[]{:S(2)}) copy-start(f32[1,56,128]{2,1,0:T(8,128)} %param.7) | copy-start | bytes 86020
  5.6 17.1 %collective-permute-start = (bf16[128,896]{1,0:T(8,128)(2,1)S(1)}, bf16[128,896]{1,0:T(8,128)(2,1)S(1)}, u32[]{:S(2)}, u32[]{:S(2)}) collective-permute-start(bf16[128,896]{1,0:T(8,128)(2,1)S(1)} %get-tuple-element.29), channel_id=1, source_target_pairs={{0,4},{4,0},{8,12},{12,8},{16,20},{20,16},{24,28},{28,24},{1,5},{5... | collective-permute-start | bytes 688136 | tf_op jit(solution)/shard_map/ppermute | solution.py:322
  7.2 15.6 %collective-permute-start.1 = (bf16[128,896]{1,0:T(8,128)(2,1)S(1)}, bf16[128,896]{1,0:T(8,128)(2,1)S(1)}, u32[]{:S(2)}, u32[]{:S(2)}) collective-permute-start(bf16[128,896]{1,0:T(8,128)(2,1)S(1)} %get-tuple-element.30), channel_id=1, source_target_pairs={{0,8},{4,12},{8,0},{12,4},{16,24},{20,28},{24,16},{28,20},{1,9},{5... | collective-permute-start | bytes 688136 | tf_op jit(solution)/shard_map/ppermute | solution.py:322
  8.8 14.0 %collective-permute-start.2 = (bf16[128,896]{1,0:T(8,128)(2,1)S(1)}, bf16[128,896]{1,0:T(8,128)(2,1)S(1)}, u32[]{:S(2)}, u32[]{:S(2)}) collective-permute-start(bf16[128,896]{1,0:T(8,128)(2,1)S(1)} %get-tuple-element.31), channel_id=1, source_target_pairs={{0,12},{4,8},{8,4},{12,0},{16,28},{20,24},{24,20},{28,16},{1,13},{... | collective-permute-start | bytes 688136 | tf_op jit(solution)/shard_map/ppermute | solution.py:322
  9.2 0.7 %copy-start.3 = (f32[56]{0:T(128)S(1)}, f32[56]{0:T(128)}, u32[]{:S(2)}) copy-start(f32[56]{0:T(128)} %skip.1) | copy-start | bytes 676
  9.8 17.8 %copy-start.4 = (bf16[896,128]{1,0:T(8,128)(2,1)S(1)}, bf16[896,128]{1,0:T(8,128)(2,1)}, u32[]{:S(2)}) copy-start(bf16[896,128]{1,0:T(8,128)(2,1)} %param.9) | copy-start | bytes 688132
  12.4 5.6 %collective-permute-start.3 = (f32[40,128]{1,0:T(8,128)S(1)}, f32[40,128]{1,0:T(8,128)S(1)}, u32[]{:S(2)}, u32[]{:S(2)}) collective-permute-start(f32[40,128]{1,0:T(8,128)S(1)} %get-tuple-element.33), channel_id=1, source_target_pairs={{0,4},{4,0},{8,12},{12,8},{16,20},{20,16},{24,28},{28,24},{1,5},{5... | collective-permute-start | bytes 61448 | tf_op jit(solution)/shard_map/ppermute | solution.py:322
  14.0 6.6 %collective-permute-start.4 = (f32[40,128]{1,0:T(8,128)S(1)}, f32[40,128]{1,0:T(8,128)S(1)}, u32[]{:S(2)}, u32[]{:S(2)}) collective-permute-start(f32[40,128]{1,0:T(8,128)S(1)} %get-tuple-element.34), channel_id=1, source_target_pairs={{0,8},{4,12},{8,0},{12,4},{16,24},{20,28},{24,16},{28,20},{1,9},{5... | collective-permute-start | bytes 61448 | tf_op jit(solution)/shard_map/ppermute | solution.py:322
  18.1 4.7 %collective-permute-start.5 = (f32[40,128]{1,0:T(8,128)S(1)}, f32[40,128]{1,0:T(8,128)S(1)}, u32[]{:S(2)}, u32[]{:S(2)}) collective-permute-start(f32[40,128]{1,0:T(8,128)S(1)} %get-tuple-element.35), channel_id=1, source_target_pairs={{0,12},{4,8},{8,4},{12,0},{16,28},{20,24},{24,20},{28,16},{1,13},{... | collective-permute-start | bytes 61448 | tf_op jit(solution)/shard_map/ppermute | solution.py:322
  23.6 7.4 %collective-permute-start.6 = (bf16[128,896]{1,0:T(8,128)(2,1)S(1)}, bf16[128,896]{1,0:T(8,128)(2,1)S(1)}, u32[]{:S(2)}, u32[]{:S(2)}) collective-permute-start(bf16[128,896]{1,0:T(8,128)(2,1)S(1)} %shard_map.70.total), channel_id=1, source_target_pairs={{0,16},{4,20},{8,24},{12,28},{16,0},{20,4},{24,8},{28,12},{1,17},{... | collective-permute-start | bytes 688136 | tf_op jit(solution)/shard_map/ppermute | solution.py:322
  24.9 6.1 %collective-permute-start.7 = (f32[24,128]{1,0:T(8,128)S(1)}, f32[24,128]{1,0:T(8,128)S(1)}, u32[]{:S(2)}, u32[]{:S(2)}) collective-permute-start(f32[24,128]{1,0:T(8,128)S(1)} %shard_map.71.mine), channel_id=1, source_target_pairs={{0,16},{4,20},{8,24},{12,28},{16,0},{20,4},{24,8},{28,12},{1,17},{... | collective-permute-start | bytes 36872 | tf_op jit(solution)/shard_map/ppermute | solution.py:322
  27.6 10.8 %collective-permute-start.11 = (bf16[896,128]{1,0:T(8,128)(2,1)S(1)}, bf16[896,128]{1,0:T(8,128)(2,1)S(1)}, u32[]{:S(2)}, u32[]{:S(2)}) collective-permute-start(bf16[896,128]{1,0:T(8,128)(2,1)S(1)} %copy-done.4), channel_id=1, source_target_pairs={{0,0},{4,1},{8,2},{12,3},{1,4},{5,5},{9,6},{13,7},{2,8},{6,9},{10,... | collective-permute-start | bytes 688136 | tf_op jit(solution)/shard_map/ppermute | solution.py:358
  32.1 13.8 %collective-permute-start.9 = (bf16[128,896]{1,0:T(8,128)(2,1)S(1)}, bf16[128,896]{1,0:T(8,128)(2,1)S(1)}, u32[]{:S(2)}, u32[]{:S(2)}) collective-permute-start(bf16[128,896]{1,0:T(8,128)(2,1)S(1)} %get-tuple-element.38), channel_id=1, source_target_pairs={{0,4},{4,0},{8,12},{12,8},{16,20},{20,16},{24,28},{28,24},{1,5},{5... | collective-permute-start | bytes 688136 | tf_op jit(solution)/shard_map/ppermute | solution.py:322
  35.0 13.4 %collective-permute-start.10 = (bf16[128,896]{1,0:T(8,128)(2,1)S(1)}, bf16[128,896]{1,0:T(8,128)(2,1)S(1)}, u32[]{:S(2)}, u32[]{:S(2)}) collective-permute-start(bf16[128,896]{1,0:T(8,128)(2,1)S(1)} %get-tuple-element.39), channel_id=1, source_target_pairs={{0,8},{4,12},{8,0},{12,4},{16,24},{20,28},{24,16},{28,20},{1,9},{5... | collective-permute-start | bytes 688136 | tf_op jit(solution)/shard_map/ppermute | solution.py:322
  37.7 12.9 %collective-permute-start.8 = (bf16[128,896]{1,0:T(8,128)(2,1)S(1)}, bf16[128,896]{1,0:T(8,128)(2,1)S(1)}, u32[]{:S(2)}, u32[]{:S(2)}) collective-permute-start(bf16[128,896]{1,0:T(8,128)(2,1)S(1)} %get-tuple-element.36), channel_id=1, source_target_pairs={{0,12},{4,8},{8,4},{12,0},{16,28},{20,24},{24,20},{28,16},{1,13},{... | collective-permute-start | bytes 688136 | tf_op jit(solution)/shard_map/ppermute | solution.py:322
  39.3 12.8 %collective-permute-start.14 = (f32[8,128]{1,0:T(8,128)S(1)}, f32[8,128]{1,0:T(8,128)S(1)}, u32[]{:S(2)}, u32[]{:S(2)}) collective-permute-start(f32[8,128]{1,0:T(8,128)S(1)} %shard_map.75.refs_0_), channel_id=1, source_target_pairs={{0,12},{4,8},{8,4},{12,0},{16,28},{20,24},{24,20},{28,16},{1,13},{... | collective-permute-start | bytes 12296 | tf_op jit(solution)/shard_map/ppermute | solution.py:322
  41.6 10.5 %collective-permute-start.13 = (f32[8,128]{1,0:T(8,128)S(1)}, f32[8,128]{1,0:T(8,128)S(1)}, u32[]{:S(2)}, u32[]{:S(2)}) collective-permute-start(f32[8,128]{1,0:T(8,128)S(1)} %shard_map.75.refs_0_), channel_id=1, source_target_pairs={{0,8},{4,12},{8,0},{12,4},{16,24},{20,28},{24,16},{28,20},{1,9},{5... | collective-permute-start | bytes 12296 | tf_op jit(solution)/shard_map/ppermute | solution.py:322
  45.9 6.2 %collective-permute-start.12 = (f32[8,128]{1,0:T(8,128)S(1)}, f32[8,128]{1,0:T(8,128)S(1)}, u32[]{:S(2)}, u32[]{:S(2)}) collective-permute-start(f32[8,128]{1,0:T(8,128)S(1)} %shard_map.75.refs_0_), channel_id=1, source_target_pairs={{0,4},{4,0},{8,12},{12,8},{16,20},{20,16},{24,28},{28,24},{1,5},{5... | collective-permute-start | bytes 12296 | tf_op jit(solution)/shard_map/ppermute | solution.py:322

commit v3 on v1

v3 whole, which is shorter than its diff:
```python
import functools
import jax
import jax.numpy as jnp
from jax import lax
from jax.experimental import pallas as pl
from jax.experimental.pallas import tpu as pltpu
from jax.sharding import PartitionSpec as P

N = 128
GROUP = 128

epsilon = 1e-06
PIECES = 2

F32 = jnp.float32
BF16 = jnp.bfloat16
HIGHEST = lax.Precision.HIGHEST
LIMIT = 48 * 1024 * 1024

VMEM = pl.BlockSpec(memory_space=pltpu.VMEM)
ANY = pl.BlockSpec(memory_space=pl.ANY)
SMEM = pl.BlockSpec(memory_space=pltpu.SMEM)


def dot(a, b, contract=((1,), (0,)), precision=None):
    return lax.dot_general(a, b, (contract, ((), ())), preferred_element_type=F32, precision=precision)


def iota(shape, dim):
    return lax.broadcasted_iota(jnp.int32, shape, dim)


def split(x):
    high = x.astype(BF16)
    return high, (x - high.astype(F32)).astype(BF16)


def cumulative_by_position(log_decay):
    upto = (iota((GROUP, GROUP), 1) <= iota((GROUP, GROUP), 0)).astype(F32)
    return dot(upto, log_decay, ((1,), (1,)), HIGHEST)


def cumulative_by_head(log_decay):
    upto = (iota((GROUP, GROUP), 0) <= iota((GROUP, GROUP), 1)).astype(F32)
    return dot(log_decay, upto, precision=HIGHEST)


def spread(x, first_head, lanes, head_dim):
    heads = x.shape[1]
    member = (iota((heads, lanes), 0) == first_head + iota((heads, lanes), 1) // head_dim).astype(BF16)
    return dot(jnp.concatenate(split(x), axis=1), jnp.concatenate([member, member], axis=0))


INDEX, WHICH, OWN, HELD = range(4)


def start_all(pairs, sems):
    copies = [pltpu.make_async_copy(source, target, sems.at[i]) for i, (source, target) in enumerate(pairs)]
    for copy in copies:
        copy.start()
    return copies


def head_rows(lanes, head_dim):
    return -(-(lanes // head_dim) // 8) * 8


def tiles_of(x):
    return [x[i : i + 1, j : j + 128] for i in range(x.shape[0]) for j in range(0, x.shape[1], 128)]


def notes_rows(tiles, width):
    return -(-tiles // (width // 128) // 8) * 8


def notes(tiles, width):
    per = width // 128
    rows = notes_rows(len(tiles), width)
    tiles = tiles + [jnp.zeros((1, 128), F32)] * (rows * per - len(tiles))
    rows = [jnp.concatenate(tiles[i : i + per], axis=1) for i in range(0, len(tiles), per)]
    return jnp.concatenate(rows, axis=0).astype(BF16)


def read_notes(ref, counts):
    tiles = tiles_of(ref[pl.ds(N, ref.shape[0] - N), :].astype(F32))
    runs = []
    for count in counts:
        runs.append(tiles[:count])
        tiles = tiles[count:]
    return runs


def wide(tiles):
    return jnp.concatenate(tiles, axis=1)


def heads_of(tiles, rows):
    return jnp.concatenate(tiles + [jnp.zeros((1, 128), F32)] * (rows - len(tiles)), axis=0)


def pieces_of(x):
    return [y.astype(F32) for y in split(x)]


def part_counts(lanes, head_dim):
    return [lanes // 128] * 2 + [lanes // head_dim] * 2


def state_kernel(head_dim, place, kq_from, values_from, log_decay_from, *refs):
    *parts, kq, values, log_decay, sems = refs
    copies = start_all([(log_decay_from, log_decay), (kq_from, kq), (values_from, values)], sems)
    lanes = parts[0].shape[1]
    part_heads = lanes // head_dim
    copies[0].wait()
    ld = log_decay[...]
    heads = ld.shape[0]
    by_position = cumulative_by_position(ld)
    final = by_position[GROUP - 1 :, :]
    decay_left = jnp.exp(final - by_position)
    last = jnp.broadcast_to(jnp.exp(final), (8, heads))
    growth = split(jnp.exp(cumulative_by_head(ld)))
    copies[1].wait()
    query_sums = dot(growth[0], kq[:, N:]) + dot(growth[1], kq[:, N:])
    keys = jnp.transpose(kq[:, :N])
    wides = []
    for m, part in enumerate(parts):
        first = (place[OWN] ^ m) * part_heads
        broad = spread(jnp.concatenate([decay_left, last], axis=0), first, lanes, head_dim)
        wides.append(broad[:GROUP])
        own = iota((head_rows(lanes, head_dim), heads), 1) == first + iota((head_rows(lanes, head_dim), heads), 0)
        mine = dot(own.astype(F32), query_sums, precision=HIGHEST)
        tiles = [tile for x in pieces_of(broad[GROUP : GROUP + 1]) for tile in tiles_of(x)]
        tiles += [tile for x in pieces_of(mine[:part_heads]) for tile in tiles_of(x)]
        below = notes(tiles, lanes)
        part[pl.ds(N, below.shape[0]), :] = below
    copies[2].wait()
    for m, part in enumerate(parts):
        start = pl.multiple_of((place[OWN] ^ m) * lanes, 128)
        weighted = (values[:, pl.ds(start, lanes)].astype(F32) * wides[m]).astype(BF16)
        part[pl.ds(0, N), :] = dot(keys, weighted).astype(BF16)


def part_notes(part, head_dim):
    lanes = part.shape[1]
    high, low, query_high, query_low = read_notes(part, part_counts(lanes, head_dim))
    rows = head_rows(lanes, head_dim)
    queries = jnp.concatenate([heads_of(query_high, rows), heads_of(query_low, rows)], axis=0)
    return wide(high) + wide(low), queries


def block_kernel(head_dim, kq_from, values_from, log_decay_from, skip, out, wide_growth, sums, kept, *scratch):
    kq, values, log_decay, sems = scratch
    copies = start_all([(kq_from, kq), (values_from, values), (log_decay_from, log_decay)], sems)
    for copy in copies:
        copy.wait()
    ld = log_decay[...]
    by_position = cumulative_by_position(ld)
    by_head = cumulative_by_head(ld)
    queries = kq[:, N:]
    kept[...] = queries
    scores = dot(queries, kq[:, :N], ((1,), (1,)))
    causal = iota((GROUP, GROUP), 0) >= iota((GROUP, GROUP), 1)
    per = 128 // head_dim
    lane = iota((GROUP, 128), 1) // head_dim
    lane_row = iota((1, 128), 1) // head_dim
    tiles = values.shape[1] // 128
    part_tiles = tiles // (sums.shape[0] // 8)
    sums[...] = jnp.zeros_like(sums)
    for i in range(tiles):
        at = slice(i * 128, (i + 1) * 128)
        value = values[:, at]
        mixes, tops = [], []
        direct = jnp.zeros((1, 128), F32)
        growth = None
        for j in range(per):
            h = i * per + j
            here = jnp.broadcast_to(by_position[:, h : h + 1], (GROUP, 128))
            gap = here - by_head[h : h + 1, :]
            mixes.append((scores * jnp.exp(jnp.where(causal, gap, -jnp.inf))).astype(BF16))
            tops.append(jnp.where(lane == j, value, jnp.zeros_like(value)))
            direct = jnp.where(lane_row == j, skip[h], direct)
            growth = here if growth is None else jnp.where(lane == j, here, growth)
        mixed = dot(jnp.concatenate(mixes, axis=1), jnp.concatenate(tops, axis=0))
        mixed = mixed + direct * value.astype(F32)
        out[:, at] = mixed
        wide_growth[:, at] = jnp.exp(growth)
        line = i // part_tiles * 8 + i % part_tiles
        sums[line : line + 1, :] = jnp.sum(mixed, axis=0, keepdims=True)


def total_kernel(head_dim, count, width, place, *refs):
    parts, total, ordered, factors = refs[:count], *refs[count:]
    for m, part in enumerate(parts):
        ordered[place[INDEX] ^ m] = part[pl.ds(0, N), pl.ds(0, width)]
        factors[place[INDEX] ^ m] = part_notes(part, head_dim)[0][:, :width]
    running = ordered[0].astype(F32)
    for j in range(1, count):
        running = factors[j] * running + ordered[j].astype(F32)
    total[...] = running.astype(BF16)


def totals_kernel(head_dim, count, pair, place, sums, *refs):
    parts, refs = refs[:count], refs[count:]
    *totals, ordered, factors, queries = refs
    if not pair:
        *totals, decay = totals
    lanes = parts[0].shape[1]
    rows = head_rows(lanes, head_dim)
    for m, part in enumerate(parts):
        ordered[place[INDEX] ^ m] = part[pl.ds(0, N), :]
        factors[place[INDEX] ^ m], queries[place[INDEX] ^ m] = part_notes(part, head_dim)
    running = ordered[0].astype(F32)
    factor = factors[0]
    if pair:
        own = (iota((rows, lanes), 0) == iota((rows, lanes), 1) // head_dim).astype(F32) / head_dim
        weight = queries[0, pl.ds(0, rows), :] + queries[0, pl.ds(rows, rows), :]
        carried = jnp.zeros((rows, lanes), F32)
    for j in range(1, count):
        if pair:
            by_head = jnp.sum(own * factor, axis=1, keepdims=True)
            weight = weight + by_head * (queries[j, pl.ds(0, rows), :] + queries[j, pl.ds(rows, rows), :])
            carried = carried + heads_dot(queries[j].astype(BF16), running.astype(BF16))
        factor = factor * factors[j]
        running = factors[j] * running + ordered[j].astype(F32)
    at = lanes - sum(total.shape[1] for total in totals)
    for total in totals:
        total[pl.ds(0, N), :] = running[:, at : at + total.shape[1]].astype(BF16)
        at += total.shape[1]
    if pair:
        base = own_heads(carried, head_dim) + own_sums(place, sums, lanes)
        tiles = [tile for x in thirds(base) for tile in tiles_of(x.astype(F32))]
        tiles += [tile for x in pieces_of(weight[: lanes // head_dim]) for tile in tiles_of(x)]
        below = notes(tiles, totals[-1].shape[1])
        totals[-1][pl.ds(N, below.shape[0]), :] = below
    else:
        decay[...] = factor


def own_sums(place, sums, lanes):
    own = sums[pl.ds(pl.multiple_of(place[OWN] * 8, 8), 8), :]
    return wide([own[i : i + 1] for i in range(lanes // 128)])


def starts_kernel(head_dim, count, at, place, *refs):
    parts, outs, refs, scratch = refs[-3 - 2 * count : -3 - count], refs[-3 - count : -3], refs[: -3 - 2 * count], refs[-3:]
    ordered, factors, results = scratch
    lanes, width = parts[0].shape[1], outs[0].shape[1]
    for m, part in enumerate(parts):
        ordered[place[INDEX] ^ m] = part[pl.ds(0, N), pl.ds(at, width)]
        factors[place[INDEX] ^ m] = part_notes(part, head_dim)[0][:, at : at + width]
    running = jnp.where(place[WHICH] == 0, 0.0, refs[-1][pl.ds(0, N), :].astype(F32))
    for j in range(count):
        results[j] = running.astype(BF16)
        if j < count - 1:
            running = factors[j] * running + ordered[j].astype(F32)
    if len(refs) > 1:
        sums = sums_of(place, head_dim, lanes, refs[: len(refs) // 2], refs[len(refs) // 2 :])
        below = notes([tile for x in thirds(sums) for tile in tiles_of(x.astype(F32))], width)
    for m, out in enumerate(outs):
        out[pl.ds(0, N), :] = results[place[INDEX] ^ m]
        if len(refs) > 1:
            out[pl.ds(N, below.shape[0]), :] = below


def sums_of(place, head_dim, lanes, totals, before):
    first = place[WHICH] == 0
    rows = head_rows(lanes, head_dim)
    counts = [lanes // 128] * 3 + [lanes // head_dim] * 2
    mine, other = read_notes(totals[-1], counts), read_notes(before[-1], counts)
    weight = [
        jnp.where(first, heads_of(there, rows), heads_of(here, rows)) for here, there in zip(mine[3:], other[3:])
    ]
    state = [
        jnp.where(first, total[pl.ds(0, N), :].astype(F32), got[pl.ds(0, N), :].astype(F32)).astype(BF16)
        for total, got in zip(totals, before)
    ]
    product = heads_dot(jnp.concatenate(weight, axis=0).astype(BF16), wide(state))
    both = sum(wide(here) + wide(there) for here, there in zip(mine[:3], other[:3]))
    return own_heads(product, head_dim) + both


def thirds(x):
    high = x.astype(BF16)
    return high, *split(x - high.astype(F32))


def heads_dot(queries, state):
    both = dot(queries, state)
    rows = queries.shape[0] // 2
    return both[:rows] + both[rows:]


def own_heads(x, head_dim):
    mine = iota(x.shape, 0) == iota(x.shape, 1) // head_dim
    return jnp.sum(jnp.where(mine, x, 0.0), axis=0, keepdims=True)


def sums_kernel(head_dim, count, place, sums, *refs):
    parts, states, out = refs[:count], refs[count:-1], refs[-1]
    carried = 0.0
    for m, part in enumerate(parts):
        state = wide([x[pl.ds(0, N), :] for x in states[m::count]])
        carried = carried + heads_dot(part_notes(part, head_dim)[1].astype(BF16), state)
    out[...] = own_heads(carried, head_dim) + own_sums(place, sums, out.shape[1])


def output_kernel(ms, count, lanes, offset, step, positions, place, queries, local, wide_growth, *refs):
    carried, refs = refs[: len(ms)], refs[len(ms) :]
    *refs, made, sems = refs
    copies = []
    at = [pl.multiple_of((place[OWN] ^ m) * lanes + offset, 128) for m in ms]
    width = carried[0].shape[1]
    mixed = refs[{0: -1, 1: -2, 2: -3}[step]]
    for i, state in enumerate(carried):
        here = pl.ds(at[i], width)
        made[i] = (local[:, here] + wide_growth[:, here] * dot(queries[...], state[pl.ds(0, N), :])).astype(BF16)
        copies.append(pltpu.make_async_copy(made.at[i], mixed.at[:, here], sems.at[i]))
        copies[-1].start()
    if step:
        whole = shares_of(ms, lanes, positions, place, carried, refs[:count])
    if step == 1:
        refs[-1][...] = whole
    if step == 2:
        whole = whole + refs[count][...]
        logits, scaled = refs[-2], refs[-1]
        scaled[...] = jnp.broadcast_to(whole[0:1] / jnp.sqrt(whole[1:2] / (lanes * count) + epsilon), scaled.shape)
        copies.append(pltpu.make_async_copy(scaled.at[pl.ds(0, 1)], logits, sems.at[len(ms)]))
        copies[-1].start()
    for copy in copies:
        copy.wait()


def shares_of(ms, lanes, positions, place, carried, weights):
    whole = 0.0
    row = iota((8, weights[0].shape[1]), 0)
    for m, state in zip(ms, carried):
        pooled = sum(wide(x) for x in read_notes(state, [lanes // 128] * 3)) / positions
        high, low = split(jnp.broadcast_to(pooled, (8, lanes)))
        distance = place[HELD] ^ place[OWN] ^ m
        rows = weights[0][...]
        for k in range(1, len(weights)):
            rows = jnp.where(distance == k, weights[k][...], rows)
        product = dot(high, rows) + dot(low, rows)
        square = jnp.sum(pooled * pooled, axis=1, keepdims=True)
        whole = whole + jnp.where(row == 0, product, jnp.where(row == 1, square, 0.0))
    return whole


def call(kernel, outs, in_specs, scratch=(), flops=0, moved=0, out_specs=None, aliases=None):
    return pl.pallas_call(
        kernel,
        out_shape=outs,
        in_specs=in_specs,
        out_specs=out_specs or jax.tree.map(lambda _: VMEM, outs),
        scratch_shapes=scratch,
        input_output_aliases=aliases or {},
        cost_estimate=pl.CostEstimate(flops=flops, bytes_accessed=moved, transcendentals=0),
        compiler_params=pltpu.CompilerParams(vmem_limit_bytes=LIMIT),
    )


def local(inputs, keys_queries, log_decay, skip, classifier):
    _, positions, channels = inputs.shape
    heads = log_decay.shape[1]
    head_dim = channels // heads
    size, wide = lax.axis_size("seq"), lax.axis_size("fsdp")
    group = wide
    pair = size == 2 * group
    lanes = channels // group
    classes = classifier.shape[1]
    index, column = lax.axis_index("seq"), lax.axis_index("fsdp")
    place = jnp.stack([index % group, index // group, (index % group) ^ column, column]).astype(jnp.int32)
    values, kq, ld = inputs[0], keys_queries[0], log_decay[0]
    sources = [pltpu.with_memory_space_constraint(x, pltpu.HBM) for x in (kq, values, ld)]
    landing = [pltpu.VMEM(x.shape, x.dtype) for x in (kq, values, ld)] + [pltpu.SemaphoreType.DMA((3,))]
    part = jax.ShapeDtypeStruct((N + notes_rows(sum(part_counts(lanes, head_dim)), lanes), lanes), BF16)
    state = jax.ShapeDtypeStruct((N, lanes), BF16)
    row = jax.ShapeDtypeStruct((1, lanes), F32)
    full = jax.ShapeDtypeStruct((positions, channels), F32)
    share = jax.ShapeDtypeStruct((8, classes), F32)
    rows = head_rows(lanes, head_dim)

    def swap(x, m, axis="seq"):
        return lax.ppermute(x, axis, [(i, i ^ m) for i in range(lax.axis_size(axis))])

    def swap_all(xs, axis="seq"):
        return [xs[0]] + [swap(xs[m], m, axis) for m in range(1, group)]

    def shift(x, by):
        return lax.ppermute(x, "seq", [(i, i + by) for i in range(size - by)])

    parts = call(
        functools.partial(state_kernel, head_dim),
        [part] * group,
        [SMEM] + [ANY] * 3,
        landing,
        flops=2 * positions * N * channels,
        moved=4 * positions * channels,
    )(place, *sources)
    parts, skip, classifier = lax.optimization_barrier((parts, skip, classifier))
    parts = swap_all(parts)
    crossed = swap(classifier, 2, "fsdp")
    made = call(
        functools.partial(block_kernel, head_dim),
        [full, full, jax.ShapeDtypeStruct((8 * group, 128), F32), jax.ShapeDtypeStruct((positions, N), BF16)],
        [ANY] * 3 + [SMEM],
        landing,
        flops=8 * positions * N * channels,
        moved=6 * positions * channels,
    )(*sources, skip)
    from_block, wide_growth, sums, queries = made
    guard = lax.optimization_barrier((place, made, crossed))[0]
    reach = 1
    while reach < group:
        sums = sums + swap(sums, reach)
        reach *= 2

    tiles = lanes // 128
    widths = [(tiles + 1) // 2 * 128, tiles // 2 * 128] if PIECES == 2 else [lanes]
    offsets = [0, widths[0]][:PIECES]
    pieces = [jax.ShapeDtypeStruct((N, width), BF16) for width in widths]

    def with_notes(count):
        return [*pieces[:-1], jax.ShapeDtypeStruct((N + notes_rows(count, widths[-1]), widths[-1]), BF16)]

    totals = []
    if pair and PIECES == 2:
        totals.append(
            call(
                functools.partial(total_kernel, head_dim, group, widths[0]),
                pieces[0],
                [SMEM] + [VMEM] * group,
                [pltpu.VMEM((group, N, widths[0]), BF16), pltpu.VMEM((group, 1, widths[0]), F32)],
            )(guard, *parts)
        )
        guard = lax.optimization_barrier((place, totals))[0]
    totals += call(
        functools.partial(totals_kernel, head_dim, group, pair),
        with_notes(3 * tiles + 2 * (lanes // head_dim))[-1:] if pair else [*pieces, row],
        [SMEM] + [VMEM] * (1 + group),
        [
            pltpu.VMEM((group, *state.shape), BF16),
            pltpu.VMEM((group, *row.shape), F32),
            pltpu.VMEM((group, 2 * rows, N), F32),
        ],
    )(guard, sums, *parts)
    classifier, crossed = lax.optimization_barrier((classifier, crossed, totals))[:2]
    if pair:
        before = [swap(total, group) for total in totals]
        across = [*totals, *before]
    else:
        *totals, decay = totals
        before = []
        for total, at, width in zip(totals, offsets, widths):
            running, factor = shift(total, group).astype(F32), shift(decay[:, at : at + width], group)
            reach = 1
            while reach < size // group - 1:
                running = running + factor * shift(running, group * reach)
                factor = factor * shift(factor, group * reach)
                reach *= 2
            before.append(running.astype(BF16))
    weights = [classifier, swap(classifier, 1, "fsdp"), crossed, swap(crossed, 1, "fsdp")]

    starts = []
    for k, (width, at) in enumerate(zip(widths, offsets)):
        last = k == PIECES - 1
        operands = across if last and pair else [before[k]]
        starts.append(
            call(
                functools.partial(starts_kernel, head_dim, group, at),
                [with_notes(3 * tiles)[k] if pair else pieces[k]] * group,
                [SMEM] + [VMEM] * (len(operands) + group),
                [
                    pltpu.VMEM((group, N, width), BF16),
                    pltpu.VMEM((group, 1, width), F32),
                    pltpu.VMEM((group, N, width), BF16),
                ],
            )(place, *operands, *parts)
        )
    if not pair:
        whole = call(
            functools.partial(sums_kernel, head_dim, group), row, [SMEM] + [VMEM] * (1 + (1 + PIECES) * group)
        )(place, sums, *parts, *[x for piece in starts for x in piece])
        reach = group
        while reach < size:
            whole = whole + swap(whole, reach)
            reach *= 2
        below = notes([tile for x in thirds(whole) for tile in tiles_of(x.astype(F32))], widths[-1])
        starts[-1] = [jnp.concatenate([x, below], axis=0) for x in starts[-1]]
    starts = [swap_all(x) for x in starts]

    plan = [(tuple(range(group)), k, 0) for k in range(PIECES - 1)]
    plan += [(tuple(range(group - 1)), PIECES - 1, 1), ((group - 1,), PIECES - 1, 2)]
    mixed = shares = logits = None
    for i, (ms, k, step) in enumerate(plan):
        extra = [*weights] if step else []
        extra += [shares] if step == 2 else []
        operands = [queries, from_block, wide_growth, *[starts[k][m] for m in ms], *extra]
        outs = [pltpu.HBM((positions, channels), BF16)]
        outs += {0: [], 1: [share], 2: [pltpu.HBM((1, classes), F32)]}[step]
        scratch = [pltpu.VMEM(share.shape, F32)] if step == 2 else []
        mixed, *rest = call(
            functools.partial(output_kernel, ms, group, lanes, offsets[k], step, positions * size),
            outs,
            [SMEM] + [VMEM] * len(operands) + [ANY] * (i > 0),
            scratch
            + [
                pltpu.VMEM((len(ms), positions, widths[k]), BF16),
                pltpu.SemaphoreType.DMA((len(ms) + 1,)),
            ],
            out_specs=[ANY] + {0: [], 1: [VMEM], 2: [ANY]}[step],
            aliases={1 + len(operands): 0} if i else None,
        )(place, *operands, *([mixed] if i else []))
        if step == 1:
            (shares,) = rest
        if step == 2:
            (logits,) = rest
    return mixed[None], logits


def solution(mesh):
    return jax.shard_map(
        local,
        mesh=mesh,
        in_specs=(
            P("fsdp", "seq", None),
            P("fsdp", "seq", None),
            P("fsdp", None, "seq"),
            P(),
            P("fsdp", None),
        ),
        out_specs=(P("fsdp", "seq", None), P("fsdp", None)),
        check_vma=False,
    )
```

time: 73.8 us -> 46 us (0.62)
  waiting for transfers between devices: 27.4 us -> 7.88 us
  blocking collectives: 9.29 us -> 0 us
  Pallas kernels: 7.34 us -> 14.2 us
  local copies, waits for them, and re-layouts: 2.78 us -> 0.66 us
  starting transfers between devices: 23.9 us -> 22.2 us
  matrix products: 0.75 us -> 0 us
    ppermute x10 -> x16, waiting for transfers between devices: 27.4 us -> 7.88 us  [swap(): lax.ppermute(x, axis, [(i, i ^ m) for i in range(lax.axis_size(axis))])]
    all_gather x1 -> x0, blocking collectives: 9.29 us -> none  [local(): gathered = lax.all_gather(classifier, 'fsdp', axis=0, tiled=True)]
    pallas_call x4 -> x8, Pallas kernels: 5.71 us -> 11.6 us  [the longest x3 4.66 us: local(): call(functools.partial(output_kernel, ms, group, lanes, offsets[k], step,...]
    unnamed x14 -> x4, local copies, waits for them, and re-layouts: 2.78 us -> 0.66 us
    ppermute x10 -> x16, starting transfers between devices: 23.9 us -> 22.2 us  [swap(): lax.ppermute(x, axis, [(i, i ^ m) for i in range(lax.axis_size(axis))])]
    pallas_call x1, Pallas kernels: 1.63 us -> 2.65 us  [local(): call(functools.partial(state_kernel, head_dim), [part] * group, [SMEM] +...]
    dot_general x1 -> x0, matrix products: 0.75 us -> none  [local(): logits = jnp.dot(normed, gathered, preferred_element_type=F32)]
  transfers between devices with their start and end apart: 10 -> 16, of which waited for: 8 -> 6; matrix products, arithmetic and copies ran while one was open for 0% -> 0% of each run, Pallas kernels for 3% -> 22%
where the time goes in v3:
time: 46 us; the launch traced here: 45.8 us
  starting transfers between devices  22.2 us (48%)
  Pallas kernels  14.2 us (31%)
  waiting for transfers between devices  7.88 us (17%)
  between operations  0.77 us (2%)
  local copies, waits for them, and re-layouts  0.66 us (1%)
    ppermute x16, starting transfers between devices, swap(): lax.ppermute(x, axis, [(i, i ^ m) for i in range(lax.axis_size(axis))])  22.2 us
    ppermute x16, waiting for transfers between devices, swap(): lax.ppermute(x, axis, [(i, i ^ m) for i in range(lax.axis_size(axis))])  7.88 us
    pallas_call x3, Pallas kernels, local(): call(functools.partial(output_kernel, ms, group, lanes, offsets[k], step,...  4.66 us
    pallas_call x1, Pallas kernels, local(): call(functools.partial(block_kernel, head_dim), [full, full, jax.ShapeDty...  3.69 us
    pallas_call x1, Pallas kernels, local(): call(functools.partial(state_kernel, head_dim), [part] * group, [SMEM] +...  2.65 us
    pallas_call x2, Pallas kernels, local(): call(functools.partial(starts_kernel, head_dim, group, at), [with_notes(3...  1.57 us
    pallas_call x1, Pallas kernels, local(): call(functools.partial(totals_kernel, head_dim, group, pair), with_notes(...  0.93 us
  transfers between devices with their start and end apart: 16, of which 6 were waited for; matrix products, arithmetic and copies ran while one was open for 0% of the time, Pallas kernels for 22%

profile of v3, /device:TPU:0, one launch (start us, length us, event | category | flops | bytes accessed | tf_op | source)
XLA Modules:
  0.0 45.8 jit_solution(388808559512609580)
XLA Ops:
  0.7 0.1 pad_add_fusion.place
  0.7 2.7 %shard_map.68 = (bf16[136,896]{1,0:T(8,128)(2,1)S(1)}, bf16[136,896]{1,0:T(8,128)(2,1)S(1)}, bf16[136,896]{1,0:T(8,128)(2,1)S(1)}, bf16[136,896]{1,0:T(8,128)(2,1)S(1)}) custom-call(s32[4]{0:T(128)S(1)} %pad_add_fusion.place, bf16[128,256]{1,0:T(8,128)(2,1)} %bitcast.11, bf16[128,3584]{1,0:T(8,128)(2,1)} %bitcast.9, f32[56,128]{1,0:T(8,128)} %bitcast.13), custom_call_target="tpu_custom_call" | custom-call | flops 117440512 | bytes 1835008 | tf_op jit(solution)/shard_map/pallas_call | solution.py:392
  3.4 3.0 %collective-permute-start.1 = (bf16[136,896]{1,0:T(8,128)(2,1)S(1)}, bf16[136,896]{1,0:T(8,128)(2,1)S(1)}, u32[]{:S(2)}, u32[]{:S(2)}) collective-permute-start(bf16[136,896]{1,0:T(8,128)(2,1)S(1)} %get-tuple-element.44), channel_id=1, source_target_pairs={{0,4},{4,0},{8,12},{12,8},{16,20},{20,16},{24,28},{28,24},{1,5},{5... | collective-permute-start | bytes 731144 | tf_op jit(solution)/shard_map/ppermute | solution.py:384
  6.4 1.6 %collective-permute-start.2 = (bf16[136,896]{1,0:T(8,128)(2,1)S(1)}, bf16[136,896]{1,0:T(8,128)(2,1)S(1)}, u32[]{:S(2)}, u32[]{:S(2)}) collective-permute-start(bf16[136,896]{1,0:T(8,128)(2,1)S(1)} %get-tuple-element.45), channel_id=1, source_target_pairs={{0,8},{4,12},{8,0},{12,4},{16,24},{20,28},{24,16},{28,20},{1,9},{5... | collective-permute-start | bytes 731144 | tf_op jit(solution)/shard_map/ppermute | solution.py:384
  8.0 0.0 collective-permute-start.3
  8.0 1.9 %collective-permute-start = (bf16[896,128]{1,0:T(8,128)(2,1)}, bf16[896,128]{1,0:T(8,128)(2,1)S(1)}, u32[]{:S(2)}, u32[]{:S(2)}) collective-permute-start(bf16[896,128]{1,0:T(8,128)(2,1)} %refs_1_), channel_id=1, source_target_pairs={{0,2},{1,3},{2,0},{3,1},{4,6},{5,7},{6,4},{7,5},{8,10},{9,11},{10,... | collective-permute-start | bytes 688136 | tf_op jit(solution)/shard_map/ppermute | solution.py:384
  9.9 0.0 copy-start.1
  9.9 0.7 %copy-done.1 = f32[56]{0:T(128)S(1)} copy-done((f32[56]{0:T(128)S(1)}, f32[56]{0:T(128)}, u32[]{:S(2)}) %copy-start.1) | copy-done | bytes 248
  10.5 3.7 %shard_map.69 = (f32[128,3584]{1,0:T(8,128)S(1)}, f32[128,3584]{1,0:T(8,128)S(1)}, f32[32,128]{1,0:T(8,128)S(1)}, bf16[128,128]{1,0:T(8,128)(2,1)S(1)}) custom-call(bf16[128,256]{1,0:T(8,128)(2,1)} %bitcast.12, bf16[128,3584]{1,0:T(8,128)(2,1)} %bitcast.10, f32[56,128]{1,0:T(8,128)} %bitcast.14, f32[56]{0:T(128)S(1)} %copy-done.1), custom_call_target="tpu_custom_call" | custom-call | flops 469762048 | bytes 2752512 | tf_op jit(solution)/shard_map/pallas_call | solution.py:403
  14.2 0.0 copy-start
  14.2 1.6 %collective-permute-start.4 = (f32[32,128]{1,0:T(8,128)S(1)}, f32[32,128]{1,0:T(8,128)S(1)}, u32[]{:S(2)}, u32[]{:S(2)}) collective-permute-start(f32[32,128]{1,0:T(8,128)S(1)} %get-tuple-element.40), channel_id=1, source_target_pairs={{0,4},{4,0},{8,12},{12,8},{16,20},{20,16},{24,28},{28,24},{1,5},{5... | collective-permute-start | bytes 49160 | tf_op jit(solution)/shard_map/ppermute | solution.py:384
  15.8 0.0 collective-permute-done.refs_5_.refs_3_
  15.8 0.0 collective-permute-done.1.refs_1_.refs_5_.refs_2_
  15.8 0.0 collective-permute-done.2.refs_2_.refs_6_.refs_3_
  15.8 3.1 %collective-permute-done.3.refs_3_.refs_7_.refs_4_ = bf16[136,896]{1,0:T(8,128)(2,1)S(1)} collective-permute-done((bf16[136,896]{1,0:T(8,128)(2,1)S(1)}, bf16[136,896]{1,0:T(8,128)(2,1)S(1)}, u32[]{:S(2)}, u32[]{:S(2)}) %collective-permute-start.3) | collective-permute-done | bytes 243744 | tf_op jit(solution)/shard_map/ppermute | solution.py:384
  18.9 0.7 %shard_map.70.refs_0_ = bf16[128,512]{1,0:T(8,128)(2,1)S(1)} custom-call(s32[4]{0:T(128)S(1)} %pad_add_fusion.place, bf16[136,896]{1,0:T(8,128)(2,1)S(1)} %get-tuple-element.43.refs_0_.refs_4_.refs_1_, bf16[136,896]{1,0:T(8,128)(2,1)S(1)} %collective-permute-done.1.refs_1_.refs_5_.refs_2_, ...), custom_call_target="tpu_custom_call" | custom-call | tf_op jit(solution)/shard_map/pallas_call | solution.py:429
  19.6 2.8 %collective-permute-start.6 = (bf16[128,512]{1,0:T(8,128)(2,1)S(1)}, bf16[128,512]{1,0:T(8,128)(2,1)S(1)}, u32[]{:S(2)}, u32[]{:S(2)}) collective-permute-start(bf16[128,512]{1,0:T(8,128)(2,1)S(1)} %shard_map.70.refs_0_), channel_id=1, source_target_pairs={{0,16},{4,20},{8,24},{12,28},{16,0},{20,4},{24,8},{28,12},{1,17},{... | collective-permute-start | bytes 393224 | tf_op jit(solution)/shard_map/ppermute | solution.py:384
  22.4 0.0 collective-permute-done.4
  22.4 1.6 %collective-permute-start.5 = (f32[32,128]{1,0:T(8,128)S(1)}, f32[32,128]{1,0:T(8,128)S(1)}, u32[]{:S(2)}, u32[]{:S(2)}) collective-permute-start(f32[32,128]{1,0:T(8,128)S(1)} %add.13), channel_id=1, source_target_pairs={{0,8},{4,12},{8,0},{12,4},{16,24},{20,28},{24,16},{28,20},{1,9},{5... | collective-permute-start | bytes 49160 | tf_op jit(solution)/shard_map/ppermute | solution.py:384
  24.1 2.2 %collective-permute-done.5 = f32[32,128]{1,0:T(8,128)S(1)} collective-permute-done((f32[32,128]{1,0:T(8,128)S(1)}, f32[32,128]{1,0:T(8,128)S(1)}, u32[]{:S(2)}, u32[]{:S(2)}) %collective-permute-start.5) | collective-permute-done | bytes 16416 | tf_op jit(solution)/shard_map/ppermute | solution.py:384
  26.2 0.9 %shard_map.71.refs_1_ = bf16[152,384]{1,0:T(8,128)(2,1)S(1)} custom-call(s32[4]{0:T(128)S(1)} %pad_add_fusion.place, f32[32,128]{1,0:T(8,128)S(1)} %add.14.sums, bf16[136,896]{1,0:T(8,128)(2,1)S(1)} %get-tuple-element.43.refs_0_.refs_4_.refs_1_, bf16[136,896]{1,0:T(8,128)(2,1)S(1)} %collective-permute-done.1.refs_1_.refs_5_.refs_2_, ...), custom_call_target="tpu_custom_call" | custom-call | tf_op jit(solution)/shard_map/pallas_call | solution.py:437
  27.2 1.3 %collective-permute-start.7 = (bf16[152,384]{1,0:T(8,128)(2,1)S(1)}, bf16[152,384]{1,0:T(8,128)(2,1)S(1)}, u32[]{:S(2)}, u32[]{:S(2)}) collective-permute-start(bf16[152,384]{1,0:T(8,128)(2,1)S(1)} %shard_map.71.refs_1_), channel_id=1, source_target_pairs={{0,16},{4,20},{8,24},{12,28},{16,0},{20,4},{24,8},{28,12},{1,17},{... | collective-permute-start | bytes 350216 | tf_op jit(solution)/shard_map/ppermute | solution.py:384
  28.5 0.0 collective-permute-done.6.refs_2_.refs_0_
  28.5 0.8 %shard_map.73 = (bf16[128,512]{1,0:T(8,128)(2,1)S(1)}, bf16[128,512]{1,0:T(8,128)(2,1)S(1)}, bf16[128,512]{1,0:T(8,128)(2,1)S(1)}, bf16[128,512]{1,0:T(8,128)(2,1)S(1)}) custom-call(s32[4]{0:T(128)S(1)} %pad_add_fusion.place, bf16[128,512]{1,0:T(8,128)(2,1)S(1)} %collective-permute-done.6.refs_2_.refs_0_, ...), custom_call_target="tpu_custom_call" | custom-call | tf_op jit(solution)/shard_map/pallas_call | solution.py:469
  29.3 1.6 %collective-permute-start.13 = (bf16[128,512]{1,0:T(8,128)(2,1)S(1)}, bf16[128,512]{1,0:T(8,128)(2,1)S(1)}, u32[]{:S(2)}, u32[]{:S(2)}) collective-permute-start(bf16[128,512]{1,0:T(8,128)(2,1)S(1)} %get-tuple-element.55), channel_id=1, source_target_pairs={{0,4},{4,0},{8,12},{12,8},{16,20},{20,16},{24,28},{28,24},{1,5},{5... | collective-permute-start | bytes 393224 | tf_op jit(solution)/shard_map/ppermute | solution.py:384
  30.9 1.8 %collective-permute-start.14 = (bf16[128,512]{1,0:T(8,128)(2,1)S(1)}, bf16[128,512]{1,0:T(8,128)(2,1)S(1)}, u32[]{:S(2)}, u32[]{:S(2)}) collective-permute-start(bf16[128,512]{1,0:T(8,128)(2,1)S(1)} %get-tuple-element.56), channel_id=1, source_target_pairs={{0,8},{4,12},{8,0},{12,4},{16,24},{20,28},{24,16},{28,20},{1,9},{5... | collective-permute-start | bytes 393224 | tf_op jit(solution)/shard_map/ppermute | solution.py:384
  32.7 0.1 collective-permute-start.15
  32.9 0.0 copy-done
  32.9 0.0 collective-permute-start.9
  32.9 0.6 %collective-permute-done.7.refs_3_ = bf16[152,384]{1,0:T(8,128)(2,1)S(1)} collective-permute-done((bf16[152,384]{1,0:T(8,128)(2,1)S(1)}, bf16[152,384]{1,0:T(8,128)(2,1)S(1)}, u32[]{:S(2)}, u32[]{:S(2)}) %collective-permute-start.7) | collective-permute-done | bytes 116768 | tf_op jit(solution)/shard_map/ppermute | solution.py:384
  33.5 0.0 collective-permute-start.10
  33.5 0.8 %shard_map.72 = (bf16[136,384]{1,0:T(8,128)(2,1)S(1)}, bf16[136,384]{1,0:T(8,128)(2,1)S(1)}, bf16[136,384]{1,0:T(8,128)(2,1)S(1)}, bf16[136,384]{1,0:T(8,128)(2,1)S(1)}) custom-call(s32[4]{0:T(128)S(1)} %pad_add_fusion.place, bf16[128,512]{1,0:T(8,128)(2,1)S(1)} %shard_map.70.refs_0_, bf16[152,384]{1,0:T(8,128)(2,1)S(1)} %shard_map.71.refs_1_, ...), custom_call_target="tpu_custom_call" | custom-call | tf_op jit(solution)/shard_map/pallas_call | solution.py:469
  34.3 0.8 %collective-permute-done.13.refs_1_ = bf16[128,512]{1,0:T(8,128)(2,1)S(1)} collective-permute-done((bf16[128,512]{1,0:T(8,128)(2,1)S(1)}, bf16[128,512]{1,0:T(8,128)(2,1)S(1)}, u32[]{:S(2)}, u32[]{:S(2)}) %collective-permute-start.13) | collective-permute-done | bytes 131104 | tf_op jit(solution)/shard_map/ppermute | solution.py:384
  35.1 2.1 %collective-permute-start.11 = (bf16[136,384]{1,0:T(8,128)(2,1)S(1)}, bf16[136,384]{1,0:T(8,128)(2,1)S(1)}, u32[]{:S(2)}, u32[]{:S(2)}) collective-permute-start(bf16[136,384]{1,0:T(8,128)(2,1)S(1)} %get-tuple-element.52), channel_id=1, source_target_pairs={{0,4},{4,0},{8,12},{12,8},{16,20},{20,16},{24,28},{28,24},{1,5},{5... | collective-permute-start | bytes 313352 | tf_op jit(solution)/shard_map/ppermute | solution.py:384
  37.1 0.0 collective-permute-done.14.refs_2_
  37.2 1.5 %collective-permute-start.12 = (bf16[136,384]{1,0:T(8,128)(2,1)S(1)}, bf16[136,384]{1,0:T(8,128)(2,1)S(1)}, u32[]{:S(2)}, u32[]{:S(2)}) collective-permute-start(bf16[136,384]{1,0:T(8,128)(2,1)S(1)} %get-tuple-element.53), channel_id=1, source_target_pairs={{0,8},{4,12},{8,0},{12,4},{16,24},{20,28},{24,16},{28,20},{1,9},{5... | collective-permute-start | bytes 313352 | tf_op jit(solution)/shard_map/ppermute | solution.py:384
  38.6 0.1 collective-permute-done.15.refs_3_
  38.7 1.3 %collective-permute-start.8 = (bf16[136,384]{1,0:T(8,128)(2,1)S(1)}, bf16[136,384]{1,0:T(8,128)(2,1)S(1)}, u32[]{:S(2)}, u32[]{:S(2)}) collective-permute-start(bf16[136,384]{1,0:T(8,128)(2,1)S(1)} %get-tuple-element.48), channel_id=1, source_target_pairs={{0,12},{4,8},{8,4},{12,0},{16,28},{20,24},{24,20},{28,16},{1,13},{... | collective-permute-start | bytes 313352 | tf_op jit(solution)/shard_map/ppermute | solution.py:384
  40.0 1.6 %shard_map.74.refs_7_ = bf16[128,3584]{1,0:T(8,128)(2,1)} custom-call(s32[4]{0:T(128)S(1)} %pad_add_fusion.place, bf16[128,128]{1,0:T(8,128)(2,1)S(1)} %get-tuple-element.37.queries, f32[128,3584]{1,0:T(8,128)S(1)} %get-tuple-element.38.local, f32[128,3584]{1,0:T(8,128)S(1)} %get-tuple-element.39.wide_growth, ...), custom_call_target="tpu_custom_call" | custom-call | tf_op jit(solution)/shard_map/pallas_call | solution.py:502
  41.6 0.0 collective-permute-done.9.refs_4_.refs_2_
  41.6 0.0 collective-permute-done.10.refs_6_.refs_4_
  41.6 0.0 collective-permute-done.11.refs_1_
  41.6 1.1 %collective-permute-done.12.refs_2_ = bf16[136,384]{1,0:T(8,128)(2,1)S(1)} collective-permute-done((bf16[136,384]{1,0:T(8,128)(2,1)S(1)}, bf16[136,384]{1,0:T(8,128)(2,1)S(1)}, u32[]{:S(2)}, u32[]{:S(2)}) %collective-permute-start.12) | collective-permute-done | bytes 104480 | tf_op jit(solution)/shard_map/ppermute | solution.py:384
  42.7 1.7 %shard_map.75 = (bf16[128,3584]{1,0:T(8,128)(2,1)}, f32[8,128]{1,0:T(8,128)S(1)}) custom-call(s32[4]{0:T(128)S(1)} %pad_add_fusion.place, bf16[128,128]{1,0:T(8,128)(2,1)S(1)} %get-tuple-element.37.queries, f32[128,3584]{1,0:T(8,128)S(1)} %get-tuple-element.38.local, ...), custom_call_target="tpu_custom_call", output_to_operand_aliasing={{0}: (11, {})} | custom-call | tf_op jit(solution)/shard_map/pallas_call | solution.py:502
  44.4 0.0 collective-permute-done.8.refs_0_
  44.5 1.4 %shard_map.76 = (bf16[128,3584]{1,0:T(8,128)(2,1)}, f32[1,128]{1,0:T(1,128)}) custom-call(s32[4]{0:T(128)S(1)} %pad_add_fusion.place, bf16[128,128]{1,0:T(8,128)(2,1)S(1)} %get-tuple-element.37.queries, f32[128,3584]{1,0:T(8,128)S(1)} %get-tuple-element.38.local, f32[128,3584]{1,0:T(8,128)S(1)} %get-tuple-element.39.wide_growth, ...), custom_call_target="tpu_custom_call", output_to_operand_aliasing={{0}: (10, {})} | custom-call | tf_op jit(solution)/shard_map/pallas_call | solution.py:502
  (2 shorter events, 0.0 us)
Async XLA Ops:
  3.4 12.4 %collective-permute-start.1 = (bf16[136,896]{1,0:T(8,128)(2,1)S(1)}, bf16[136,896]{1,0:T(8,128)(2,1)S(1)}, u32[]{:S(2)}, u32[]{:S(2)}) collective-permute-start(bf16[136,896]{1,0:T(8,128)(2,1)S(1)} %get-tuple-element.44), channel_id=1, source_target_pairs={{0,4},{4,0},{8,12},{12,8},{16,20},{20,16},{24,28},{28,24},{1,5},{5... | collective-permute-start | bytes 731144 | tf_op jit(solution)/shard_map/ppermute | solution.py:384
  6.4 9.4 %collective-permute-start.2 = (bf16[136,896]{1,0:T(8,128)(2,1)S(1)}, bf16[136,896]{1,0:T(8,128)(2,1)S(1)}, u32[]{:S(2)}, u32[]{:S(2)}) collective-permute-start(bf16[136,896]{1,0:T(8,128)(2,1)S(1)} %get-tuple-element.45), channel_id=1, source_target_pairs={{0,8},{4,12},{8,0},{12,4},{16,24},{20,28},{24,16},{28,20},{1,9},{5... | collective-permute-start | bytes 731144 | tf_op jit(solution)/shard_map/ppermute | solution.py:384
  8.0 10.9 %collective-permute-start.3 = (bf16[136,896]{1,0:T(8,128)(2,1)S(1)}, bf16[136,896]{1,0:T(8,128)(2,1)S(1)}, u32[]{:S(2)}, u32[]{:S(2)}) collective-permute-start(bf16[136,896]{1,0:T(8,128)(2,1)S(1)} %get-tuple-element.46), channel_id=1, source_target_pairs={{0,12},{4,8},{8,4},{12,0},{16,28},{20,24},{24,20},{28,16},{1,13},{... | collective-permute-start | bytes 731144 | tf_op jit(solution)/shard_map/ppermute | solution.py:384
  8.0 7.8 %collective-permute-start = (bf16[896,128]{1,0:T(8,128)(2,1)}, bf16[896,128]{1,0:T(8,128)(2,1)S(1)}, u32[]{:S(2)}, u32[]{:S(2)}) collective-permute-start(bf16[896,128]{1,0:T(8,128)(2,1)} %refs_1_), channel_id=1, source_target_pairs={{0,2},{1,3},{2,0},{3,1},{4,6},{5,7},{6,4},{7,5},{8,10},{9,11},{10,... | collective-permute-start | bytes 688136 | tf_op jit(solution)/shard_map/ppermute | solution.py:384
  9.9 0.7 %copy-start.1 = (f32[56]{0:T(128)S(1)}, f32[56]{0:T(128)}, u32[]{:S(2)}) copy-start(f32[56]{0:T(128)} %skip) | copy-start | bytes 676
  14.2 18.6 %copy-start = (bf16[896,128]{1,0:T(8,128)(2,1)S(1)}, bf16[896,128]{1,0:T(8,128)(2,1)}, u32[]{:S(2)}) copy-start(bf16[896,128]{1,0:T(8,128)(2,1)} %refs_1_) | copy-start | bytes 688132
  14.2 8.2 %collective-permute-start.4 = (f32[32,128]{1,0:T(8,128)S(1)}, f32[32,128]{1,0:T(8,128)S(1)}, u32[]{:S(2)}, u32[]{:S(2)}) collective-permute-start(f32[32,128]{1,0:T(8,128)S(1)} %get-tuple-element.40), channel_id=1, source_target_pairs={{0,4},{4,0},{8,12},{12,8},{16,20},{20,16},{24,28},{28,24},{1,5},{5... | collective-permute-start | bytes 49160 | tf_op jit(solution)/shard_map/ppermute | solution.py:384
  19.6 8.9 %collective-permute-start.6 = (bf16[128,512]{1,0:T(8,128)(2,1)S(1)}, bf16[128,512]{1,0:T(8,128)(2,1)S(1)}, u32[]{:S(2)}, u32[]{:S(2)}) collective-permute-start(bf16[128,512]{1,0:T(8,128)(2,1)S(1)} %shard_map.70.refs_0_), channel_id=1, source_target_pairs={{0,16},{4,20},{8,24},{12,28},{16,0},{20,4},{24,8},{28,12},{1,17},{... | collective-permute-start | bytes 393224 | tf_op jit(solution)/shard_map/ppermute | solution.py:384
  22.4 3.8 %collective-permute-start.5 = (f32[32,128]{1,0:T(8,128)S(1)}, f32[32,128]{1,0:T(8,128)S(1)}, u32[]{:S(2)}, u32[]{:S(2)}) collective-permute-start(f32[32,128]{1,0:T(8,128)S(1)} %add.13), channel_id=1, source_target_pairs={{0,8},{4,12},{8,0},{12,4},{16,24},{20,28},{24,16},{28,20},{1,9},{5... | collective-permute-start | bytes 49160 | tf_op jit(solution)/shard_map/ppermute | solution.py:384
  27.2 6.3 %collective-permute-start.7 = (bf16[152,384]{1,0:T(8,128)(2,1)S(1)}, bf16[152,384]{1,0:T(8,128)(2,1)S(1)}, u32[]{:S(2)}, u32[]{:S(2)}) collective-permute-start(bf16[152,384]{1,0:T(8,128)(2,1)S(1)} %shard_map.71.refs_1_), channel_id=1, source_target_pairs={{0,16},{4,20},{8,24},{12,28},{16,0},{20,4},{24,8},{28,12},{1,17},{... | collective-permute-start | bytes 350216 | tf_op jit(solution)/shard_map/ppermute | solution.py:384
  29.3 5.8 %collective-permute-start.13 = (bf16[128,512]{1,0:T(8,128)(2,1)S(1)}, bf16[128,512]{1,0:T(8,128)(2,1)S(1)}, u32[]{:S(2)}, u32[]{:S(2)}) collective-permute-start(bf16[128,512]{1,0:T(8,128)(2,1)S(1)} %get-tuple-element.55), channel_id=1, source_target_pairs={{0,4},{4,0},{8,12},{12,8},{16,20},{20,16},{24,28},{28,24},{1,5},{5... | collective-permute-start | bytes 393224 | tf_op jit(solution)/shard_map/ppermute | solution.py:384
  30.9 6.3 %collective-permute-start.14 = (bf16[128,512]{1,0:T(8,128)(2,1)S(1)}, bf16[128,512]{1,0:T(8,128)(2,1)S(1)}, u32[]{:S(2)}, u32[]{:S(2)}) collective-permute-start(bf16[128,512]{1,0:T(8,128)(2,1)S(1)} %get-tuple-element.56), channel_id=1, source_target_pairs={{0,8},{4,12},{8,0},{12,4},{16,24},{20,28},{24,16},{28,20},{1,9},{5... | collective-permute-start | bytes 393224 | tf_op jit(solution)/shard_map/ppermute | solution.py:384
  32.7 6.0 %collective-permute-start.15 = (bf16[128,512]{1,0:T(8,128)(2,1)S(1)}, bf16[128,512]{1,0:T(8,128)(2,1)S(1)}, u32[]{:S(2)}, u32[]{:S(2)}) collective-permute-start(bf16[128,512]{1,0:T(8,128)(2,1)S(1)} %get-tuple-element.57), channel_id=1, source_target_pairs={{0,12},{4,8},{8,4},{12,0},{16,28},{20,24},{24,20},{28,16},{1,13},{... | collective-permute-start | bytes 393224 | tf_op jit(solution)/shard_map/ppermute | solution.py:384
  32.9 8.7 %collective-permute-start.9 = (bf16[896,128]{1,0:T(8,128)(2,1)S(1)}, bf16[896,128]{1,0:T(8,128)(2,1)S(1)}, u32[]{:S(2)}, u32[]{:S(2)}) collective-permute-start(bf16[896,128]{1,0:T(8,128)(2,1)S(1)} %copy-done), channel_id=1, source_target_pairs={{0,1},{1,0},{2,3},{3,2},{4,5},{5,4},{6,7},{7,6},{8,9},{9,8},{10,11... | collective-permute-start | bytes 688136 | tf_op jit(solution)/shard_map/ppermute | solution.py:384
  33.5 8.1 %collective-permute-start.10 = (bf16[896,128]{1,0:T(8,128)(2,1)S(1)}, bf16[896,128]{1,0:T(8,128)(2,1)S(1)}, u32[]{:S(2)}, u32[]{:S(2)}) collective-permute-start(bf16[896,128]{1,0:T(8,128)(2,1)S(1)} %collective-permute-done.refs_5_.refs_3_), channel_id=1, source_target_pairs={{0,1},{1,0},{2,3},{3,2},{4,5},{5,4},{6,7},{7,6},{8,9},{9,8},{10,11... | collective-permute-start | bytes 688136 | tf_op jit(solution)/shard_map/ppermute | solution.py:384
  35.1 6.5 %collective-permute-start.11 = (bf16[136,384]{1,0:T(8,128)(2,1)S(1)}, bf16[136,384]{1,0:T(8,128)(2,1)S(1)}, u32[]{:S(2)}, u32[]{:S(2)}) collective-permute-start(bf16[136,384]{1,0:T(8,128)(2,1)S(1)} %get-tuple-element.52), channel_id=1, source_target_pairs={{0,4},{4,0},{8,12},{12,8},{16,20},{20,16},{24,28},{28,24},{1,5},{5... | collective-permute-start | bytes 313352 | tf_op jit(solution)/shard_map/ppermute | solution.py:384
  37.2 5.6 %collective-permute-start.12 = (bf16[136,384]{1,0:T(8,128)(2,1)S(1)}, bf16[136,384]{1,0:T(8,128)(2,1)S(1)}, u32[]{:S(2)}, u32[]{:S(2)}) collective-permute-start(bf16[136,384]{1,0:T(8,128)(2,1)S(1)} %get-tuple-element.53), channel_id=1, source_target_pairs={{0,8},{4,12},{8,0},{12,4},{16,24},{20,28},{24,16},{28,20},{1,9},{5... | collective-permute-start | bytes 313352 | tf_op jit(solution)/shard_map/ppermute | solution.py:384
  38.7 5.8 %collective-permute-start.8 = (bf16[136,384]{1,0:T(8,128)(2,1)S(1)}, bf16[136,384]{1,0:T(8,128)(2,1)S(1)}, u32[]{:S(2)}, u32[]{:S(2)}) collective-permute-start(bf16[136,384]{1,0:T(8,128)(2,1)S(1)} %get-tuple-element.48), channel_id=1, source_target_pairs={{0,12},{4,8},{8,4},{12,0},{16,28},{20,24},{24,20},{28,16},{1,13},{... | collective-permute-start | bytes 313352 | tf_op jit(solution)/shard_map/ppermute | solution.py:384

commit v4 on v3

v4 whole, which is shorter than its diff:
```python
import functools
import jax
import jax.numpy as jnp
from jax import lax
from jax.experimental import pallas as pl
from jax.experimental.pallas import tpu as pltpu
from jax.sharding import PartitionSpec as P

N = 128
GROUP = 128

epsilon = 1e-06
PIECES = 2

F32 = jnp.float32
BF16 = jnp.bfloat16
HIGHEST = lax.Precision.HIGHEST
LIMIT = 48 * 1024 * 1024

VMEM = pl.BlockSpec(memory_space=pltpu.VMEM)
ANY = pl.BlockSpec(memory_space=pl.ANY)
SMEM = pl.BlockSpec(memory_space=pltpu.SMEM)


def dot(a, b, contract=((1,), (0,)), precision=None):
    return lax.dot_general(a, b, (contract, ((), ())), preferred_element_type=F32, precision=precision)


def iota(shape, dim):
    return lax.broadcasted_iota(jnp.int32, shape, dim)


def split(x):
    high = x.astype(BF16)
    return high, (x - high.astype(F32)).astype(BF16)


def cumulative_by_position(log_decay):
    upto = (iota((GROUP, GROUP), 1) <= iota((GROUP, GROUP), 0)).astype(F32)
    return dot(upto, log_decay, ((1,), (1,)), HIGHEST)


def cumulative_by_head(log_decay):
    upto = (iota((GROUP, GROUP), 0) <= iota((GROUP, GROUP), 1)).astype(F32)
    return dot(log_decay, upto, precision=HIGHEST)


def spread(x, first_head, lanes, head_dim):
    heads = x.shape[1]
    member = (iota((heads, lanes), 0) == first_head + iota((heads, lanes), 1) // head_dim).astype(BF16)
    return dot(jnp.concatenate(split(x), axis=1), jnp.concatenate([member, member], axis=0))


INDEX, WHICH, OWN, HELD = range(4)


def start_all(pairs, sems):
    copies = [pltpu.make_async_copy(source, target, sems.at[i]) for i, (source, target) in enumerate(pairs)]
    for copy in copies:
        copy.start()
    return copies


def head_rows(lanes, head_dim):
    return -(-(lanes // head_dim) // 8) * 8


def tiles_of(x):
    return [x[i : i + 1, j : j + 128] for i in range(x.shape[0]) for j in range(0, x.shape[1], 128)]


def notes_rows(tiles, width):
    return -(-tiles // (width // 128) // 8) * 8


def notes(tiles, width):
    per = width // 128
    rows = notes_rows(len(tiles), width)
    tiles = tiles + [jnp.zeros((1, 128), F32)] * (rows * per - len(tiles))
    rows = [jnp.concatenate(tiles[i : i + per], axis=1) for i in range(0, len(tiles), per)]
    return jnp.concatenate(rows, axis=0).astype(BF16)


def read_notes(ref, counts):
    tiles = tiles_of(ref[pl.ds(N, ref.shape[0] - N), :].astype(F32))
    runs = []
    for count in counts:
        runs.append(tiles[:count])
        tiles = tiles[count:]
    return runs


def wide(tiles):
    return jnp.concatenate(tiles, axis=1)


def heads_of(tiles, rows):
    return jnp.concatenate(tiles + [jnp.zeros((1, 128), F32)] * (rows - len(tiles)), axis=0)


def pieces_of(x):
    return [y.astype(F32) for y in split(x)]


def piece_counts(width, head_dim):
    return [width // 128] * 2 + [width // head_dim] * 2


def state_kernel(head_dim, count, place, kq_from, values_from, log_decay_from, *refs):
    *outs, kq, values, log_decay, sems = refs
    copies = start_all([(log_decay_from, log_decay), (kq_from, kq), (values_from, values)], sems)
    pieces = [outs[i : i + count] for i in range(0, len(outs), count)]
    lanes = sum(piece[0].shape[1] for piece in pieces)
    copies[0].wait()
    ld = log_decay[...]
    heads = ld.shape[0]
    by_position = cumulative_by_position(ld)
    final = by_position[GROUP - 1 :, :]
    decay_left = jnp.exp(final - by_position)
    last = jnp.broadcast_to(jnp.exp(final), (8, heads))
    growth = split(jnp.exp(cumulative_by_head(ld)))
    copies[1].wait()
    query_sums = dot(growth[0], kq[:, N:]) + dot(growth[1], kq[:, N:])
    keys = jnp.transpose(kq[:, :N])
    rows = head_rows(lanes, head_dim)
    broads = []
    for m in range(count):
        first = (place[OWN] ^ m) * (lanes // head_dim)
        broad = spread(jnp.concatenate([decay_left, last], axis=0), first, lanes, head_dim)
        broads.append(broad[:GROUP])
        own = iota((rows, heads), 1) == first + iota((rows, heads), 0)
        mine = dot(own.astype(F32), query_sums, precision=HIGHEST)
        at = 0
        for piece in pieces:
            width = piece[m].shape[1]
            here = mine[at // head_dim : (at + width) // head_dim]
            tiles = [tile for x in pieces_of(broad[GROUP : GROUP + 1, at : at + width]) for tile in tiles_of(x)]
            tiles += [tile for x in pieces_of(here) for tile in tiles_of(x)]
            below = notes(tiles, width)
            piece[m][pl.ds(N, below.shape[0]), :] = below
            at += width
    copies[2].wait()
    for m in range(count):
        at = 0
        for piece in pieces:
            width = piece[m].shape[1]
            start = pl.multiple_of((place[OWN] ^ m) * lanes + at, 128)
            weighted = (values[:, pl.ds(start, width)].astype(F32) * broads[m][:, at : at + width]).astype(BF16)
            piece[m][pl.ds(0, N), :] = dot(keys, weighted).astype(BF16)
            at += width


def piece_notes(piece, head_dim):
    width = piece.shape[1]
    high, low, query_high, query_low = read_notes(piece, piece_counts(width, head_dim))
    rows = head_rows(width, head_dim)
    queries = jnp.concatenate([heads_of(query_high, rows), heads_of(query_low, rows)], axis=0)
    return wide(high) + wide(low), queries


def block_kernel(head_dim, kq_from, values_from, log_decay_from, skip, out, wide_growth, sums, kept, *scratch):
    kq, values, log_decay, sems = scratch
    copies = start_all([(kq_from, kq), (values_from, values), (log_decay_from, log_decay)], sems)
    for copy in copies:
        copy.wait()
    ld = log_decay[...]
    by_position = cumulative_by_position(ld)
    by_head = cumulative_by_head(ld)
    queries = kq[:, N:]
    kept[...] = queries
    scores = dot(queries, kq[:, :N], ((1,), (1,)))
    causal = iota((GROUP, GROUP), 0) >= iota((GROUP, GROUP), 1)
    per = 128 // head_dim
    lane = iota((GROUP, 128), 1) // head_dim
    lane_row = iota((1, 128), 1) // head_dim
    tiles = values.shape[1] // 128
    part_tiles = tiles // (sums.shape[0] // 8)
    sums[...] = jnp.zeros_like(sums)
    for i in range(tiles):
        at = slice(i * 128, (i + 1) * 128)
        value = values[:, at]
        mixes, tops = [], []
        direct = jnp.zeros((1, 128), F32)
        growth = None
        for j in range(per):
            h = i * per + j
            here = jnp.broadcast_to(by_position[:, h : h + 1], (GROUP, 128))
            gap = here - by_head[h : h + 1, :]
            mixes.append((scores * jnp.exp(jnp.where(causal, gap, -jnp.inf))).astype(BF16))
            tops.append(jnp.where(lane == j, value, jnp.zeros_like(value)))
            direct = jnp.where(lane_row == j, skip[h], direct)
            growth = here if growth is None else jnp.where(lane == j, here, growth)
        mixed = dot(jnp.concatenate(mixes, axis=1), jnp.concatenate(tops, axis=0))
        mixed = mixed + direct * value.astype(F32)
        out[:, at] = mixed
        wide_growth[:, at] = jnp.exp(growth)
        line = i // part_tiles * 8 + i % part_tiles
        sums[line : line + 1, :] = jnp.sum(mixed, axis=0, keepdims=True)


def total_kernel(head_dim, place, *refs):
    *pieces, total, ordered, factors = refs
    for m, piece in enumerate(pieces):
        ordered[place[INDEX] ^ m] = piece[pl.ds(0, N), :]
        factors[place[INDEX] ^ m] = piece_notes(piece, head_dim)[0]
    running = ordered[0].astype(F32)
    for j in range(1, len(pieces)):
        running = factors[j] * running + ordered[j].astype(F32)
    total[...] = running.astype(BF16)


def totals_kernel(head_dim, count, pair, place, sums, *refs):
    scratch = refs[-3 * PIECES :]
    parts, outs = refs[: PIECES * count], refs[PIECES * count : -3 * PIECES]
    lanes = 0
    carried, weights, totals, decays = [], [], [], []
    for k in range(PIECES):
        ordered, factors, queries = scratch[3 * k : 3 * k + 3]
        for m, piece in enumerate(parts[k * count : (k + 1) * count]):
            ordered[place[INDEX] ^ m] = piece[pl.ds(0, N), :]
            factors[place[INDEX] ^ m], queries[place[INDEX] ^ m] = piece_notes(piece, head_dim)
        width = ordered.shape[2]
        lanes += width
        rows = head_rows(width, head_dim)
        running = ordered[0].astype(F32)
        factor = factors[0]
        if pair:
            own = (iota((rows, width), 0) == iota((rows, width), 1) // head_dim).astype(F32) / head_dim
            weight = queries[0, pl.ds(0, rows), :] + queries[0, pl.ds(rows, rows), :]
            added = jnp.zeros((rows, width), F32)
        for j in range(1, count):
            if pair:
                by_head = jnp.sum(own * factor, axis=1, keepdims=True)
                weight = weight + by_head * (queries[j, pl.ds(0, rows), :] + queries[j, pl.ds(rows, rows), :])
                added = added + heads_dot(queries[j].astype(BF16), running.astype(BF16))
            factor = factor * factors[j]
            running = factors[j] * running + ordered[j].astype(F32)
        totals.append(running.astype(BF16))
        decays.append(factor)
        if pair:
            carried.append(own_heads(added, head_dim))
            weights += [tile for x in pieces_of(weight[: width // head_dim]) for tile in tiles_of(x)]
    if not pair:
        for out, x in zip(outs, [*totals, wide(decays)]):
            out[...] = x
        return
    tiles = [tile for x in thirds(wide(carried)) for tile in tiles_of(x.astype(F32))] + weights
    for x in pieces_of(sums[...]):
        tiles += sums_tiles(x, lanes)
    below = notes(tiles, outs[0].shape[1])
    outs[0][pl.ds(0, N), :] = totals[-1]
    outs[0][pl.ds(N, below.shape[0]), :] = below


def sums_tiles(sums, lanes):
    return [sums[i : i + 1] for i in range(sums.shape[0]) if i % 8 < lanes // 128]


def starts_kernel(head_dim, count, lanes, place, *refs):
    refs, pieces, outs, scratch = refs[: -3 - 2 * count], refs[-3 - 2 * count : -3 - count], refs[-3 - count : -3], refs[-3:]
    ordered, factors, results = scratch
    width = outs[0].shape[1]
    for m, piece in enumerate(pieces):
        ordered[place[INDEX] ^ m] = piece[pl.ds(0, N), :]
        factors[place[INDEX] ^ m] = piece_notes(piece, head_dim)[0]
    running = jnp.where(place[WHICH] == 0, 0.0, refs[-1][pl.ds(0, N), :].astype(F32))
    for j in range(count):
        results[j] = running.astype(BF16)
        if j < count - 1:
            running = factors[j] * running + ordered[j].astype(F32)
    if len(refs) > 1:
        sums, fellows = sums_of(place, head_dim, lanes, count, refs[: len(refs) // 2], refs[len(refs) // 2 :])
        below = notes(sums_notes(sums, fellows), width)
    for m, out in enumerate(outs):
        out[pl.ds(0, N), :] = results[place[INDEX] ^ m]
        if len(refs) > 1:
            out[pl.ds(N, below.shape[0]), :] = below


def sums_notes(sums, fellows):
    tiles = [tile for x in thirds(sums) for tile in tiles_of(x.astype(F32))]
    return tiles + [tile for x in pieces_of(fellows) for tile in tiles_of(x)]


def sums_of(place, head_dim, lanes, count, totals, before):
    first = place[WHICH] == 0
    counts = [lanes // 128] * 3
    for total in totals:
        counts += [total.shape[1] // head_dim] * 2
    counts += [count * lanes // 128] * 2
    mine, other = read_notes(totals[-1], counts), read_notes(before[-1], counts)
    products = []
    for k, (total, got) in enumerate(zip(totals, before)):
        rows = head_rows(total.shape[1], head_dim)
        weight = [
            jnp.where(first, heads_of(there, rows), heads_of(here, rows))
            for here, there in zip(mine[3 + 2 * k : 5 + 2 * k], other[3 + 2 * k : 5 + 2 * k])
        ]
        state = jnp.where(first, total[pl.ds(0, N), :].astype(F32), got[pl.ds(0, N), :].astype(F32)).astype(BF16)
        products.append(own_heads(heads_dot(jnp.concatenate(weight, axis=0).astype(BF16), state), head_dim))
    fellows = sum(wide(here) + wide(there) for here, there in zip(mine[-2:], other[-2:]))
    return wide(products) + sum(wide(here) + wide(there) for here, there in zip(mine[:3], other[:3])), fellows


def thirds(x):
    high = x.astype(BF16)
    return high, *split(x - high.astype(F32))


def heads_dot(queries, state):
    both = dot(queries, state)
    rows = queries.shape[0] // 2
    return both[:rows] + both[rows:]


def own_heads(x, head_dim):
    mine = iota(x.shape, 0) == iota(x.shape, 1) // head_dim
    return jnp.sum(jnp.where(mine, x, 0.0), axis=0, keepdims=True)


def sums_kernel(head_dim, count, *refs):
    *refs, out = refs
    pieces, states = refs[: PIECES * count], refs[PIECES * count :]
    carried = []
    for k in range(PIECES):
        added = 0.0
        for piece, state in zip(pieces[k * count : (k + 1) * count], states[k * count : (k + 1) * count]):
            added = added + heads_dot(piece_notes(piece, head_dim)[1].astype(BF16), state[pl.ds(0, N), :])
        carried.append(own_heads(added, head_dim))
    out[...] = wide(carried)


def output_kernel(ms, count, lanes, offset, step, positions, place, queries, local, wide_growth, *refs):
    carried, refs = refs[: len(ms)], refs[len(ms) :]
    *refs, made, sems = refs
    copies = []
    at = [pl.multiple_of((place[OWN] ^ m) * lanes + offset, 128) for m in ms]
    width = carried[0].shape[1]
    mixed = refs[{0: -1, 1: -3, 2: -4}[step]]
    for i, state in enumerate(carried):
        here = pl.ds(at[i], width)
        made[i] = (local[:, here] + wide_growth[:, here] * dot(queries[...], state[pl.ds(0, N), :])).astype(BF16)
        copies.append(pltpu.make_async_copy(made.at[i], mixed.at[:, here], sems.at[i]))
        copies[-1].start()
    if step == 1:
        weights, (pooled, rows) = refs[:count], refs[-2:]
        for k, x in enumerate(weights):
            rows[place[HELD] ^ place[OWN] ^ k] = x[...]
        pooled[...] = jnp.zeros_like(pooled)
    if step == 2:
        before, rows, logits, pooled, scaled = refs[0], refs[1], refs[-3], refs[-2], refs[-1]
        pooled[...] = before[...]
    if step:
        for m, state in zip(ms, carried):
            *own, high, low = read_notes(state, [lanes // 128] * 3 + [count * lanes // 128] * 2)
            pooled[m] += jnp.broadcast_to(sum(wide(x) for x in own), (8, lanes))
            for k in range(count):
                part = slice(k * (lanes // 128), (k + 1) * (lanes // 128))
                pooled[place[OWN] ^ k] += jnp.broadcast_to(wide(high[part]) + wide(low[part]), (8, lanes))
    if step == 2:
        product = square = 0.0
        for m in range(count):
            mean = pooled[m] / positions
            high, low = split(mean)
            product = product + dot(high, rows[m]) + dot(low, rows[m])
            square = square + jnp.sum(mean * mean, axis=1, keepdims=True)
        scaled[...] = product / jnp.sqrt(square / (lanes * count) + epsilon)
        copies.append(pltpu.make_async_copy(scaled.at[pl.ds(0, 1)], logits, sems.at[len(ms)]))
        copies[-1].start()
    for copy in copies:
        copy.wait()


def call(kernel, outs, in_specs, scratch=(), flops=0, moved=0, out_specs=None, aliases=None):
    return pl.pallas_call(
        kernel,
        out_shape=outs,
        in_specs=in_specs,
        out_specs=out_specs or jax.tree.map(lambda _: VMEM, outs),
        scratch_shapes=scratch,
        input_output_aliases=aliases or {},
        cost_estimate=pl.CostEstimate(flops=flops, bytes_accessed=moved, transcendentals=0),
        compiler_params=pltpu.CompilerParams(vmem_limit_bytes=LIMIT),
    )


def local(inputs, keys_queries, log_decay, skip, classifier):
    _, positions, channels = inputs.shape
    heads = log_decay.shape[1]
    head_dim = channels // heads
    size, group = lax.axis_size("seq"), lax.axis_size("fsdp")
    pair = size == 2 * group
    lanes = channels // group
    classes = classifier.shape[1]
    index, column = lax.axis_index("seq"), lax.axis_index("fsdp")
    place = jnp.stack([index % group, index // group, (index % group) ^ column, column]).astype(jnp.int32)
    values, kq, ld = inputs[0], keys_queries[0], log_decay[0]
    sources = [pltpu.with_memory_space_constraint(x, pltpu.HBM) for x in (kq, values, ld)]
    landing = [pltpu.VMEM(x.shape, x.dtype) for x in (kq, values, ld)] + [pltpu.SemaphoreType.DMA((3,))]
    tiles = lanes // 128
    widths = [(tiles + 1) // 2 * 128, tiles // 2 * 128] if PIECES == 2 else [lanes]
    offsets = [0, widths[0]][:PIECES]

    def piece(width, count):
        return jax.ShapeDtypeStruct((N + (notes_rows(count, width) if count else 0), width), BF16)

    row = jax.ShapeDtypeStruct((1, lanes), F32)
    full = jax.ShapeDtypeStruct((positions, channels), F32)
    share = jax.ShapeDtypeStruct((8, classes), F32)
    gathered = [
        jax.ShapeDtypeStruct((group, 8, lanes), F32),
        jax.ShapeDtypeStruct((group, lanes, classes), BF16),
    ]
    def swap(x, m, axis="seq"):
        return lax.ppermute(x, axis, [(i, i ^ m) for i in range(lax.axis_size(axis))])

    def swap_all(xs, axis="seq"):
        return [xs[0]] + [swap(xs[m], m, axis) for m in range(1, group)]

    def shift(x, by):
        return lax.ppermute(x, "seq", [(i, i + by) for i in range(size - by)])

    parts = call(
        functools.partial(state_kernel, head_dim, group),
        [piece(width, sum(piece_counts(width, head_dim))) for width in widths for _ in range(group)],
        [SMEM] + [ANY] * 3,
        landing,
        flops=2 * positions * N * channels,
        moved=4 * positions * channels,
    )(place, *sources)
    parts = [swap_all(parts[i : i + group]) for i in range(0, len(parts), group)]
    classifier, parts[0][1] = lax.optimization_barrier((classifier, parts[0][1]))
    totals = []
    if pair and PIECES == 2:
        totals.append(
            call(
                functools.partial(total_kernel, head_dim),
                piece(widths[0], 0),
                [SMEM] + [VMEM] * group,
                [pltpu.VMEM((group, N, widths[0]), BF16), pltpu.VMEM((group, 1, widths[0]), F32)],
            )(place, *parts[0])
        )
        skip = lax.optimization_barrier((skip, totals))[0]
    made = call(
        functools.partial(block_kernel, head_dim),
        [full, full, jax.ShapeDtypeStruct((8 * group, 128), F32), jax.ShapeDtypeStruct((positions, N), BF16)],
        [ANY] * 3 + [SMEM],
        landing,
        flops=8 * positions * N * channels,
        moved=6 * positions * channels,
    )(*sources, skip)
    from_block, wide_growth, sums, queries = made
    scratch = []
    for width in widths:
        scratch += [
            pltpu.VMEM((group, N, width), BF16),
            pltpu.VMEM((group, 1, width), F32),
            pltpu.VMEM((group, 2 * head_rows(width, head_dim), N), F32),
        ]
    totals += call(
        functools.partial(totals_kernel, head_dim, group, pair),
        [piece(widths[-1], 3 * tiles + 2 * (lanes // head_dim) + 2 * group * tiles)] if pair else [piece(w, 0) for w in widths] + [row],
        [SMEM] + [VMEM] * (1 + PIECES * group),
        scratch,
    )(place, sums, *[x for part in parts for x in part])
    crossed = swap(classifier, 2, "fsdp")
    if pair:
        before = [swap(total, group) for total in totals]
        across = [*totals, *before]
    else:
        *totals, decay = totals
        before = []
        for total, at, width in zip(totals, offsets, widths):
            running, factor = shift(total, group).astype(F32), shift(decay[:, at : at + width], group)
            reach = 1
            while reach < size // group - 1:
                running = running + factor * shift(running, group * reach)
                factor = factor * shift(factor, group * reach)
                reach *= 2
            before.append(running.astype(BF16))
    weights = [classifier, swap(classifier, 1, "fsdp"), crossed, swap(crossed, 1, "fsdp")]

    starts = []
    for k, width in enumerate(widths):
        last = k == PIECES - 1
        operands = across if last and pair else [before[k]]
        starts.append(
            call(
                functools.partial(starts_kernel, head_dim, group, lanes),
                [piece(width, 3 * tiles + 2 * group * tiles if last and pair else 0)] * group,
                [SMEM] + [VMEM] * (len(operands) + group),
                [
                    pltpu.VMEM((group, N, width), BF16),
                    pltpu.VMEM((group, 1, width), F32),
                    pltpu.VMEM((group, N, width), BF16),
                ],
            )(place, *operands, *parts[k])
        )
    if not pair:
        whole = call(
            functools.partial(sums_kernel, head_dim, group), row, [VMEM] * (2 * PIECES * group)
        )(*[x for part in parts for x in part], *[x for part in starts for x in part])
        reach = group
        while reach < size:
            whole = whole + swap(whole, reach)
            reach *= 2
        reach = 1
        while reach < size:
            sums = sums + swap(sums, reach)
            reach *= 2
        below = notes(sums_notes(whole, wide(sums_tiles(sums / group, lanes))), widths[-1])
        starts[-1] = [jnp.concatenate([x, below], axis=0) for x in starts[-1]]
    starts = [swap_all(x) for x in starts]

    plan = [(tuple(range(group)), k, 0) for k in range(PIECES - 1)]
    plan += [(tuple(range(group - 1)), PIECES - 1, 1), ((group - 1,), PIECES - 1, 2)]
    mixed, rest = None, []
    for i, (ms, k, step) in enumerate(plan):
        operands = [queries, from_block, wide_growth, *[starts[k][m] for m in ms]]
        operands += {0: [], 1: weights, 2: rest}[step]
        outs = [pltpu.HBM((positions, channels), BF16)]
        outs += {0: [], 1: gathered, 2: [pltpu.HBM((1, classes), F32)]}[step]
        scratch = [pltpu.VMEM(gathered[0].shape, F32), pltpu.VMEM(share.shape, F32)] if step == 2 else []
        mixed, *rest = call(
            functools.partial(output_kernel, ms, group, lanes, offsets[k], step, positions * size),
            outs,
            [SMEM] + [VMEM] * len(operands) + [ANY] * (i > 0),
            scratch
            + [
                pltpu.VMEM((len(ms), positions, widths[k]), BF16),
                pltpu.SemaphoreType.DMA((len(ms) + 1,)),
            ],
            out_specs=[ANY] + {0: [], 1: [VMEM] * 2, 2: [ANY]}[step],
            aliases={1 + len(operands): 0} if i else None,
        )(place, *operands, *([mixed] if i else []))
    (logits,) = rest
    return mixed[None], logits


def solution(mesh):
    return jax.shard_map(
        local,
        mesh=mesh,
        in_specs=(
            P("fsdp", "seq", None),
            P("fsdp", "seq", None),
            P("fsdp", None, "seq"),
            P(),
            P("fsdp", None),
        ),
        out_specs=(P("fsdp", "seq", None), P("fsdp", None)),
        check_vma=False,
    )
```

time: 46 us -> 43.5 us (0.946)
  waiting for transfers between devices: 7.88 us -> 2.46 us
  starting transfers between devices: 22.2 us -> 25.1 us
    ppermute x16 -> x17, waiting for transfers between devices: 7.88 us -> 2.46 us  [swap(): lax.ppermute(x, axis, [(i, i ^ m) for i in range(lax.axis_size(axis))])]
    ppermute x16 -> x17, starting transfers between devices: 22.2 us -> 25.1 us  [swap(): lax.ppermute(x, axis, [(i, i ^ m) for i in range(lax.axis_size(axis))])]
  transfers between devices with their start and end apart: 16 -> 17, of which waited for: 6 -> 4; matrix products, arithmetic and copies ran while one was open for 0% -> 0% of each run, Pallas kernels for 22% -> 23%
where the time goes in v4:
time: 43.5 us; the launch traced here: 43.3 us
  starting transfers between devices  25.1 us (58%)
  Pallas kernels  14.2 us (33%)
  waiting for transfers between devices  2.46 us (6%)
  between operations  0.78 us (2%)
  local copies, waits for them, and re-layouts  0.66 us (2%)
    ppermute x17, starting transfers between devices, swap(): lax.ppermute(x, axis, [(i, i ^ m) for i in range(lax.axis_size(axis))])  25.1 us
    pallas_call x3, Pallas kernels, local(): call(functools.partial(output_kernel, ms, group, lanes, offsets[k], step,...  4.6 us
    pallas_call x1, Pallas kernels, local(): call(functools.partial(block_kernel, head_dim), [full, full, jax.ShapeDty...  3.68 us
    pallas_call x1, Pallas kernels, local(): call(functools.partial(state_kernel, head_dim, group), [piece(width, sum(...  2.65 us
    ppermute x17, waiting for transfers between devices, swap(): lax.ppermute(x, axis, [(i, i ^ m) for i in range(lax.axis_size(axis))])  2.46 us
    pallas_call x2, Pallas kernels, local(): call(functools.partial(starts_kernel, head_dim, group, lanes), [piece(wid...  1.64 us
    pallas_call x1, Pallas kernels, local(): call(functools.partial(totals_kernel, head_dim, group, pair), [piece(widt...  0.93 us
  transfers between devices with their start and end apart: 17, of which 4 were waited for; matrix products, arithmetic and copies ran while one was open for 0% of the time, Pallas kernels for 23%

profile of v4, /device:TPU:0, one launch (start us, length us, event | category | flops | bytes accessed | tf_op | source)
XLA Modules:
  0.0 43.3 jit_solution(1708170509394222984)
XLA Ops:
  0.7 0.1 pad_add_fusion.place
  0.7 2.6 %shard_map.68 = (bf16[136,512]{1,0:T(8,128)(2,1)S(1)}, bf16[136,512]{1,0:T(8,128)(2,1)S(1)}, bf16[136,512]{1,0:T(8,128)(2,1)S(1)}, bf16[136,512]{1,0:T(8,128)(2,...) custom-call(s32[4]{0:T(128)S(1)} %pad_add_fusion.place, ...), custom_call_target="tpu_custom_call" | custom-call | flops 117440512 | bytes 1835008 | tf_op jit(solution)/shard_map/pallas_call | solution.py:423
  3.4 3.0 %collective-permute-start = (bf16[136,512]{1,0:T(8,128)(2,1)S(1)}, bf16[136,512]{1,0:T(8,128)(2,1)S(1)}, u32[]{:S(2)}, u32[]{:S(2)}) collective-permute-start(bf16[136,512]{1,0:T(8,128)(2,1)S(1)} %get-tuple-element.31), channel_id=1, source_target_pairs={{0,4},{4,0},{8,12},{12,8},{16,20},{20,16},{24,28},{28,24},{1,5},{5... | collective-permute-start | bytes 417800 | tf_op jit(solution)/shard_map/ppermute | solution.py:415
  6.4 1.6 %collective-permute-start.1 = (bf16[136,512]{1,0:T(8,128)(2,1)S(1)}, bf16[136,512]{1,0:T(8,128)(2,1)S(1)}, u32[]{:S(2)}, u32[]{:S(2)}) collective-permute-start(bf16[136,512]{1,0:T(8,128)(2,1)S(1)} %get-tuple-element.33), channel_id=1, source_target_pairs={{0,8},{4,12},{8,0},{12,4},{16,24},{20,28},{24,16},{28,20},{1,9},{5... | collective-permute-start | bytes 417800 | tf_op jit(solution)/shard_map/ppermute | solution.py:415
  8.0 0.0 collective-permute-start.2
  8.0 1.9 %collective-permute-start.3 = (bf16[136,384]{1,0:T(8,128)(2,1)S(1)}, bf16[136,384]{1,0:T(8,128)(2,1)S(1)}, u32[]{:S(2)}, u32[]{:S(2)}) collective-permute-start(bf16[136,384]{1,0:T(8,128)(2,1)S(1)} %get-tuple-element.41), channel_id=1, source_target_pairs={{0,4},{4,0},{8,12},{12,8},{16,20},{20,16},{24,28},{28,24},{1,5},{5... | collective-permute-start | bytes 313352 | tf_op jit(solution)/shard_map/ppermute | solution.py:415
  9.9 1.6 %collective-permute-start.4 = (bf16[136,384]{1,0:T(8,128)(2,1)S(1)}, bf16[136,384]{1,0:T(8,128)(2,1)S(1)}, u32[]{:S(2)}, u32[]{:S(2)}) collective-permute-start(bf16[136,384]{1,0:T(8,128)(2,1)S(1)} %get-tuple-element.42), channel_id=1, source_target_pairs={{0,8},{4,12},{8,0},{12,4},{16,24},{20,28},{24,16},{28,20},{1,9},{5... | collective-permute-start | bytes 313352 | tf_op jit(solution)/shard_map/ppermute | solution.py:415
  11.5 0.0 collective-permute-done.refs_1_.refs_2_
  11.5 2.2 %collective-permute-start.5 = (bf16[136,384]{1,0:T(8,128)(2,1)S(1)}, bf16[136,384]{1,0:T(8,128)(2,1)S(1)}, u32[]{:S(2)}, u32[]{:S(2)}) collective-permute-start(bf16[136,384]{1,0:T(8,128)(2,1)S(1)} %get-tuple-element.43), channel_id=1, source_target_pairs={{0,12},{4,8},{8,4},{12,0},{16,28},{20,24},{24,20},{28,16},{1,13},{... | collective-permute-start | bytes 313352 | tf_op jit(solution)/shard_map/ppermute | solution.py:415
  13.7 0.0 collective-permute-done.1.refs_2_.refs_3_
  13.7 1.5 %collective-permute-start.12 = (bf16[896,128]{1,0:T(8,128)(2,1)}, bf16[896,128]{1,0:T(8,128)(2,1)S(1)}, u32[]{:S(2)}, u32[]{:S(2)}) collective-permute-start(bf16[896,128]{1,0:T(8,128)(2,1)} %refs_3_), channel_id=1, source_target_pairs={{0,2},{1,3},{2,0},{3,1},{4,6},{5,7},{6,4},{7,5},{8,10},{9,11},{10,... | collective-permute-start | bytes 688136 | tf_op jit(solution)/shard_map/ppermute | solution.py:415
  15.2 0.4 collective-permute-done.2.refs_3_.refs_4_
  15.6 0.7 %shard_map.69.refs_0_ = bf16[128,512]{1,0:T(8,128)(2,1)S(1)} custom-call(s32[4]{0:T(128)S(1)} %pad_add_fusion.place, bf16[136,512]{1,0:T(8,128)(2,1)S(1)} %get-tuple-element.30.refs_0_.refs_1_, bf16[136,512]{1,0:T(8,128)(2,1)S(1)} %collective-permute-done.refs_1_.refs_2_, bf16[136,512]{1,0:T(8,128)(2,1)S(1)} %collective-permute-done.1.refs_2_.refs_3_, ...), custom_call_target="tpu_custom_call" | custom-call | tf_op jit(solution)/shard_map/pallas_call | solution.py:436
  16.3 0.0 copy-start
  16.3 2.6 %collective-permute-start.6 = (bf16[128,512]{1,0:T(8,128)(2,1)S(1)}, bf16[128,512]{1,0:T(8,128)(2,1)S(1)}, u32[]{:S(2)}, u32[]{:S(2)}) collective-permute-start(bf16[128,512]{1,0:T(8,128)(2,1)S(1)} %shard_map.69.refs_0_), channel_id=1, source_target_pairs={{0,16},{4,20},{8,24},{12,28},{16,0},{20,4},{24,8},{28,12},{1,17},{... | collective-permute-start | bytes 393224 | tf_op jit(solution)/shard_map/ppermute | solution.py:415
  18.9 0.0 copy-start.1
  18.9 0.7 %copy-done.1 = f32[56]{0:T(128)S(1)} copy-done((f32[56]{0:T(128)S(1)}, f32[56]{0:T(128)}, u32[]{:S(2)}) %copy-start.1) | copy-done | bytes 248
  19.6 3.7 %shard_map.70 = (f32[128,3584]{1,0:T(8,128)S(1)}, f32[128,3584]{1,0:T(8,128)S(1)}, f32[32,128]{1,0:T(8,128)S(1)}, bf16[128,128]{1,0:T(8,128)(2,1)S(1)}) custom-call(bf16[128,256]{1,0:T(8,128)(2,1)} %bitcast.12, bf16[128,3584]{1,0:T(8,128)(2,1)} %bitcast.10, f32[56,128]{1,0:T(8,128)} %bitcast.14, f32[56]{0:T(128)S(1)} %copy-done.1), custom_call_target="tpu_custom_call" | custom-call | flops 469762048 | bytes 2752512 | tf_op jit(solution)/shard_map/pallas_call | solution.py:444
  23.2 0.0 collective-permute-done.3.refs_5_
  23.2 0.0 collective-permute-done.4.refs_6_
  23.3 0.0 collective-permute-done.5.refs_7_
  23.3 0.9 %shard_map.71.refs_1_ = bf16[168,384]{1,0:T(8,128)(2,1)S(1)} custom-call(s32[4]{0:T(128)S(1)} %pad_add_fusion.place, f32[32,128]{1,0:T(8,128)S(1)} %get-tuple-element.39.sums, bf16[136,512]{1,0:T(8,128)(2,1)S(1)} %get-tuple-element.30.refs_0_.refs_1_, bf16[136,512]{1,0:T(8,128)(2,1)S(1)} %collective-permute-done.refs_1_.refs_2_, ...), custom_call_target="tpu_custom_call" | custom-call | tf_op jit(solution)/shard_map/pallas_call | solution.py:460
  24.2 0.4 %collective-permute-start.7 = (bf16[168,384]{1,0:T(8,128)(2,1)S(1)}, bf16[168,384]{1,0:T(8,128)(2,1)S(1)}, u32[]{:S(2)}, u32[]{:S(2)}) collective-permute-start(bf16[168,384]{1,0:T(8,128)(2,1)S(1)} %shard_map.71.refs_1_), channel_id=1, source_target_pairs={{0,16},{4,20},{8,24},{12,28},{16,0},{20,4},{24,8},{28,12},{1,17},{... | collective-permute-start | bytes 387080 | tf_op jit(solution)/shard_map/ppermute | solution.py:415
  24.7 0.0 collective-permute-done.6.refs_2_.refs_0_
  24.7 0.8 %shard_map.73 = (bf16[128,512]{1,0:T(8,128)(2,1)S(1)}, bf16[128,512]{1,0:T(8,128)(2,1)S(1)}, bf16[128,512]{1,0:T(8,128)(2,1)S(1)}, bf16[128,512]{1,0:T(8,128)(2,1)S(1)}) custom-call(s32[4]{0:T(128)S(1)} %pad_add_fusion.place, bf16[128,512]{1,0:T(8,128)(2,1)S(1)} %collective-permute-done.6.refs_2_.refs_0_, ...), custom_call_target="tpu_custom_call" | custom-call | tf_op jit(solution)/shard_map/pallas_call | solution.py:488
  25.4 2.0 %collective-permute-start.14 = (bf16[128,512]{1,0:T(8,128)(2,1)S(1)}, bf16[128,512]{1,0:T(8,128)(2,1)S(1)}, u32[]{:S(2)}, u32[]{:S(2)}) collective-permute-start(bf16[128,512]{1,0:T(8,128)(2,1)S(1)} %get-tuple-element.50), channel_id=1, source_target_pairs={{0,4},{4,0},{8,12},{12,8},{16,20},{20,16},{24,28},{28,24},{1,5},{5... | collective-permute-start | bytes 393224 | tf_op jit(solution)/shard_map/ppermute | solution.py:415
  27.4 2.3 %collective-permute-start.15 = (bf16[128,512]{1,0:T(8,128)(2,1)S(1)}, bf16[128,512]{1,0:T(8,128)(2,1)S(1)}, u32[]{:S(2)}, u32[]{:S(2)}) collective-permute-start(bf16[128,512]{1,0:T(8,128)(2,1)S(1)} %get-tuple-element.51), channel_id=1, source_target_pairs={{0,8},{4,12},{8,0},{12,4},{16,24},{20,28},{24,16},{28,20},{1,9},{5... | collective-permute-start | bytes 393224 | tf_op jit(solution)/shard_map/ppermute | solution.py:415
  29.8 0.0 collective-permute-start.16
  29.8 0.4 collective-permute-done.7.refs_3_
  30.1 0.0 copy-done
  30.1 0.0 collective-permute-start.11
  30.1 0.0 collective-permute-done.12.refs_5_
  30.1 0.5 %collective-permute-start.13 = (bf16[896,128]{1,0:T(8,128)(2,1)S(1)}, bf16[896,128]{1,0:T(8,128)(2,1)S(1)}, u32[]{:S(2)}, u32[]{:S(2)}) collective-permute-start(bf16[896,128]{1,0:T(8,128)(2,1)S(1)} %collective-permute-done.12.refs_5_), channel_id=1, source_target_pairs={{0,1},{1,0},{2,3},{3,2},{4,5},{5,4},{6,7},{7,6},{8,9},{9,8},{10,11... | collective-permute-start | bytes 688136 | tf_op jit(solution)/shard_map/ppermute | solution.py:415
  30.6 0.9 %shard_map.72 = (bf16[160,384]{1,0:T(8,128)(2,1)S(1)}, bf16[160,384]{1,0:T(8,128)(2,1)S(1)}, bf16[160,384]{1,0:T(8,128)(2,1)S(1)}, bf16[160,384]{1,0:T(8,128)(2,1)S(1)}) custom-call(s32[4]{0:T(128)S(1)} %pad_add_fusion.place, bf16[128,512]{1,0:T(8,128)(2,1)S(1)} %shard_map.69.refs_0_, bf16[168,384]{1,0:T(8,128)(2,1)S(1)} %shard_map.71.refs_1_, ...), custom_call_target="tpu_custom_call" | custom-call | tf_op jit(solution)/shard_map/pallas_call | solution.py:488
  31.5 0.0 collective-permute-done.14.refs_1_
  31.5 2.5 %collective-permute-start.9 = (bf16[160,384]{1,0:T(8,128)(2,1)S(1)}, bf16[160,384]{1,0:T(8,128)(2,1)S(1)}, u32[]{:S(2)}, u32[]{:S(2)}) collective-permute-start(bf16[160,384]{1,0:T(8,128)(2,1)S(1)} %get-tuple-element.46), channel_id=1, source_target_pairs={{0,4},{4,0},{8,12},{12,8},{16,20},{20,16},{24,28},{28,24},{1,5},{5... | collective-permute-start | bytes 368648 | tf_op jit(solution)/shard_map/ppermute | solution.py:415
  34.0 0.0 collective-permute-done.15.refs_2_
  34.0 2.0 %collective-permute-start.10 = (bf16[160,384]{1,0:T(8,128)(2,1)S(1)}, bf16[160,384]{1,0:T(8,128)(2,1)S(1)}, u32[]{:S(2)}, u32[]{:S(2)}) collective-permute-start(bf16[160,384]{1,0:T(8,128)(2,1)S(1)} %get-tuple-element.47), channel_id=1, source_target_pairs={{0,8},{4,12},{8,0},{12,4},{16,24},{20,28},{24,16},{28,20},{1,9},{5... | collective-permute-start | bytes 368648 | tf_op jit(solution)/shard_map/ppermute | solution.py:415
  36.0 0.0 collective-permute-done.16.refs_3_
  36.0 1.1 %collective-permute-start.8 = (bf16[160,384]{1,0:T(8,128)(2,1)S(1)}, bf16[160,384]{1,0:T(8,128)(2,1)S(1)}, u32[]{:S(2)}, u32[]{:S(2)}) collective-permute-start(bf16[160,384]{1,0:T(8,128)(2,1)S(1)} %get-tuple-element.44), channel_id=1, source_target_pairs={{0,12},{4,8},{8,4},{12,0},{16,28},{20,24},{24,20},{28,16},{1,13},{... | collective-permute-start | bytes 368648 | tf_op jit(solution)/shard_map/ppermute | solution.py:415
  37.0 1.5 %shard_map.74.refs_7_ = bf16[128,3584]{1,0:T(8,128)(2,1)} custom-call(s32[4]{0:T(128)S(1)} %pad_add_fusion.place, bf16[128,128]{1,0:T(8,128)(2,1)S(1)} %get-tuple-element.36.queries, f32[128,3584]{1,0:T(8,128)S(1)} %get-tuple-element.37.local, f32[128,3584]{1,0:T(8,128)S(1)} %get-tuple-element.38.wide_growth, ...), custom_call_target="tpu_custom_call" | custom-call | tf_op jit(solution)/shard_map/pallas_call | solution.py:524
  38.6 0.0 collective-permute-done.11.refs_4_
  38.6 0.0 collective-permute-done.9.refs_1_
  38.6 1.6 %collective-permute-done.10.refs_2_ = bf16[160,384]{1,0:T(8,128)(2,1)S(1)} collective-permute-done((bf16[160,384]{1,0:T(8,128)(2,1)S(1)}, bf16[160,384]{1,0:T(8,128)(2,1)S(1)}, u32[]{:S(2)}, u32[]{:S(2)}) %collective-permute-start.10) | collective-permute-done | bytes 122912 | tf_op jit(solution)/shard_map/ppermute | solution.py:415
  40.2 0.0 collective-permute-done.13.refs_6_
  40.2 1.5 %shard_map.75 = (bf16[128,3584]{1,0:T(8,128)(2,1)}, f32[4,8,896]{2,1,0:T(8,128)S(1)}, bf16[4,896,128]{2,1,0:T(8,128)(2,1)S(1)}) custom-call(s32[4]{0:T(128)S(1)} %pad_add_fusion.place, bf16[128,128]{1,0:T(8,128)(2,1)S(1)} %get-tuple-element.36.queries, f32[128,3584]{1,0:T(8,128)S(1)} %get-tuple-element.37.local, ...), custom_call_target="tpu_custom_call", output_to_operand_aliasing={{0}: (11, {})} | custom-call | tf_op jit(solution)/shard_map/pallas_call | solution.py:524
  41.7 0.1 collective-permute-done.8.refs_0_
  41.8 1.5 %shard_map.76 = (bf16[128,3584]{1,0:T(8,128)(2,1)}, f32[1,128]{1,0:T(1,128)}) custom-call(s32[4]{0:T(128)S(1)} %pad_add_fusion.place, bf16[128,128]{1,0:T(8,128)(2,1)S(1)} %get-tuple-element.36.queries, f32[128,3584]{1,0:T(8,128)S(1)} %get-tuple-element.37.local, f32[128,3584]{1,0:T(8,128)S(1)} %get-tuple-element.38.wide_growth, ...), custom_call_target="tpu_custom_call", output_to_operand_aliasing={{0}: (7, {})} | custom-call | tf_op jit(solution)/shard_map/pallas_call | solution.py:524
Async XLA Ops:
  3.4 8.1 %collective-permute-start = (bf16[136,512]{1,0:T(8,128)(2,1)S(1)}, bf16[136,512]{1,0:T(8,128)(2,1)S(1)}, u32[]{:S(2)}, u32[]{:S(2)}) collective-permute-start(bf16[136,512]{1,0:T(8,128)(2,1)S(1)} %get-tuple-element.31), channel_id=1, source_target_pairs={{0,4},{4,0},{8,12},{12,8},{16,20},{20,16},{24,28},{28,24},{1,5},{5... | collective-permute-start | bytes 417800 | tf_op jit(solution)/shard_map/ppermute | solution.py:415
  6.4 7.2 %collective-permute-start.1 = (bf16[136,512]{1,0:T(8,128)(2,1)S(1)}, bf16[136,512]{1,0:T(8,128)(2,1)S(1)}, u32[]{:S(2)}, u32[]{:S(2)}) collective-permute-start(bf16[136,512]{1,0:T(8,128)(2,1)S(1)} %get-tuple-element.33), channel_id=1, source_target_pairs={{0,8},{4,12},{8,0},{12,4},{16,24},{20,28},{24,16},{28,20},{1,9},{5... | collective-permute-start | bytes 417800 | tf_op jit(solution)/shard_map/ppermute | solution.py:415
  8.0 7.6 %collective-permute-start.2 = (bf16[136,512]{1,0:T(8,128)(2,1)S(1)}, bf16[136,512]{1,0:T(8,128)(2,1)S(1)}, u32[]{:S(2)}, u32[]{:S(2)}) collective-permute-start(bf16[136,512]{1,0:T(8,128)(2,1)S(1)} %get-tuple-element.34), channel_id=1, source_target_pairs={{0,12},{4,8},{8,4},{12,0},{16,28},{20,24},{24,20},{28,16},{1,13},{... | collective-permute-start | bytes 417800 | tf_op jit(solution)/shard_map/ppermute | solution.py:415
  8.0 15.2 %collective-permute-start.3 = (bf16[136,384]{1,0:T(8,128)(2,1)S(1)}, bf16[136,384]{1,0:T(8,128)(2,1)S(1)}, u32[]{:S(2)}, u32[]{:S(2)}) collective-permute-start(bf16[136,384]{1,0:T(8,128)(2,1)S(1)} %get-tuple-element.41), channel_id=1, source_target_pairs={{0,4},{4,0},{8,12},{12,8},{16,20},{20,16},{24,28},{28,24},{1,5},{5... | collective-permute-start | bytes 313352 | tf_op jit(solution)/shard_map/ppermute | solution.py:415
  9.9 13.3 %collective-permute-start.4 = (bf16[136,384]{1,0:T(8,128)(2,1)S(1)}, bf16[136,384]{1,0:T(8,128)(2,1)S(1)}, u32[]{:S(2)}, u32[]{:S(2)}) collective-permute-start(bf16[136,384]{1,0:T(8,128)(2,1)S(1)} %get-tuple-element.42), channel_id=1, source_target_pairs={{0,8},{4,12},{8,0},{12,4},{16,24},{20,28},{24,16},{28,20},{1,9},{5... | collective-permute-start | bytes 313352 | tf_op jit(solution)/shard_map/ppermute | solution.py:415
  11.5 11.8 %collective-permute-start.5 = (bf16[136,384]{1,0:T(8,128)(2,1)S(1)}, bf16[136,384]{1,0:T(8,128)(2,1)S(1)}, u32[]{:S(2)}, u32[]{:S(2)}) collective-permute-start(bf16[136,384]{1,0:T(8,128)(2,1)S(1)} %get-tuple-element.43), channel_id=1, source_target_pairs={{0,12},{4,8},{8,4},{12,0},{16,28},{20,24},{24,20},{28,16},{1,13},{... | collective-permute-start | bytes 313352 | tf_op jit(solution)/shard_map/ppermute | solution.py:415
  13.7 16.5 %collective-permute-start.12 = (bf16[896,128]{1,0:T(8,128)(2,1)}, bf16[896,128]{1,0:T(8,128)(2,1)S(1)}, u32[]{:S(2)}, u32[]{:S(2)}) collective-permute-start(bf16[896,128]{1,0:T(8,128)(2,1)} %refs_3_), channel_id=1, source_target_pairs={{0,2},{1,3},{2,0},{3,1},{4,6},{5,7},{6,4},{7,5},{8,10},{9,11},{10,... | collective-permute-start | bytes 688136 | tf_op jit(solution)/shard_map/ppermute | solution.py:415
  16.3 13.9 %copy-start = (bf16[896,128]{1,0:T(8,128)(2,1)S(1)}, bf16[896,128]{1,0:T(8,128)(2,1)}, u32[]{:S(2)}) copy-start(bf16[896,128]{1,0:T(8,128)(2,1)} %refs_3_) | copy-start | bytes 688132
  16.3 8.4 %collective-permute-start.6 = (bf16[128,512]{1,0:T(8,128)(2,1)S(1)}, bf16[128,512]{1,0:T(8,128)(2,1)S(1)}, u32[]{:S(2)}, u32[]{:S(2)}) collective-permute-start(bf16[128,512]{1,0:T(8,128)(2,1)S(1)} %shard_map.69.refs_0_), channel_id=1, source_target_pairs={{0,16},{4,20},{8,24},{12,28},{16,0},{20,4},{24,8},{28,12},{1,17},{... | collective-permute-start | bytes 393224 | tf_op jit(solution)/shard_map/ppermute | solution.py:415
  18.9 0.7 %copy-start.1 = (f32[56]{0:T(128)S(1)}, f32[56]{0:T(128)}, u32[]{:S(2)}) copy-start(f32[56]{0:T(128)} %skip) | copy-start | bytes 676
  24.2 5.9 %collective-permute-start.7 = (bf16[168,384]{1,0:T(8,128)(2,1)S(1)}, bf16[168,384]{1,0:T(8,128)(2,1)S(1)}, u32[]{:S(2)}, u32[]{:S(2)}) collective-permute-start(bf16[168,384]{1,0:T(8,128)(2,1)S(1)} %shard_map.71.refs_1_), channel_id=1, source_target_pairs={{0,16},{4,20},{8,24},{12,28},{16,0},{20,4},{24,8},{28,12},{1,17},{... | collective-permute-start | bytes 387080 | tf_op jit(solution)/shard_map/ppermute | solution.py:415
  25.4 6.1 %collective-permute-start.14 = (bf16[128,512]{1,0:T(8,128)(2,1)S(1)}, bf16[128,512]{1,0:T(8,128)(2,1)S(1)}, u32[]{:S(2)}, u32[]{:S(2)}) collective-permute-start(bf16[128,512]{1,0:T(8,128)(2,1)S(1)} %get-tuple-element.50), channel_id=1, source_target_pairs={{0,4},{4,0},{8,12},{12,8},{16,20},{20,16},{24,28},{28,24},{1,5},{5... | collective-permute-start | bytes 393224 | tf_op jit(solution)/shard_map/ppermute | solution.py:415
  27.4 6.6 %collective-permute-start.15 = (bf16[128,512]{1,0:T(8,128)(2,1)S(1)}, bf16[128,512]{1,0:T(8,128)(2,1)S(1)}, u32[]{:S(2)}, u32[]{:S(2)}) collective-permute-start(bf16[128,512]{1,0:T(8,128)(2,1)S(1)} %get-tuple-element.51), channel_id=1, source_target_pairs={{0,8},{4,12},{8,0},{12,4},{16,24},{20,28},{24,16},{28,20},{1,9},{5... | collective-permute-start | bytes 393224 | tf_op jit(solution)/shard_map/ppermute | solution.py:415
  29.8 6.2 %collective-permute-start.16 = (bf16[128,512]{1,0:T(8,128)(2,1)S(1)}, bf16[128,512]{1,0:T(8,128)(2,1)S(1)}, u32[]{:S(2)}, u32[]{:S(2)}) collective-permute-start(bf16[128,512]{1,0:T(8,128)(2,1)S(1)} %get-tuple-element.52), channel_id=1, source_target_pairs={{0,12},{4,8},{8,4},{12,0},{16,28},{20,24},{24,20},{28,16},{1,13},{... | collective-permute-start | bytes 393224 | tf_op jit(solution)/shard_map/ppermute | solution.py:415
  30.1 8.5 %collective-permute-start.11 = (bf16[896,128]{1,0:T(8,128)(2,1)S(1)}, bf16[896,128]{1,0:T(8,128)(2,1)S(1)}, u32[]{:S(2)}, u32[]{:S(2)}) collective-permute-start(bf16[896,128]{1,0:T(8,128)(2,1)S(1)} %copy-done), channel_id=1, source_target_pairs={{0,1},{1,0},{2,3},{3,2},{4,5},{5,4},{6,7},{7,6},{8,9},{9,8},{10,11... | collective-permute-start | bytes 688136 | tf_op jit(solution)/shard_map/ppermute | solution.py:415
  30.1 10.0 %collective-permute-start.13 = (bf16[896,128]{1,0:T(8,128)(2,1)S(1)}, bf16[896,128]{1,0:T(8,128)(2,1)S(1)}, u32[]{:S(2)}, u32[]{:S(2)}) collective-permute-start(bf16[896,128]{1,0:T(8,128)(2,1)S(1)} %collective-permute-done.12.refs_5_), channel_id=1, source_target_pairs={{0,1},{1,0},{2,3},{3,2},{4,5},{5,4},{6,7},{7,6},{8,9},{9,8},{10,11... | collective-permute-start | bytes 688136 | tf_op jit(solution)/shard_map/ppermute | solution.py:415
  31.5 7.1 %collective-permute-start.9 = (bf16[160,384]{1,0:T(8,128)(2,1)S(1)}, bf16[160,384]{1,0:T(8,128)(2,1)S(1)}, u32[]{:S(2)}, u32[]{:S(2)}) collective-permute-start(bf16[160,384]{1,0:T(8,128)(2,1)S(1)} %get-tuple-element.46), channel_id=1, source_target_pairs={{0,4},{4,0},{8,12},{12,8},{16,20},{20,16},{24,28},{28,24},{1,5},{5... | collective-permute-start | bytes 368648 | tf_op jit(solution)/shard_map/ppermute | solution.py:415
  34.0 6.2 %collective-permute-start.10 = (bf16[160,384]{1,0:T(8,128)(2,1)S(1)}, bf16[160,384]{1,0:T(8,128)(2,1)S(1)}, u32[]{:S(2)}, u32[]{:S(2)}) collective-permute-start(bf16[160,384]{1,0:T(8,128)(2,1)S(1)} %get-tuple-element.47), channel_id=1, source_target_pairs={{0,8},{4,12},{8,0},{12,4},{16,24},{20,28},{24,16},{28,20},{1,9},{5... | collective-permute-start | bytes 368648 | tf_op jit(solution)/shard_map/ppermute | solution.py:415
  36.0 5.8 %collective-permute-start.8 = (bf16[160,384]{1,0:T(8,128)(2,1)S(1)}, bf16[160,384]{1,0:T(8,128)(2,1)S(1)}, u32[]{:S(2)}, u32[]{:S(2)}) collective-permute-start(bf16[160,384]{1,0:T(8,128)(2,1)S(1)} %get-tuple-element.44), channel_id=1, source_target_pairs={{0,12},{4,8},{8,4},{12,0},{16,28},{20,24},{24,20},{28,16},{1,13},{... | collective-permute-start | bytes 368648 | tf_op jit(solution)/shard_map/ppermute | solution.py:415

commit v5 on v4

--- a/solution.py
+++ b/solution.py
@@ -102,73 +102,80 @@
     return [y.astype(F32) for y in split(x)]
 
 
-def piece_counts(width, head_dim):
-    return [width // 128] * 2 + [width // head_dim] * 2
-
-
-def state_kernel(head_dim, count, place, kq_from, values_from, log_decay_from, *refs):
-    *outs, kq, values, log_decay, sems = refs
+def piece_counts(width, heads):
+    return [width // 128] * 2 + [heads] * 2
+
+
+def first_kernel(head_dim, lanes, place, kq_from, values_from, log_decay_from, *refs):
+    *pieces, kq, values, log_decay, sems = refs
     copies = start_all([(log_decay_from, log_decay), (kq_from, kq), (values_from, values)], sems)
-    pieces = [outs[i : i + count] for i in range(0, len(outs), count)]
-    lanes = sum(piece[0].shape[1] for piece in pieces)
     copies[0].wait()
+    decay = decay_left(log_decay[...])
+    copies[1].wait()
+    keys = jnp.transpose(kq[:, :N])
+    wides = [spread(decay, first_head(place, m, lanes, head_dim), pieces[0].shape[1], head_dim) for m in range(len(pieces))]
+    copies[2].wait()
+    for m, piece in enumerate(pieces):
+        state_piece(place, m, lanes, 0, keys, values, wides[m], [], piece)
+
+
+def last_kernel(head_dim, lanes, place, kq, values, log_decay, *pieces):
+    width = pieces[0].shape[1]
+    at = lanes - width
     ld = log_decay[...]
-    heads = ld.shape[0]
-    by_position = cumulative_by_position(ld)
-    final = by_position[GROUP - 1 :, :]
-    decay_left = jnp.exp(final - by_position)
-    last = jnp.broadcast_to(jnp.exp(final), (8, heads))
+    heads, rows = ld.shape[0], head_rows(lanes, head_dim)
+    decay = decay_left(ld)
     growth = split(jnp.exp(cumulative_by_head(ld)))
-    copies[1].wait()
     query_sums = dot(growth[0], kq[:, N:]) + dot(growth[1], kq[:, N:])
     keys = jnp.transpose(kq[:, :N])
-    rows = head_rows(lanes, head_dim)
-    broads = []
-    for m in range(count):
-        first = (place[OWN] ^ m) * (lanes // head_dim)
-        broad = spread(jnp.concatenate([decay_left, last], axis=0), first, lanes, head_dim)
-        broads.append(broad[:GROUP])
+    for m, piece in enumerate(pieces):
+        first = first_head(place, m, lanes, head_dim)
         own = iota((rows, heads), 1) == first + iota((rows, heads), 0)
-        mine = dot(own.astype(F32), query_sums, precision=HIGHEST)
-        at = 0
-        for piece in pieces:
-            width = piece[m].shape[1]
-            here = mine[at // head_dim : (at + width) // head_dim]
-            tiles = [tile for x in pieces_of(broad[GROUP : GROUP + 1, at : at + width]) for tile in tiles_of(x)]
-            tiles += [tile for x in pieces_of(here) for tile in tiles_of(x)]
-            below = notes(tiles, width)
-            piece[m][pl.ds(N, below.shape[0]), :] = below
-            at += width
-    copies[2].wait()
-    for m in range(count):
-        at = 0
-        for piece in pieces:
-            width = piece[m].shape[1]
-            start = pl.multiple_of((place[OWN] ^ m) * lanes + at, 128)
-            weighted = (values[:, pl.ds(start, width)].astype(F32) * broads[m][:, at : at + width]).astype(BF16)
-            piece[m][pl.ds(0, N), :] = dot(keys, weighted).astype(BF16)
-            at += width
-
-
-def piece_notes(piece, head_dim):
+        mine = dot(own.astype(F32), query_sums, precision=HIGHEST)[: lanes // head_dim]
+        tiles = [tile for x in pieces_of(mine) for tile in tiles_of(x)]
+        broad = spread(decay, first + at // head_dim, width, head_dim)
+        state_piece(place, m, lanes, at, keys, values, broad, tiles, piece)
+
+
+def first_head(place, m, lanes, head_dim):
+    return (place[OWN] ^ m) * (lanes // head_dim)
+
+
+def decay_left(log_decay):
+    by_position = cumulative_by_position(log_decay)
+    final = by_position[GROUP - 1 :, :]
+    return jnp.concatenate([jnp.exp(final - by_position), jnp.broadcast_to(jnp.exp(final), (8, final.shape[1]))], axis=0)
+
+
+def state_piece(place, m, lanes, at, keys, values, broad, tiles, piece):
     width = piece.shape[1]
-    high, low, query_high, query_low = read_notes(piece, piece_counts(width, head_dim))
-    rows = head_rows(width, head_dim)
-    queries = jnp.concatenate([heads_of(query_high, rows), heads_of(query_low, rows)], axis=0)
-    return wide(high) + wide(low), queries
-
-
-def block_kernel(head_dim, kq_from, values_from, log_decay_from, skip, out, wide_growth, sums, kept, *scratch):
-    kq, values, log_decay, sems = scratch
-    copies = start_all([(kq_from, kq), (values_from, values), (log_decay_from, log_decay)], sems)
-    for copy in copies:
-        copy.wait()
+    below = notes([tile for x in pieces_of(broad[GROUP : GROUP + 1]) for tile in tiles_of(x)] + tiles, width)
+    piece[pl.ds(N, below.shape[0]), :] = below
+    start = pl.multiple_of((place[OWN] ^ m) * lanes + at, 128)
+    weighted = (values[:, pl.ds(start, width)].astype(F32) * broad[:GROUP]).astype(BF16)
+    piece[pl.ds(0, N), :] = dot(keys, weighted).astype(BF16)
+
+
+def piece_factor(piece):
+    high, low = read_notes(piece, [piece.shape[1] // 128] * 2)
+    return wide(high) + wide(low)
+
+
+def piece_queries(piece, head_dim, widths):
+    _, _, high, low = read_notes(piece, piece_counts(widths[-1], sum(widths) // head_dim))
+    out, at = [], 0
+    for width in widths:
+        rows, end = head_rows(width, head_dim), at + width // head_dim
+        out.append(jnp.concatenate([heads_of(high[at:end], rows), heads_of(low[at:end], rows)], axis=0))
+        at = end
+    return out
+
+
+def block_kernel(head_dim, kq, values, log_decay, skip, out, wide_growth, sums):
     ld = log_decay[...]
     by_position = cumulative_by_position(ld)
     by_head = cumulative_by_head(ld)
-    queries = kq[:, N:]
-    kept[...] = queries
-    scores = dot(queries, kq[:, :N], ((1,), (1,)))
+    scores = dot(kq[:, N:], kq[:, :N], ((1,), (1,)))
     causal = iota((GROUP, GROUP), 0) >= iota((GROUP, GROUP), 1)
     per = 128 // head_dim
     lane = iota((GROUP, 128), 1) // head_dim
@@ -198,15 +205,22 @@
         sums[line : line + 1, :] = jnp.sum(mixed, axis=0, keepdims=True)
 
 
+def at_index(place, count, body):
+    for index in range(count):
+        pl.when(place[INDEX] == index)(functools.partial(body, index))
+
+
 def total_kernel(head_dim, place, *refs):
-    *pieces, total, ordered, factors = refs
-    for m, piece in enumerate(pieces):
-        ordered[place[INDEX] ^ m] = piece[pl.ds(0, N), :]
-        factors[place[INDEX] ^ m] = piece_notes(piece, head_dim)[0]
-    running = ordered[0].astype(F32)
-    for j in range(1, len(pieces)):
-        running = factors[j] * running + ordered[j].astype(F32)
-    total[...] = running.astype(BF16)
+    *pieces, total = refs
+    factors = [piece_factor(piece) for piece in pieces]
+
+    def body(index):
+        running = pieces[index][pl.ds(0, N), :].astype(F32)
+        for j in range(1, len(pieces)):
+            running = factors[j ^ index] * running + pieces[j ^ index][pl.ds(0, N), :].astype(F32)
+        total[...] = running.astype(BF16)
+
+    at_index(place, len(pieces), body)
 
 
 def totals_kernel(head_dim, count, pair, place, sums, *refs):
@@ -214,11 +228,15 @@
     parts, outs = refs[: PIECES * count], refs[PIECES * count : -3 * PIECES]
     lanes = 0
     carried, weights, totals, decays = [], [], [], []
+    widths = [scratch[3 * k].shape[2] for k in range(PIECES)]
+    for m, piece in enumerate(parts[-count:]):
+        for k, x in enumerate(piece_queries(piece, head_dim, widths)):
+            scratch[3 * k + 2][place[INDEX] ^ m] = x
     for k in range(PIECES):
         ordered, factors, queries = scratch[3 * k : 3 * k + 3]
         for m, piece in enumerate(parts[k * count : (k + 1) * count]):
             ordered[place[INDEX] ^ m] = piece[pl.ds(0, N), :]
-            factors[place[INDEX] ^ m], queries[place[INDEX] ^ m] = piece_notes(piece, head_dim)
+            factors[place[INDEX] ^ m] = piece_factor(piece)
         width = ordered.shape[2]
         lanes += width
         rows = head_rows(width, head_dim)
@@ -244,10 +262,8 @@
         for out, x in zip(outs, [*totals, wide(decays)]):
             out[...] = x
         return
-    tiles = [tile for x in thirds(wide(carried)) for tile in tiles_of(x.astype(F32))] + weights
-    for x in pieces_of(sums[...]):
-        tiles += sums_tiles(x, lanes)
-    below = notes(tiles, outs[0].shape[1])
+    known = wide(sums_tiles(sums[...], lanes)) + in_own_part(place, count, wide(carried))
+    below = notes(weights + sums_notes(known), outs[0].shape[1])
     outs[0][pl.ds(0, N), :] = totals[-1]
     outs[0][pl.ds(N, below.shape[0]), :] = below
 
@@ -256,35 +272,36 @@
     return [sums[i : i + 1] for i in range(sums.shape[0]) if i % 8 < lanes // 128]
 
 
+def in_own_part(place, count, x):
+    return wide([jnp.where(place[OWN] == k, x, 0.0) for k in range(count)])
+
+
 def starts_kernel(head_dim, count, lanes, place, *refs):
-    refs, pieces, outs, scratch = refs[: -3 - 2 * count], refs[-3 - 2 * count : -3 - count], refs[-3 - count : -3], refs[-3:]
-    ordered, factors, results = scratch
-    width = outs[0].shape[1]
-    for m, piece in enumerate(pieces):
-        ordered[place[INDEX] ^ m] = piece[pl.ds(0, N), :]
-        factors[place[INDEX] ^ m] = piece_notes(piece, head_dim)[0]
-    running = jnp.where(place[WHICH] == 0, 0.0, refs[-1][pl.ds(0, N), :].astype(F32))
-    for j in range(count):
-        results[j] = running.astype(BF16)
-        if j < count - 1:
-            running = factors[j] * running + ordered[j].astype(F32)
+    refs, pieces, outs = refs[: -2 * count], refs[-2 * count : -count], refs[-count:]
+    factors = [piece_factor(piece) for piece in pieces]
+
+    def body(index):
+        running = jnp.where(place[WHICH] == 0, 0.0, refs[-1][pl.ds(0, N), :].astype(F32))
+        for j in range(count):
+            outs[j ^ index][pl.ds(0, N), :] = running.astype(BF16)
+            if j < count - 1:
+                running = factors[j ^ index] * running + pieces[j ^ index][pl.ds(0, N), :].astype(F32)
+
+    at_index(place, count, body)
     if len(refs) > 1:
-        sums, fellows = sums_of(place, head_dim, lanes, count, refs[: len(refs) // 2], refs[len(refs) // 2 :])
-        below = notes(sums_notes(sums, fellows), width)
-    for m, out in enumerate(outs):
-        out[pl.ds(0, N), :] = results[place[INDEX] ^ m]
-        if len(refs) > 1:
+        sums = sums_of(place, head_dim, lanes, count, refs[: len(refs) // 2], refs[len(refs) // 2 :])
+        below = notes(sums_notes(sums), outs[0].shape[1])
+        for out in outs:
             out[pl.ds(N, below.shape[0]), :] = below
 
 
-def sums_notes(sums, fellows):
-    tiles = [tile for x in thirds(sums) for tile in tiles_of(x.astype(F32))]
-    return tiles + [tile for x in pieces_of(fellows) for tile in tiles_of(x)]
+def sums_notes(sums):
+    return [tile for x in pieces_of(sums) for tile in tiles_of(x)]
 
 
 def sums_of(place, head_dim, lanes, count, totals, before):
     first = place[WHICH] == 0
-    counts = [lanes // 128] * 3
+    counts = []
     for total in totals:
         counts += [total.shape[1] // head_dim] * 2
     counts += [count * lanes // 128] * 2
@@ -294,17 +311,12 @@
         rows = head_rows(total.shape[1], head_dim)
         weight = [
             jnp.where(first, heads_of(there, rows), heads_of(here, rows))
-            for here, there in zip(mine[3 + 2 * k : 5 + 2 * k], other[3 + 2 * k : 5 + 2 * k])
+            for here, there in zip(mine[2 * k : 2 * k + 2], other[2 * k : 2 * k + 2])
         ]
         state = jnp.where(first, total[pl.ds(0, N), :].astype(F32), got[pl.ds(0, N), :].astype(F32)).astype(BF16)
         products.append(own_heads(heads_dot(jnp.concatenate(weight, axis=0).astype(BF16), state), head_dim))
-    fellows = sum(wide(here) + wide(there) for here, there in zip(mine[-2:], other[-2:]))
-    return wide(products) + sum(wide(here) + wide(there) for here, there in zip(mine[:3], other[:3])), fellows
-
-
-def thirds(x):
-    high = x.astype(BF16)
-    return high, *split(x - high.astype(F32))
+    known = sum(wide(here) + wide(there) for here, there in zip(mine[-2:], other[-2:]))
+    return known + in_own_part(place, count, wide(products))
 
 
 def heads_dot(queries, state):
@@ -322,15 +334,17 @@
     *refs, out = refs
     pieces, states = refs[: PIECES * count], refs[PIECES * count :]
     carried = []
+    widths = [pieces[k * count].shape[1] for k in range(PIECES)]
+    queries = [piece_queries(piece, head_dim, widths) for piece in pieces[-count:]]
     for k in range(PIECES):
         added = 0.0
-        for piece, state in zip(pieces[k * count : (k + 1) * count], states[k * count : (k + 1) * count]):
-            added = added + heads_dot(piece_notes(piece, head_dim)[1].astype(BF16), state[pl.ds(0, N), :])
+        for query, state in zip(queries, states[k * count : (k + 1) * count]):
+            added = added + heads_dot(query[k].astype(BF16), state[pl.ds(0, N), :])
         carried.append(own_heads(added, head_dim))
     out[...] = wide(carried)
 
 
-def output_kernel(ms, count, lanes, offset, step, positions, place, queries, local, wide_growth, *refs):
+def output_kernel(ms, count, lanes, offset, step, positions, place, kq, local, wide_growth, *refs):
     carried, refs = refs[: len(ms)], refs[len(ms) :]
     *refs, made, sems = refs
     copies = []
@@ -339,21 +353,20 @@
     mixed = refs[{0: -1, 1: -3, 2: -4}[step]]
     for i, state in enumerate(carried):
         here = pl.ds(at[i], width)
-        made[i] = (local[:, here] + wide_growth[:, here] * dot(queries[...], state[pl.ds(0, N), :])).astype(BF16)
+        made[i] = (local[:, here] + wide_growth[:, here] * dot(kq[:, N:], state[pl.ds(0, N), :])).astype(BF16)
         copies.append(pltpu.make_async_copy(made.at[i], mixed.at[:, here], sems.at[i]))
         copies[-1].start()
     if step == 1:
         weights, (pooled, rows) = refs[:count], refs[-2:]
-        for k, x in enumerate(weights):
-            rows[place[HELD] ^ place[OWN] ^ k] = x[...]
+        for k in range(count):
+            rows[place[HELD] ^ place[OWN] ^ k] = weights[k][...]
         pooled[...] = jnp.zeros_like(pooled)
     if step == 2:
         before, rows, logits, pooled, scaled = refs[0], refs[1], refs[-3], refs[-2], refs[-1]
         pooled[...] = before[...]
     if step:
         for m, state in zip(ms, carried):
-            *own, high, low = read_notes(state, [lanes // 128] * 3 + [count * lanes // 128] * 2)
-            pooled[m] += jnp.broadcast_to(sum(wide(x) for x in own), (8, lanes))
+            high, low = read_notes(state, [count * lanes // 128] * 2)
             for k in range(count):
                 part = slice(k * (lanes // 128), (k + 1) * (lanes // 128))
                 pooled[place[OWN] ^ k] += jnp.broadcast_to(wide(high[part]) + wide(low[part]), (8, lanes))
@@ -396,7 +409,7 @@
     place = jnp.stack([index % group, index // group, (index % group) ^ column, column]).astype(jnp.int32)
     values, kq, ld = inputs[0], keys_queries[0], log_decay[0]
     sources = [pltpu.with_memory_space_constraint(x, pltpu.HBM) for x in (kq, values, ld)]
-    landing = [pltpu.VMEM(x.shape, x.dtype) for x in (kq, values, ld)] + [pltpu.SemaphoreType.DMA((3,))]
+    landing = [jax.ShapeDtypeStruct(x.shape, x.dtype) for x in (kq, values, ld)]
     tiles = lanes // 128
     widths = [(tiles + 1) // 2 * 128, tiles // 2 * 128] if PIECES == 2 else [lanes]
     offsets = [0, widths[0]][:PIECES]
@@ -420,15 +433,20 @@
     def shift(x, by):
         return lax.ppermute(x, "seq", [(i, i + by) for i in range(size - by)])
 
-    parts = call(
-        functools.partial(state_kernel, head_dim, group),
-        [piece(width, sum(piece_counts(width, head_dim))) for width in widths for _ in range(group)],
+    *first, kq, values, ld = call(
+        functools.partial(first_kernel, head_dim, lanes),
+        [piece(widths[0], sum(piece_counts(widths[0], 0)))] * group + landing,
         [SMEM] + [ANY] * 3,
-        landing,
+        [pltpu.SemaphoreType.DMA((3,))],
         flops=2 * positions * N * channels,
         moved=4 * positions * channels,
     )(place, *sources)
-    parts = [swap_all(parts[i : i + group]) for i in range(0, len(parts), group)]
+    last = call(
+        functools.partial(last_kernel, head_dim, lanes),
+        [piece(widths[1], sum(piece_counts(widths[1], lanes // head_dim)))] * group,
+        [SMEM] + [VMEM] * 3,
+    )(place, kq, values, ld)
+    parts = [swap_all(first), swap_all(last)]
     classifier, parts[0][1] = lax.optimization_barrier((classifier, parts[0][1]))
     totals = []
     if pair and PIECES == 2:
@@ -437,19 +455,17 @@
                 functools.partial(total_kernel, head_dim),
                 piece(widths[0], 0),
                 [SMEM] + [VMEM] * group,
-                [pltpu.VMEM((group, N, widths[0]), BF16), pltpu.VMEM((group, 1, widths[0]), F32)],
             )(place, *parts[0])
         )
         skip = lax.optimization_barrier((skip, totals))[0]
     made = call(
         functools.partial(block_kernel, head_dim),
-        [full, full, jax.ShapeDtypeStruct((8 * group, 128), F32), jax.ShapeDtypeStruct((positions, N), BF16)],
-        [ANY] * 3 + [SMEM],
-        landing,
+        [full, full, jax.ShapeDtypeStruct((8 * group, 128), F32)],
+        [VMEM] * 3 + [SMEM],
         flops=8 * positions * N * channels,
         moved=6 * positions * channels,
-    )(*sources, skip)
-    from_block, wide_growth, sums, queries = made
+    )(kq, values, ld, skip)
+    from_block, wide_growth, sums = made
     scratch = []
     for width in widths:
         scratch += [
@@ -459,7 +475,7 @@
         ]
     totals += call(
         functools.partial(totals_kernel, head_dim, group, pair),
-        [piece(widths[-1], 3 * tiles + 2 * (lanes // head_dim) + 2 * group * tiles)] if pair else [piece(w, 0) for w in widths] + [row],
+        [piece(widths[-1], 2 * (lanes // head_dim) + 2 * group * tiles)] if pair else [piece(w, 0) for w in widths] + [row],
         [SMEM] + [VMEM] * (1 + PIECES * group),
         scratch,
     )(place, sums, *[x for part in parts for x in part])
@@ -478,8 +494,8 @@
                 factor = factor * shift(factor, group * reach)
                 reach *= 2
             before.append(running.astype(BF16))
+
     weights = [classifier, swap(classifier, 1, "fsdp"), crossed, swap(crossed, 1, "fsdp")]
-
     starts = []
     for k, width in enumerate(widths):
         last = k == PIECES - 1
@@ -487,13 +503,8 @@
         starts.append(
             call(
                 functools.partial(starts_kernel, head_dim, group, lanes),
-                [piece(width, 3 * tiles + 2 * group * tiles if last and pair else 0)] * group,
+                [piece(width, 2 * group * tiles if last and pair else 0)] * group,
                 [SMEM] + [VMEM] * (len(operands) + group),
-                [
-                    pltpu.VMEM((group, N, width), BF16),
-                    pltpu.VMEM((group, 1, width), F32),
-                    pltpu.VMEM((group, N, width), BF16),
-                ],
             )(place, *operands, *parts[k])
         )
     if not pair:
@@ -508,7 +519,8 @@
         while reach < size:
             sums = sums + swap(sums, reach)
             reach *= 2
-        below = notes(sums_notes(whole, wide(sums_tiles(sums / group, lanes))), widths[-1])
+        known = wide(sums_tiles(sums / group, lanes)) + in_own_part(place, group, whole)
+        below = notes(sums_notes(known), widths[-1])
         starts[-1] = [jnp.concatenate([x, below], axis=0) for x in starts[-1]]
     starts = [swap_all(x) for x in starts]
 
@@ -516,7 +528,7 @@
     plan += [(tuple(range(group - 1)), PIECES - 1, 1), ((group - 1,), PIECES - 1, 2)]
     mixed, rest = None, []
     for i, (ms, k, step) in enumerate(plan):
-        operands = [queries, from_block, wide_growth, *[starts[k][m] for m in ms]]
+        operands = [kq, from_block, wide_growth, *[starts[k][m] for m in ms]]
         operands += {0: [], 1: weights, 2: rest}[step]
         outs = [pltpu.HBM((positions, channels), BF16)]
         outs += {0: [], 1: gathered, 2: [pltpu.HBM((1, classes), F32)]}[step]

time: 43.5 us -> 42.7 us (0.982)
  starting transfers between devices: 25.1 us -> 21 us
  waiting for transfers between devices: 2.46 us -> 6.16 us
  local copies, waits for them, and re-layouts: 0.66 us -> 0.01 us
    ppermute x17, starting transfers between devices: 25.1 us -> 21 us  [swap(): lax.ppermute(x, axis, [(i, i ^ m) for i in range(lax.axis_size(axis))])]
    ppermute x17, waiting for transfers between devices: 2.46 us -> 6.16 us  [swap(): lax.ppermute(x, axis, [(i, i ^ m) for i in range(lax.axis_size(axis))])]
    pallas_call x1 -> x2, Pallas kernels: 2.65 us -> 4.18 us  [the longest x1 2.3 us: local(): call(functools.partial(first_kernel, head_dim, lanes), [piece(widths[0],...]
    pallas_call x1, Pallas kernels: 3.68 us -> 2.43 us  [local(): call(functools.partial(block_kernel, head_dim), [full, full, jax.ShapeDty...]
    unnamed x4, local copies, waits for them, and re-layouts: 0.66 us -> 0.01 us
  transfers between devices with their start and end apart: 17 -> 17, of which waited for: 4 -> 6; matrix products, arithmetic and copies ran while one was open for 0% -> 0% of each run, Pallas kernels for 23% -> 25%
where the time goes in v5:
time: 42.7 us; the launch traced here: 42.5 us
  starting transfers between devices  21 us (49%)
  Pallas kernels  14.4 us (34%)
  waiting for transfers between devices  6.16 us (14%)
  between operations  0.8 us (2%)
    ppermute x17, starting transfers between devices, swap(): lax.ppermute(x, axis, [(i, i ^ m) for i in range(lax.axis_size(axis))])  21 us
    ppermute x17, waiting for transfers between devices, swap(): lax.ppermute(x, axis, [(i, i ^ m) for i in range(lax.axis_size(axis))])  6.16 us
    pallas_call x3, Pallas kernels, local(): call(functools.partial(output_kernel, ms, group, lanes, offsets[k], step,...  4.6 us
    pallas_call x1, Pallas kernels, local(): call(functools.partial(block_kernel, head_dim), [full, full, jax.ShapeDty...  2.43 us
    pallas_call x1, Pallas kernels, local(): call(functools.partial(first_kernel, head_dim, lanes), [piece(widths[0],...  2.3 us
    pallas_call x1, Pallas kernels, local(): call(functools.partial(last_kernel, head_dim, lanes), [piece(widths[1], s...  1.88 us
    pallas_call x2, Pallas kernels, local(): call(functools.partial(starts_kernel, head_dim, group, lanes), [piece(wid...  1.57 us
    pallas_call x1, Pallas kernels, local(): call(functools.partial(totals_kernel, head_dim, group, pair), [piece(widt...  0.97 us
  transfers between devices with their start and end apart: 17, of which 6 were waited for; matrix products, arithmetic and copies ran while one was open for 0% of the time, Pallas kernels for 25%

profile of v5, /device:TPU:0, one launch (start us, length us, event | category | flops | bytes accessed | tf_op | source)
XLA Modules:
  0.0 42.5 jit_solution(1416704771617410417)
XLA Ops:
  0.6 0.0 copy-start
  0.6 0.0 copy-start.1
  0.7 0.1 pad_add_fusion.place
  0.7 2.3 %shard_map.68 = (bf16[136,512]{1,0:T(8,128)(2,1)S(1)}, bf16[136,512]{1,0:T(8,128)(2,1)S(1)}, bf16[136,512]{1,0:T(8,128)(2,1)S(1)}, bf16[136,512]{1,0:T(8,128)(2,...) custom-call(s32[4]{0:T(128)S(1)} %pad_add_fusion.place, ...), custom_call_target="tpu_custom_call" | custom-call | flops 117440512 | bytes 1835008 | tf_op jit(solution)/shard_map/pallas_call | solution.py:436
  3.1 3.0 %collective-permute-start = (bf16[136,512]{1,0:T(8,128)(2,1)S(1)}, bf16[136,512]{1,0:T(8,128)(2,1)S(1)}, u32[]{:S(2)}, u32[]{:S(2)}) collective-permute-start(bf16[136,512]{1,0:T(8,128)(2,1)S(1)} %get-tuple-element.36), channel_id=1, source_target_pairs={{0,4},{4,0},{8,12},{12,8},{16,20},{20,16},{24,28},{28,24},{1,5},{5... | collective-permute-start | bytes 417800 | tf_op jit(solution)/shard_map/ppermute | solution.py:428
  6.1 1.6 %collective-permute-start.1 = (bf16[136,512]{1,0:T(8,128)(2,1)S(1)}, bf16[136,512]{1,0:T(8,128)(2,1)S(1)}, u32[]{:S(2)}, u32[]{:S(2)}) collective-permute-start(bf16[136,512]{1,0:T(8,128)(2,1)S(1)} %get-tuple-element.38), channel_id=1, source_target_pairs={{0,8},{4,12},{8,0},{12,4},{16,24},{20,28},{24,16},{28,20},{1,9},{5... | collective-permute-start | bytes 417800 | tf_op jit(solution)/shard_map/ppermute | solution.py:428
  7.7 0.0 collective-permute-start.2
  7.7 1.9 %shard_map.71 = (bf16[144,384]{1,0:T(8,128)(2,1)S(1)}, bf16[144,384]{1,0:T(8,128)(2,1)S(1)}, bf16[144,384]{1,0:T(8,128)(2,1)S(1)}, bf16[144,384]{1,0:T(8,128)(2,1)S(1)}) custom-call(s32[4]{0:T(128)S(1)} %pad_add_fusion.place, bf16[128,256]{1,0:T(8,128)(2,1)S(1)} %get-tuple-element.32.kq, bf16[128,3584]{1,0:T(8,128)(2,1)S(1)} %get-tuple-element.33.values, ...), custom_call_target="tpu_custom_call" | custom-call | tf_op jit(solution)/shard_map/pallas_call | solution.py:444
  9.6 2.0 %collective-permute-start.3 = (bf16[144,384]{1,0:T(8,128)(2,1)S(1)}, bf16[144,384]{1,0:T(8,128)(2,1)S(1)}, u32[]{:S(2)}, u32[]{:S(2)}) collective-permute-start(bf16[144,384]{1,0:T(8,128)(2,1)S(1)} %get-tuple-element.45), channel_id=1, source_target_pairs={{0,4},{4,0},{8,12},{12,8},{16,20},{20,16},{24,28},{28,24},{1,5},{5... | collective-permute-start | bytes 331784 | tf_op jit(solution)/shard_map/ppermute | solution.py:428
  11.5 1.6 %collective-permute-start.4 = (bf16[144,384]{1,0:T(8,128)(2,1)S(1)}, bf16[144,384]{1,0:T(8,128)(2,1)S(1)}, u32[]{:S(2)}, u32[]{:S(2)}) collective-permute-start(bf16[144,384]{1,0:T(8,128)(2,1)S(1)} %get-tuple-element.46), channel_id=1, source_target_pairs={{0,8},{4,12},{8,0},{12,4},{16,24},{20,28},{24,16},{28,20},{1,9},{5... | collective-permute-start | bytes 331784 | tf_op jit(solution)/shard_map/ppermute | solution.py:428
  13.1 0.0 collective-permute-done.refs_1_.refs_2_
  13.1 0.0 collective-permute-start.5
  13.1 0.0 collective-permute-done.1.refs_2_.refs_3_
  13.1 0.0 copy-done
  13.1 1.9 %collective-permute-start.12 = (bf16[896,128]{1,0:T(8,128)(2,1)S(1)}, bf16[896,128]{1,0:T(8,128)(2,1)S(1)}, u32[]{:S(2)}, u32[]{:S(2)}) collective-permute-start(bf16[896,128]{1,0:T(8,128)(2,1)S(1)} %copy-done), channel_id=1, source_target_pairs={{0,2},{1,3},{2,0},{3,1},{4,6},{5,7},{6,4},{7,5},{8,10},{9,11},{10,... | collective-permute-start | bytes 688136 | tf_op jit(solution)/shard_map/ppermute | solution.py:428
  15.0 0.2 collective-permute-done.2.refs_3_.refs_4_
  15.2 0.7 %shard_map.69.refs_0_ = bf16[128,512]{1,0:T(8,128)(2,1)S(1)} custom-call(s32[4]{0:T(128)S(1)} %pad_add_fusion.place, bf16[136,512]{1,0:T(8,128)(2,1)S(1)} %get-tuple-element.35.refs_0_.refs_1_, bf16[136,512]{1,0:T(8,128)(2,1)S(1)} %collective-permute-done.refs_1_.refs_2_, bf16[136,512]{1,0:T(8,128)(2,1)S(1)} %collective-permute-done.1.refs_2_.refs_3_, ...), custom_call_target="tpu_custom_call" | custom-call | tf_op jit(solution)/shard_map/pallas_call | solution.py:454
  15.9 2.7 %collective-permute-start.6 = (bf16[128,512]{1,0:T(8,128)(2,1)S(1)}, bf16[128,512]{1,0:T(8,128)(2,1)S(1)}, u32[]{:S(2)}, u32[]{:S(2)}) collective-permute-start(bf16[128,512]{1,0:T(8,128)(2,1)S(1)} %shard_map.69.refs_0_), channel_id=1, source_target_pairs={{0,16},{4,20},{8,24},{12,28},{16,0},{20,4},{24,8},{28,12},{1,17},{... | collective-permute-start | bytes 393224 | tf_op jit(solution)/shard_map/ppermute | solution.py:428
  18.5 0.0 copy-done.1
  18.5 2.4 %shard_map.70 = (f32[128,3584]{1,0:T(8,128)S(1)}, f32[128,3584]{1,0:T(8,128)S(1)}, f32[32,128]{1,0:T(8,128)S(1)}) custom-call(bf16[128,256]{1,0:T(8,128)(2,1)S(1)} %get-tuple-element.32.kq, bf16[128,3584]{1,0:T(8,128)(2,1)S(1)} %get-tuple-element.33.values, f32[56,128]{1,0:T(8,128)S(1)} %get-tuple-element.34.log_decay, f32[56]{0:T(128)S(1)} %copy-done.1), custom_call_target="tpu_custom_call" | custom-call | flops 469762048 | bytes 2752512 | tf_op jit(solution)/shard_map/pallas_call | solution.py:461
  21.0 0.0 collective-permute-done.3.refs_5_
  21.0 0.0 collective-permute-done.4.refs_6_
  21.0 0.0 collective-permute-done.5.refs_7_
  21.0 1.0 %shard_map.72.refs_1_ = bf16[160,384]{1,0:T(8,128)(2,1)S(1)} custom-call(s32[4]{0:T(128)S(1)} %pad_add_fusion.place, f32[32,128]{1,0:T(8,128)S(1)} %get-tuple-element.43.sums, bf16[136,512]{1,0:T(8,128)(2,1)S(1)} %get-tuple-element.35.refs_0_.refs_1_, bf16[136,512]{1,0:T(8,128)(2,1)S(1)} %collective-permute-done.refs_1_.refs_2_, ...), custom_call_target="tpu_custom_call" | custom-call | tf_op jit(solution)/shard_map/pallas_call | solution.py:476
  22.0 1.6 %collective-permute-start.7 = (bf16[160,384]{1,0:T(8,128)(2,1)S(1)}, bf16[160,384]{1,0:T(8,128)(2,1)S(1)}, u32[]{:S(2)}, u32[]{:S(2)}) collective-permute-start(bf16[160,384]{1,0:T(8,128)(2,1)S(1)} %shard_map.72.refs_1_), channel_id=1, source_target_pairs={{0,16},{4,20},{8,24},{12,28},{16,0},{20,4},{24,8},{28,12},{1,17},{... | collective-permute-start | bytes 368648 | tf_op jit(solution)/shard_map/ppermute | solution.py:428
  23.6 2.3 %collective-permute-done.6.refs_2_.refs_0_ = bf16[128,512]{1,0:T(8,128)(2,1)S(1)} collective-permute-done((bf16[128,512]{1,0:T(8,128)(2,1)S(1)}, bf16[128,512]{1,0:T(8,128)(2,1)S(1)}, u32[]{:S(2)}, u32[]{:S(2)}) %collective-permute-start.6) | collective-permute-done | bytes 131104 | tf_op jit(solution)/shard_map/ppermute | solution.py:428
  25.9 0.7 %shard_map.74 = (bf16[128,512]{1,0:T(8,128)(2,1)S(1)}, bf16[128,512]{1,0:T(8,128)(2,1)S(1)}, bf16[128,512]{1,0:T(8,128)(2,1)S(1)}, bf16[128,512]{1,0:T(8,128)(2,1)S(1)}) custom-call(s32[4]{0:T(128)S(1)} %pad_add_fusion.place, bf16[128,512]{1,0:T(8,128)(2,1)S(1)} %collective-permute-done.6.refs_2_.refs_0_, ...), custom_call_target="tpu_custom_call" | custom-call | tf_op jit(solution)/shard_map/pallas_call | solution.py:504
  26.6 1.7 %collective-permute-start.14 = (bf16[128,512]{1,0:T(8,128)(2,1)S(1)}, bf16[128,512]{1,0:T(8,128)(2,1)S(1)}, u32[]{:S(2)}, u32[]{:S(2)}) collective-permute-start(bf16[128,512]{1,0:T(8,128)(2,1)S(1)} %get-tuple-element.54), channel_id=1, source_target_pairs={{0,4},{4,0},{8,12},{12,8},{16,20},{20,16},{24,28},{28,24},{1,5},{5... | collective-permute-start | bytes 393224 | tf_op jit(solution)/shard_map/ppermute | solution.py:428
  28.3 0.8 %collective-permute-start.15 = (bf16[128,512]{1,0:T(8,128)(2,1)S(1)}, bf16[128,512]{1,0:T(8,128)(2,1)S(1)}, u32[]{:S(2)}, u32[]{:S(2)}) collective-permute-start(bf16[128,512]{1,0:T(8,128)(2,1)S(1)} %get-tuple-element.55), channel_id=1, source_target_pairs={{0,8},{4,12},{8,0},{12,4},{16,24},{20,28},{24,16},{28,20},{1,9},{5... | collective-permute-start | bytes 393224 | tf_op jit(solution)/shard_map/ppermute | solution.py:428
  29.1 1.0 %collective-permute-start.16 = (bf16[128,512]{1,0:T(8,128)(2,1)S(1)}, bf16[128,512]{1,0:T(8,128)(2,1)S(1)}, u32[]{:S(2)}, u32[]{:S(2)}) collective-permute-start(bf16[128,512]{1,0:T(8,128)(2,1)S(1)} %get-tuple-element.56), channel_id=1, source_target_pairs={{0,12},{4,8},{8,4},{12,0},{16,28},{20,24},{24,20},{28,16},{1,13},{... | collective-permute-start | bytes 393224 | tf_op jit(solution)/shard_map/ppermute | solution.py:428
  30.1 0.0 collective-permute-done.7.refs_3_
  30.1 0.0 collective-permute-start.11
  30.1 0.0 collective-permute-done.12.refs_5_
  30.2 0.5 %collective-permute-start.13 = (bf16[896,128]{1,0:T(8,128)(2,1)S(1)}, bf16[896,128]{1,0:T(8,128)(2,1)S(1)}, u32[]{:S(2)}, u32[]{:S(2)}) collective-permute-start(bf16[896,128]{1,0:T(8,128)(2,1)S(1)} %collective-permute-done.12.refs_5_), channel_id=1, source_target_pairs={{0,1},{1,0},{2,3},{3,2},{4,5},{5,4},{6,7},{7,6},{8,9},{9,8},{10,11... | collective-permute-start | bytes 688136 | tf_op jit(solution)/shard_map/ppermute | solution.py:428
  30.7 0.9 %shard_map.73 = (bf16[152,384]{1,0:T(8,128)(2,1)S(1)}, bf16[152,384]{1,0:T(8,128)(2,1)S(1)}, bf16[152,384]{1,0:T(8,128)(2,1)S(1)}, bf16[152,384]{1,0:T(8,128)(2,1)S(1)}) custom-call(s32[4]{0:T(128)S(1)} %pad_add_fusion.place, bf16[128,512]{1,0:T(8,128)(2,1)S(1)} %shard_map.69.refs_0_, bf16[160,384]{1,0:T(8,128)(2,1)S(1)} %shard_map.72.refs_1_, ...), custom_call_target="tpu_custom_call" | custom-call | tf_op jit(solution)/shard_map/pallas_call | solution.py:504
  31.6 1.2 %collective-permute-done.14.refs_1_ = bf16[128,512]{1,0:T(8,128)(2,1)S(1)} collective-permute-done((bf16[128,512]{1,0:T(8,128)(2,1)S(1)}, bf16[128,512]{1,0:T(8,128)(2,1)S(1)}, u32[]{:S(2)}, u32[]{:S(2)}) %collective-permute-start.14) | collective-permute-done | bytes 131104 | tf_op jit(solution)/shard_map/ppermute | solution.py:428
  32.8 1.1 %collective-permute-start.9 = (bf16[152,384]{1,0:T(8,128)(2,1)S(1)}, bf16[152,384]{1,0:T(8,128)(2,1)S(1)}, u32[]{:S(2)}, u32[]{:S(2)}) collective-permute-start(bf16[152,384]{1,0:T(8,128)(2,1)S(1)} %get-tuple-element.50), channel_id=1, source_target_pairs={{0,4},{4,0},{8,12},{12,8},{16,20},{20,16},{24,28},{28,24},{1,5},{5... | collective-permute-start | bytes 350216 | tf_op jit(solution)/shard_map/ppermute | solution.py:428
  33.9 0.0 collective-permute-done.15.refs_2_
  33.9 0.3 collective-permute-start.10
  34.1 0.9 %collective-permute-done.16.refs_3_ = bf16[128,512]{1,0:T(8,128)(2,1)S(1)} collective-permute-done((bf16[128,512]{1,0:T(8,128)(2,1)S(1)}, bf16[128,512]{1,0:T(8,128)(2,1)S(1)}, u32[]{:S(2)}, u32[]{:S(2)}) %collective-permute-start.16) | collective-permute-done | bytes 131104 | tf_op jit(solution)/shard_map/ppermute | solution.py:428
  35.0 1.3 %collective-permute-start.8 = (bf16[152,384]{1,0:T(8,128)(2,1)S(1)}, bf16[152,384]{1,0:T(8,128)(2,1)S(1)}, u32[]{:S(2)}, u32[]{:S(2)}) collective-permute-start(bf16[152,384]{1,0:T(8,128)(2,1)S(1)} %get-tuple-element.48), channel_id=1, source_target_pairs={{0,12},{4,8},{8,4},{12,0},{16,28},{20,24},{24,20},{28,16},{1,13},{... | collective-permute-start | bytes 350216 | tf_op jit(solution)/shard_map/ppermute | solution.py:428
  36.4 1.5 %shard_map.75.refs_7_ = bf16[128,3584]{1,0:T(8,128)(2,1)} custom-call(s32[4]{0:T(128)S(1)} %pad_add_fusion.place, bf16[128,256]{1,0:T(8,128)(2,1)S(1)} %get-tuple-element.32.kq, f32[128,3584]{1,0:T(8,128)S(1)} %get-tuple-element.41.local, f32[128,3584]{1,0:T(8,128)S(1)} %get-tuple-element.42.wide_growth, bf16[128,512]{1,0:T(8,128)(2,1)S(1)} %get-tuple-element.53.refs_0_, ...), custom_call_target="tpu_custom_call" | custom-call | tf_op jit(solution)/shard_map/pallas_call | solution.py:536
  37.9 0.0 collective-permute-done.11.refs_4_
  38.0 0.8 %collective-permute-done.9.refs_1_ = bf16[152,384]{1,0:T(8,128)(2,1)S(1)} collective-permute-done((bf16[152,384]{1,0:T(8,128)(2,1)S(1)}, bf16[152,384]{1,0:T(8,128)(2,1)S(1)}, u32[]{:S(2)}, u32[]{:S(2)}) %collective-permute-start.9) | collective-permute-done | bytes 116768 | tf_op jit(solution)/shard_map/ppermute | solution.py:428
  38.8 0.7 %collective-permute-done.10.refs_2_ = bf16[152,384]{1,0:T(8,128)(2,1)S(1)} collective-permute-done((bf16[152,384]{1,0:T(8,128)(2,1)S(1)}, bf16[152,384]{1,0:T(8,128)(2,1)S(1)}, u32[]{:S(2)}, u32[]{:S(2)}) %collective-permute-start.10) | collective-permute-done | bytes 116768 | tf_op jit(solution)/shard_map/ppermute | solution.py:428
  39.4 0.0 collective-permute-done.13.refs_6_
  39.5 1.5 %shard_map.76 = (bf16[128,3584]{1,0:T(8,128)(2,1)}, f32[4,8,896]{2,1,0:T(8,128)S(1)}, bf16[4,896,128]{2,1,0:T(8,128)(2,1)S(1)}) custom-call(s32[4]{0:T(128)S(1)} %pad_add_fusion.place, bf16[128,256]{1,0:T(8,128)(2,1)S(1)} %get-tuple-element.32.kq, f32[128,3584]{1,0:T(8,128)S(1)} %get-tuple-element.41.local, ...), custom_call_target="tpu_custom_call", output_to_operand_aliasing={{0}: (11, {})} | custom-call | tf_op jit(solution)/shard_map/pallas_call | solution.py:536
  41.0 0.0 collective-permute-done.8.refs_0_
  41.0 1.5 %shard_map.77 = (bf16[128,3584]{1,0:T(8,128)(2,1)}, f32[1,128]{1,0:T(1,128)}) custom-call(s32[4]{0:T(128)S(1)} %pad_add_fusion.place, bf16[128,256]{1,0:T(8,128)(2,1)S(1)} %get-tuple-element.32.kq, f32[128,3584]{1,0:T(8,128)S(1)} %get-tuple-element.41.local, f32[128,3584]{1,0:T(8,128)S(1)} %get-tuple-element.42.wide_growth, ...), custom_call_target="tpu_custom_call", output_to_operand_aliasing={{0}: (7, {})} | custom-call | tf_op jit(solution)/shard_map/pallas_call | solution.py:536
Async XLA Ops:
  0.6 12.5 %copy-start = (bf16[896,128]{1,0:T(8,128)(2,1)S(1)}, bf16[896,128]{1,0:T(8,128)(2,1)}, u32[]{:S(2)}) copy-start(bf16[896,128]{1,0:T(8,128)(2,1)} %refs_3_) | copy-start | bytes 688132
  0.6 17.9 %copy-start.1 = (f32[56]{0:T(128)S(1)}, f32[56]{0:T(128)}, u32[]{:S(2)}) copy-start(f32[56]{0:T(128)} %skip) | copy-start | bytes 676
  3.1 10.1 %collective-permute-start = (bf16[136,512]{1,0:T(8,128)(2,1)S(1)}, bf16[136,512]{1,0:T(8,128)(2,1)S(1)}, u32[]{:S(2)}, u32[]{:S(2)}) collective-permute-start(bf16[136,512]{1,0:T(8,128)(2,1)S(1)} %get-tuple-element.36), channel_id=1, source_target_pairs={{0,4},{4,0},{8,12},{12,8},{16,20},{20,16},{24,28},{28,24},{1,5},{5... | collective-permute-start | bytes 417800 | tf_op jit(solution)/shard_map/ppermute | solution.py:428
  6.1 7.0 %collective-permute-start.1 = (bf16[136,512]{1,0:T(8,128)(2,1)S(1)}, bf16[136,512]{1,0:T(8,128)(2,1)S(1)}, u32[]{:S(2)}, u32[]{:S(2)}) collective-permute-start(bf16[136,512]{1,0:T(8,128)(2,1)S(1)} %get-tuple-element.38), channel_id=1, source_target_pairs={{0,8},{4,12},{8,0},{12,4},{16,24},{20,28},{24,16},{28,20},{1,9},{5... | collective-permute-start | bytes 417800 | tf_op jit(solution)/shard_map/ppermute | solution.py:428
  7.7 7.6 %collective-permute-start.2 = (bf16[136,512]{1,0:T(8,128)(2,1)S(1)}, bf16[136,512]{1,0:T(8,128)(2,1)S(1)}, u32[]{:S(2)}, u32[]{:S(2)}) collective-permute-start(bf16[136,512]{1,0:T(8,128)(2,1)S(1)} %get-tuple-element.39), channel_id=1, source_target_pairs={{0,12},{4,8},{8,4},{12,0},{16,28},{20,24},{24,20},{28,16},{1,13},{... | collective-permute-start | bytes 417800 | tf_op jit(solution)/shard_map/ppermute | solution.py:428
  9.6 11.4 %collective-permute-start.3 = (bf16[144,384]{1,0:T(8,128)(2,1)S(1)}, bf16[144,384]{1,0:T(8,128)(2,1)S(1)}, u32[]{:S(2)}, u32[]{:S(2)}) collective-permute-start(bf16[144,384]{1,0:T(8,128)(2,1)S(1)} %get-tuple-element.45), channel_id=1, source_target_pairs={{0,4},{4,0},{8,12},{12,8},{16,20},{20,16},{24,28},{28,24},{1,5},{5... | collective-permute-start | bytes 331784 | tf_op jit(solution)/shard_map/ppermute | solution.py:428
  11.5 9.5 %collective-permute-start.4 = (bf16[144,384]{1,0:T(8,128)(2,1)S(1)}, bf16[144,384]{1,0:T(8,128)(2,1)S(1)}, u32[]{:S(2)}, u32[]{:S(2)}) collective-permute-start(bf16[144,384]{1,0:T(8,128)(2,1)S(1)} %get-tuple-element.46), channel_id=1, source_target_pairs={{0,8},{4,12},{8,0},{12,4},{16,24},{20,28},{24,16},{28,20},{1,9},{5... | collective-permute-start | bytes 331784 | tf_op jit(solution)/shard_map/ppermute | solution.py:428
  13.1 7.9 %collective-permute-start.5 = (bf16[144,384]{1,0:T(8,128)(2,1)S(1)}, bf16[144,384]{1,0:T(8,128)(2,1)S(1)}, u32[]{:S(2)}, u32[]{:S(2)}) collective-permute-start(bf16[144,384]{1,0:T(8,128)(2,1)S(1)} %get-tuple-element.47), channel_id=1, source_target_pairs={{0,12},{4,8},{8,4},{12,0},{16,28},{20,24},{24,20},{28,16},{1,13},{... | collective-permute-start | bytes 331784 | tf_op jit(solution)/shard_map/ppermute | solution.py:428
  13.1 17.0 %collective-permute-start.12 = (bf16[896,128]{1,0:T(8,128)(2,1)S(1)}, bf16[896,128]{1,0:T(8,128)(2,1)S(1)}, u32[]{:S(2)}, u32[]{:S(2)}) collective-permute-start(bf16[896,128]{1,0:T(8,128)(2,1)S(1)} %copy-done), channel_id=1, source_target_pairs={{0,2},{1,3},{2,0},{3,1},{4,6},{5,7},{6,4},{7,5},{8,10},{9,11},{10,... | collective-permute-start | bytes 688136 | tf_op jit(solution)/shard_map/ppermute | solution.py:428
  15.9 10.0 %collective-permute-start.6 = (bf16[128,512]{1,0:T(8,128)(2,1)S(1)}, bf16[128,512]{1,0:T(8,128)(2,1)S(1)}, u32[]{:S(2)}, u32[]{:S(2)}) collective-permute-start(bf16[128,512]{1,0:T(8,128)(2,1)S(1)} %shard_map.69.refs_0_), channel_id=1, source_target_pairs={{0,16},{4,20},{8,24},{12,28},{16,0},{20,4},{24,8},{28,12},{1,17},{... | collective-permute-start | bytes 393224 | tf_op jit(solution)/shard_map/ppermute | solution.py:428
  22.0 8.2 %collective-permute-start.7 = (bf16[160,384]{1,0:T(8,128)(2,1)S(1)}, bf16[160,384]{1,0:T(8,128)(2,1)S(1)}, u32[]{:S(2)}, u32[]{:S(2)}) collective-permute-start(bf16[160,384]{1,0:T(8,128)(2,1)S(1)} %shard_map.72.refs_1_), channel_id=1, source_target_pairs={{0,16},{4,20},{8,24},{12,28},{16,0},{20,4},{24,8},{28,12},{1,17},{... | collective-permute-start | bytes 368648 | tf_op jit(solution)/shard_map/ppermute | solution.py:428
  26.6 6.2 %collective-permute-start.14 = (bf16[128,512]{1,0:T(8,128)(2,1)S(1)}, bf16[128,512]{1,0:T(8,128)(2,1)S(1)}, u32[]{:S(2)}, u32[]{:S(2)}) collective-permute-start(bf16[128,512]{1,0:T(8,128)(2,1)S(1)} %get-tuple-element.54), channel_id=1, source_target_pairs={{0,4},{4,0},{8,12},{12,8},{16,20},{20,16},{24,28},{28,24},{1,5},{5... | collective-permute-start | bytes 393224 | tf_op jit(solution)/shard_map/ppermute | solution.py:428
  28.3 5.5 %collective-permute-start.15 = (bf16[128,512]{1,0:T(8,128)(2,1)S(1)}, bf16[128,512]{1,0:T(8,128)(2,1)S(1)}, u32[]{:S(2)}, u32[]{:S(2)}) collective-permute-start(bf16[128,512]{1,0:T(8,128)(2,1)S(1)} %get-tuple-element.55), channel_id=1, source_target_pairs={{0,8},{4,12},{8,0},{12,4},{16,24},{20,28},{24,16},{28,20},{1,9},{5... | collective-permute-start | bytes 393224 | tf_op jit(solution)/shard_map/ppermute | solution.py:428
  29.1 5.9 %collective-permute-start.16 = (bf16[128,512]{1,0:T(8,128)(2,1)S(1)}, bf16[128,512]{1,0:T(8,128)(2,1)S(1)}, u32[]{:S(2)}, u32[]{:S(2)}) collective-permute-start(bf16[128,512]{1,0:T(8,128)(2,1)S(1)} %get-tuple-element.56), channel_id=1, source_target_pairs={{0,12},{4,8},{8,4},{12,0},{16,28},{20,24},{24,20},{28,16},{1,13},{... | collective-permute-start | bytes 393224 | tf_op jit(solution)/shard_map/ppermute | solution.py:428
  30.1 7.8 %collective-permute-start.11 = (bf16[896,128]{1,0:T(8,128)(2,1)S(1)}, bf16[896,128]{1,0:T(8,128)(2,1)S(1)}, u32[]{:S(2)}, u32[]{:S(2)}) collective-permute-start(bf16[896,128]{1,0:T(8,128)(2,1)S(1)} %copy-done), channel_id=1, source_target_pairs={{0,1},{1,0},{2,3},{3,2},{4,5},{5,4},{6,7},{7,6},{8,9},{9,8},{10,11... | collective-permute-start | bytes 688136 | tf_op jit(solution)/shard_map/ppermute | solution.py:428
  30.2 9.3 %collective-permute-start.13 = (bf16[896,128]{1,0:T(8,128)(2,1)S(1)}, bf16[896,128]{1,0:T(8,128)(2,1)S(1)}, u32[]{:S(2)}, u32[]{:S(2)}) collective-permute-start(bf16[896,128]{1,0:T(8,128)(2,1)S(1)} %collective-permute-done.12.refs_5_), channel_id=1, source_target_pairs={{0,1},{1,0},{2,3},{3,2},{4,5},{5,4},{6,7},{7,6},{8,9},{9,8},{10,11... | collective-permute-start | bytes 688136 | tf_op jit(solution)/shard_map/ppermute | solution.py:428
  32.8 6.0 %collective-permute-start.9 = (bf16[152,384]{1,0:T(8,128)(2,1)S(1)}, bf16[152,384]{1,0:T(8,128)(2,1)S(1)}, u32[]{:S(2)}, u32[]{:S(2)}) collective-permute-start(bf16[152,384]{1,0:T(8,128)(2,1)S(1)} %get-tuple-element.50), channel_id=1, source_target_pairs={{0,4},{4,0},{8,12},{12,8},{16,20},{20,16},{24,28},{28,24},{1,5},{5... | collective-permute-start | bytes 350216 | tf_op jit(solution)/shard_map/ppermute | solution.py:428
  33.9 5.6 %collective-permute-start.10 = (bf16[152,384]{1,0:T(8,128)(2,1)S(1)}, bf16[152,384]{1,0:T(8,128)(2,1)S(1)}, u32[]{:S(2)}, u32[]{:S(2)}) collective-permute-start(bf16[152,384]{1,0:T(8,128)(2,1)S(1)} %get-tuple-element.51), channel_id=1, source_target_pairs={{0,8},{4,12},{8,0},{12,4},{16,24},{20,28},{24,16},{28,20},{1,9},{5... | collective-permute-start | bytes 350216 | tf_op jit(solution)/shard_map/ppermute | solution.py:428
  35.0 5.9 %collective-permute-start.8 = (bf16[152,384]{1,0:T(8,128)(2,1)S(1)}, bf16[152,384]{1,0:T(8,128)(2,1)S(1)}, u32[]{:S(2)}, u32[]{:S(2)}) collective-permute-start(bf16[152,384]{1,0:T(8,128)(2,1)S(1)} %get-tuple-element.48), channel_id=1, source_target_pairs={{0,12},{4,8},{8,4},{12,0},{16,28},{20,24},{24,20},{28,16},{1,13},{... | collective-permute-start | bytes 350216 | tf_op jit(solution)/shard_map/ppermute | solution.py:428

commit v6 on v5

--- a/solution.py
+++ b/solution.py
@@ -70,7 +70,7 @@
 
 
 def notes_rows(tiles, width):
-    return -(-tiles // (width // 128) // 8) * 8
+    return -(-tiles // (width // 128) // 16) * 16
 
 
 def notes(tiles, width):

time: 42.7 us -> 43.5 us (1.019)
  starting transfers between devices: 21 us -> 21.6 us
    ppermute x17, starting transfers between devices: 21 us -> 21.6 us  [swap(): lax.ppermute(x, axis, [(i, i ^ m) for i in range(lax.axis_size(axis))])]
  transfers between devices with their start and end apart: 17 -> 17, of which waited for: 6 -> 6; matrix products, arithmetic and copies ran while one was open for 0% -> 0% of each run, Pallas kernels for 25% -> 24%
where the time goes in v6:
time: 43.5 us; the launch traced here: 43.3 us
  starting transfers between devices  21.6 us (50%)
  Pallas kernels  14.4 us (33%)
  waiting for transfers between devices  6.48 us (15%)
  between operations  0.8 us (2%)
    ppermute x17, starting transfers between devices, swap(): lax.ppermute(x, axis, [(i, i ^ m) for i in range(lax.axis_size(axis))])  21.6 us
    ppermute x17, waiting for transfers between devices, swap(): lax.ppermute(x, axis, [(i, i ^ m) for i in range(lax.axis_size(axis))])  6.48 us
    pallas_call x3, Pallas kernels, local(): call(functools.partial(output_kernel, ms, group, lanes, offsets[k], step,...  4.6 us
    pallas_call x1, Pallas kernels, local(): call(functools.partial(block_kernel, head_dim), [full, full, jax.ShapeDty...  2.44 us
    pallas_call x1, Pallas kernels, local(): call(functools.partial(first_kernel, head_dim, lanes), [piece(widths[0],...  2.3 us
    pallas_call x1, Pallas kernels, local(): call(functools.partial(last_kernel, head_dim, lanes), [piece(widths[1], s...  1.88 us
    pallas_call x2, Pallas kernels, local(): call(functools.partial(starts_kernel, head_dim, group, lanes), [piece(wid...  1.57 us
    pallas_call x1, Pallas kernels, local(): call(functools.partial(totals_kernel, head_dim, group, pair), [piece(widt...  0.97 us
  transfers between devices with their start and end apart: 17, of which 6 were waited for; matrix products, arithmetic and copies ran while one was open for 0% of the time, Pallas kernels for 24%

profile of v6, /device:TPU:0, one launch (start us, length us, event | category | flops | bytes accessed | tf_op | source)
XLA Modules:
  0.0 43.3 jit_solution(7319667855338737685)
XLA Ops:
  0.6 0.0 copy-start
  0.6 0.0 copy-start.1
  0.7 0.1 pad_add_fusion.place
  0.7 2.3 %shard_map.68 = (bf16[144,512]{1,0:T(8,128)(2,1)S(1)}, bf16[144,512]{1,0:T(8,128)(2,1)S(1)}, bf16[144,512]{1,0:T(8,128)(2,1)S(1)}, bf16[144,512]{1,0:T(8,128)(2,...) custom-call(s32[4]{0:T(128)S(1)} %pad_add_fusion.place, ...), custom_call_target="tpu_custom_call" | custom-call | flops 117440512 | bytes 1835008 | tf_op jit(solution)/shard_map/pallas_call | solution.py:436
  3.1 3.0 %collective-permute-start = (bf16[144,512]{1,0:T(8,128)(2,1)S(1)}, bf16[144,512]{1,0:T(8,128)(2,1)S(1)}, u32[]{:S(2)}, u32[]{:S(2)}) collective-permute-start(bf16[144,512]{1,0:T(8,128)(2,1)S(1)} %get-tuple-element.36), channel_id=1, source_target_pairs={{0,4},{4,0},{8,12},{12,8},{16,20},{20,16},{24,28},{28,24},{1,5},{5... | collective-permute-start | bytes 442376 | tf_op jit(solution)/shard_map/ppermute | solution.py:428
  6.1 1.6 %collective-permute-start.1 = (bf16[144,512]{1,0:T(8,128)(2,1)S(1)}, bf16[144,512]{1,0:T(8,128)(2,1)S(1)}, u32[]{:S(2)}, u32[]{:S(2)}) collective-permute-start(bf16[144,512]{1,0:T(8,128)(2,1)S(1)} %get-tuple-element.38), channel_id=1, source_target_pairs={{0,8},{4,12},{8,0},{12,4},{16,24},{20,28},{24,16},{28,20},{1,9},{5... | collective-permute-start | bytes 442376 | tf_op jit(solution)/shard_map/ppermute | solution.py:428
  7.7 0.0 collective-permute-start.2
  7.7 1.9 %shard_map.71 = (bf16[144,384]{1,0:T(8,128)(2,1)S(1)}, bf16[144,384]{1,0:T(8,128)(2,1)S(1)}, bf16[144,384]{1,0:T(8,128)(2,1)S(1)}, bf16[144,384]{1,0:T(8,128)(2,1)S(1)}) custom-call(s32[4]{0:T(128)S(1)} %pad_add_fusion.place, bf16[128,256]{1,0:T(8,128)(2,1)S(1)} %get-tuple-element.32.kq, bf16[128,3584]{1,0:T(8,128)(2,1)S(1)} %get-tuple-element.33.values, ...), custom_call_target="tpu_custom_call" | custom-call | tf_op jit(solution)/shard_map/pallas_call | solution.py:444
  9.6 2.0 %collective-permute-start.3 = (bf16[144,384]{1,0:T(8,128)(2,1)S(1)}, bf16[144,384]{1,0:T(8,128)(2,1)S(1)}, u32[]{:S(2)}, u32[]{:S(2)}) collective-permute-start(bf16[144,384]{1,0:T(8,128)(2,1)S(1)} %get-tuple-element.45), channel_id=1, source_target_pairs={{0,4},{4,0},{8,12},{12,8},{16,20},{20,16},{24,28},{28,24},{1,5},{5... | collective-permute-start | bytes 331784 | tf_op jit(solution)/shard_map/ppermute | solution.py:428
  11.5 1.6 %collective-permute-start.4 = (bf16[144,384]{1,0:T(8,128)(2,1)S(1)}, bf16[144,384]{1,0:T(8,128)(2,1)S(1)}, u32[]{:S(2)}, u32[]{:S(2)}) collective-permute-start(bf16[144,384]{1,0:T(8,128)(2,1)S(1)} %get-tuple-element.46), channel_id=1, source_target_pairs={{0,8},{4,12},{8,0},{12,4},{16,24},{20,28},{24,16},{28,20},{1,9},{5... | collective-permute-start | bytes 331784 | tf_op jit(solution)/shard_map/ppermute | solution.py:428
  13.1 0.0 collective-permute-done.refs_1_.refs_2_
  13.1 0.0 collective-permute-start.5
  13.1 0.0 collective-permute-done.1.refs_2_.refs_3_
  13.1 0.0 copy-done
  13.1 1.9 %collective-permute-start.12 = (bf16[896,128]{1,0:T(8,128)(2,1)S(1)}, bf16[896,128]{1,0:T(8,128)(2,1)S(1)}, u32[]{:S(2)}, u32[]{:S(2)}) collective-permute-start(bf16[896,128]{1,0:T(8,128)(2,1)S(1)} %copy-done), channel_id=1, source_target_pairs={{0,2},{1,3},{2,0},{3,1},{4,6},{5,7},{6,4},{7,5},{8,10},{9,11},{10,... | collective-permute-start | bytes 688136 | tf_op jit(solution)/shard_map/ppermute | solution.py:428
  15.0 0.4 collective-permute-done.2.refs_3_.refs_4_
  15.4 0.7 %shard_map.69.refs_0_ = bf16[128,512]{1,0:T(8,128)(2,1)S(1)} custom-call(s32[4]{0:T(128)S(1)} %pad_add_fusion.place, bf16[144,512]{1,0:T(8,128)(2,1)S(1)} %get-tuple-element.35.refs_0_.refs_1_, bf16[144,512]{1,0:T(8,128)(2,1)S(1)} %collective-permute-done.refs_1_.refs_2_, bf16[144,512]{1,0:T(8,128)(2,1)S(1)} %collective-permute-done.1.refs_2_.refs_3_, ...), custom_call_target="tpu_custom_call" | custom-call | tf_op jit(solution)/shard_map/pallas_call | solution.py:454
  16.1 2.7 %collective-permute-start.6 = (bf16[128,512]{1,0:T(8,128)(2,1)S(1)}, bf16[128,512]{1,0:T(8,128)(2,1)S(1)}, u32[]{:S(2)}, u32[]{:S(2)}) collective-permute-start(bf16[128,512]{1,0:T(8,128)(2,1)S(1)} %shard_map.69.refs_0_), channel_id=1, source_target_pairs={{0,16},{4,20},{8,24},{12,28},{16,0},{20,4},{24,8},{28,12},{1,17},{... | collective-permute-start | bytes 393224 | tf_op jit(solution)/shard_map/ppermute | solution.py:428
  18.8 0.0 copy-done.1
  18.8 2.4 %shard_map.70 = (f32[128,3584]{1,0:T(8,128)S(1)}, f32[128,3584]{1,0:T(8,128)S(1)}, f32[32,128]{1,0:T(8,128)S(1)}) custom-call(bf16[128,256]{1,0:T(8,128)(2,1)S(1)} %get-tuple-element.32.kq, bf16[128,3584]{1,0:T(8,128)(2,1)S(1)} %get-tuple-element.33.values, f32[56,128]{1,0:T(8,128)S(1)} %get-tuple-element.34.log_decay, f32[56]{0:T(128)S(1)} %copy-done.1), custom_call_target="tpu_custom_call" | custom-call | flops 469762048 | bytes 2752512 | tf_op jit(solution)/shard_map/pallas_call | solution.py:461
  21.2 0.0 collective-permute-done.3.refs_5_
  21.2 0.0 collective-permute-done.4.refs_6_
  21.3 0.0 collective-permute-done.5.refs_7_
  21.3 1.0 %shard_map.72.refs_1_ = bf16[160,384]{1,0:T(8,128)(2,1)S(1)} custom-call(s32[4]{0:T(128)S(1)} %pad_add_fusion.place, f32[32,128]{1,0:T(8,128)S(1)} %get-tuple-element.43.sums, bf16[144,512]{1,0:T(8,128)(2,1)S(1)} %get-tuple-element.35.refs_0_.refs_1_, bf16[144,512]{1,0:T(8,128)(2,1)S(1)} %collective-permute-done.refs_1_.refs_2_, ...), custom_call_target="tpu_custom_call" | custom-call | tf_op jit(solution)/shard_map/pallas_call | solution.py:476
  22.2 1.6 %collective-permute-start.7 = (bf16[160,384]{1,0:T(8,128)(2,1)S(1)}, bf16[160,384]{1,0:T(8,128)(2,1)S(1)}, u32[]{:S(2)}, u32[]{:S(2)}) collective-permute-start(bf16[160,384]{1,0:T(8,128)(2,1)S(1)} %shard_map.72.refs_1_), channel_id=1, source_target_pairs={{0,16},{4,20},{8,24},{12,28},{16,0},{20,4},{24,8},{28,12},{1,17},{... | collective-permute-start | bytes 368648 | tf_op jit(solution)/shard_map/ppermute | solution.py:428
  23.8 2.0 %collective-permute-done.6.refs_2_.refs_0_ = bf16[128,512]{1,0:T(8,128)(2,1)S(1)} collective-permute-done((bf16[128,512]{1,0:T(8,128)(2,1)S(1)}, bf16[128,512]{1,0:T(8,128)(2,1)S(1)}, u32[]{:S(2)}, u32[]{:S(2)}) %collective-permute-start.6) | collective-permute-done | bytes 131104 | tf_op jit(solution)/shard_map/ppermute | solution.py:428
  25.9 0.7 %shard_map.74 = (bf16[128,512]{1,0:T(8,128)(2,1)S(1)}, bf16[128,512]{1,0:T(8,128)(2,1)S(1)}, bf16[128,512]{1,0:T(8,128)(2,1)S(1)}, bf16[128,512]{1,0:T(8,128)(2,1)S(1)}) custom-call(s32[4]{0:T(128)S(1)} %pad_add_fusion.place, bf16[128,512]{1,0:T(8,128)(2,1)S(1)} %collective-permute-done.6.refs_2_.refs_0_, ...), custom_call_target="tpu_custom_call" | custom-call | tf_op jit(solution)/shard_map/pallas_call | solution.py:504
  26.6 2.5 %collective-permute-start.14 = (bf16[128,512]{1,0:T(8,128)(2,1)S(1)}, bf16[128,512]{1,0:T(8,128)(2,1)S(1)}, u32[]{:S(2)}, u32[]{:S(2)}) collective-permute-start(bf16[128,512]{1,0:T(8,128)(2,1)S(1)} %get-tuple-element.54), channel_id=1, source_target_pairs={{0,4},{4,0},{8,12},{12,8},{16,20},{20,16},{24,28},{28,24},{1,5},{5... | collective-permute-start | bytes 393224 | tf_op jit(solution)/shard_map/ppermute | solution.py:428
  29.1 0.7 %collective-permute-start.15 = (bf16[128,512]{1,0:T(8,128)(2,1)S(1)}, bf16[128,512]{1,0:T(8,128)(2,1)S(1)}, u32[]{:S(2)}, u32[]{:S(2)}) collective-permute-start(bf16[128,512]{1,0:T(8,128)(2,1)S(1)} %get-tuple-element.55), channel_id=1, source_target_pairs={{0,8},{4,12},{8,0},{12,4},{16,24},{20,28},{24,16},{28,20},{1,9},{5... | collective-permute-start | bytes 393224 | tf_op jit(solution)/shard_map/ppermute | solution.py:428
  29.7 0.9 %collective-permute-start.16 = (bf16[128,512]{1,0:T(8,128)(2,1)S(1)}, bf16[128,512]{1,0:T(8,128)(2,1)S(1)}, u32[]{:S(2)}, u32[]{:S(2)}) collective-permute-start(bf16[128,512]{1,0:T(8,128)(2,1)S(1)} %get-tuple-element.56), channel_id=1, source_target_pairs={{0,12},{4,8},{8,4},{12,0},{16,28},{20,24},{24,20},{28,16},{1,13},{... | collective-permute-start | bytes 393224 | tf_op jit(solution)/shard_map/ppermute | solution.py:428
  30.6 0.0 collective-permute-done.7.refs_3_
  30.6 0.0 collective-permute-start.11
  30.6 0.0 collective-permute-done.12.refs_5_
  30.6 0.5 %collective-permute-start.13 = (bf16[896,128]{1,0:T(8,128)(2,1)S(1)}, bf16[896,128]{1,0:T(8,128)(2,1)S(1)}, u32[]{:S(2)}, u32[]{:S(2)}) collective-permute-start(bf16[896,128]{1,0:T(8,128)(2,1)S(1)} %collective-permute-done.12.refs_5_), channel_id=1, source_target_pairs={{0,1},{1,0},{2,3},{3,2},{4,5},{5,4},{6,7},{7,6},{8,9},{9,8},{10,11... | collective-permute-start | bytes 688136 | tf_op jit(solution)/shard_map/ppermute | solution.py:428
  31.1 0.9 %shard_map.73 = (bf16[160,384]{1,0:T(8,128)(2,1)S(1)}, bf16[160,384]{1,0:T(8,128)(2,1)S(1)}, bf16[160,384]{1,0:T(8,128)(2,1)S(1)}, bf16[160,384]{1,0:T(8,128)(2,1)S(1)}) custom-call(s32[4]{0:T(128)S(1)} %pad_add_fusion.place, bf16[128,512]{1,0:T(8,128)(2,1)S(1)} %shard_map.69.refs_0_, bf16[160,384]{1,0:T(8,128)(2,1)S(1)} %shard_map.72.refs_1_, ...), custom_call_target="tpu_custom_call" | custom-call | tf_op jit(solution)/shard_map/pallas_call | solution.py:504
  32.0 1.4 %collective-permute-done.14.refs_1_ = bf16[128,512]{1,0:T(8,128)(2,1)S(1)} collective-permute-done((bf16[128,512]{1,0:T(8,128)(2,1)S(1)}, bf16[128,512]{1,0:T(8,128)(2,1)S(1)}, u32[]{:S(2)}, u32[]{:S(2)}) %collective-permute-start.14) | collective-permute-done | bytes 131104 | tf_op jit(solution)/shard_map/ppermute | solution.py:428
  33.4 0.6 %collective-permute-start.9 = (bf16[160,384]{1,0:T(8,128)(2,1)S(1)}, bf16[160,384]{1,0:T(8,128)(2,1)S(1)}, u32[]{:S(2)}, u32[]{:S(2)}) collective-permute-start(bf16[160,384]{1,0:T(8,128)(2,1)S(1)} %get-tuple-element.50), channel_id=1, source_target_pairs={{0,4},{4,0},{8,12},{12,8},{16,20},{20,16},{24,28},{28,24},{1,5},{5... | collective-permute-start | bytes 368648 | tf_op jit(solution)/shard_map/ppermute | solution.py:428
  34.1 0.0 collective-permute-done.15.refs_2_
  34.1 0.7 %collective-permute-start.10 = (bf16[160,384]{1,0:T(8,128)(2,1)S(1)}, bf16[160,384]{1,0:T(8,128)(2,1)S(1)}, u32[]{:S(2)}, u32[]{:S(2)}) collective-permute-start(bf16[160,384]{1,0:T(8,128)(2,1)S(1)} %get-tuple-element.51), channel_id=1, source_target_pairs={{0,8},{4,12},{8,0},{12,4},{16,24},{20,28},{24,16},{28,20},{1,9},{5... | collective-permute-start | bytes 368648 | tf_op jit(solution)/shard_map/ppermute | solution.py:428
  34.7 1.0 %collective-permute-done.16.refs_3_ = bf16[128,512]{1,0:T(8,128)(2,1)S(1)} collective-permute-done((bf16[128,512]{1,0:T(8,128)(2,1)S(1)}, bf16[128,512]{1,0:T(8,128)(2,1)S(1)}, u32[]{:S(2)}, u32[]{:S(2)}) %collective-permute-start.16) | collective-permute-done | bytes 131104 | tf_op jit(solution)/shard_map/ppermute | solution.py:428
  35.7 1.4 %collective-permute-start.8 = (bf16[160,384]{1,0:T(8,128)(2,1)S(1)}, bf16[160,384]{1,0:T(8,128)(2,1)S(1)}, u32[]{:S(2)}, u32[]{:S(2)}) collective-permute-start(bf16[160,384]{1,0:T(8,128)(2,1)S(1)} %get-tuple-element.48), channel_id=1, source_target_pairs={{0,12},{4,8},{8,4},{12,0},{16,28},{20,24},{24,20},{28,16},{1,13},{... | collective-permute-start | bytes 368648 | tf_op jit(solution)/shard_map/ppermute | solution.py:428
  37.0 1.6 %shard_map.75.refs_7_ = bf16[128,3584]{1,0:T(8,128)(2,1)} custom-call(s32[4]{0:T(128)S(1)} %pad_add_fusion.place, bf16[128,256]{1,0:T(8,128)(2,1)S(1)} %get-tuple-element.32.kq, f32[128,3584]{1,0:T(8,128)S(1)} %get-tuple-element.41.local, f32[128,3584]{1,0:T(8,128)S(1)} %get-tuple-element.42.wide_growth, bf16[128,512]{1,0:T(8,128)(2,1)S(1)} %get-tuple-element.53.refs_0_, ...), custom_call_target="tpu_custom_call" | custom-call | tf_op jit(solution)/shard_map/pallas_call | solution.py:536
  38.6 0.0 collective-permute-done.11.refs_4_
  38.6 1.0 %collective-permute-done.9.refs_1_ = bf16[160,384]{1,0:T(8,128)(2,1)S(1)} collective-permute-done((bf16[160,384]{1,0:T(8,128)(2,1)S(1)}, bf16[160,384]{1,0:T(8,128)(2,1)S(1)}, u32[]{:S(2)}, u32[]{:S(2)}) %collective-permute-start.9) | collective-permute-done | bytes 122912 | tf_op jit(solution)/shard_map/ppermute | solution.py:428
  39.6 0.7 %collective-permute-done.10.refs_2_ = bf16[160,384]{1,0:T(8,128)(2,1)S(1)} collective-permute-done((bf16[160,384]{1,0:T(8,128)(2,1)S(1)}, bf16[160,384]{1,0:T(8,128)(2,1)S(1)}, u32[]{:S(2)}, u32[]{:S(2)}) %collective-permute-start.10) | collective-permute-done | bytes 122912 | tf_op jit(solution)/shard_map/ppermute | solution.py:428
  40.3 0.0 collective-permute-done.13.refs_6_
  40.3 1.5 %shard_map.76 = (bf16[128,3584]{1,0:T(8,128)(2,1)}, f32[4,8,896]{2,1,0:T(8,128)S(1)}, bf16[4,896,128]{2,1,0:T(8,128)(2,1)S(1)}) custom-call(s32[4]{0:T(128)S(1)} %pad_add_fusion.place, bf16[128,256]{1,0:T(8,128)(2,1)S(1)} %get-tuple-element.32.kq, f32[128,3584]{1,0:T(8,128)S(1)} %get-tuple-element.41.local, ...), custom_call_target="tpu_custom_call", output_to_operand_aliasing={{0}: (11, {})} | custom-call | tf_op jit(solution)/shard_map/pallas_call | solution.py:536
  41.8 0.0 collective-permute-done.8.refs_0_
  41.8 1.5 %shard_map.77 = (bf16[128,3584]{1,0:T(8,128)(2,1)}, f32[1,128]{1,0:T(1,128)}) custom-call(s32[4]{0:T(128)S(1)} %pad_add_fusion.place, bf16[128,256]{1,0:T(8,128)(2,1)S(1)} %get-tuple-element.32.kq, f32[128,3584]{1,0:T(8,128)S(1)} %get-tuple-element.41.local, f32[128,3584]{1,0:T(8,128)S(1)} %get-tuple-element.42.wide_growth, ...), custom_call_target="tpu_custom_call", output_to_operand_aliasing={{0}: (7, {})} | custom-call | tf_op jit(solution)/shard_map/pallas_call | solution.py:536
Async XLA Ops:
  0.6 12.5 %copy-start = (bf16[896,128]{1,0:T(8,128)(2,1)S(1)}, bf16[896,128]{1,0:T(8,128)(2,1)}, u32[]{:S(2)}) copy-start(bf16[896,128]{1,0:T(8,128)(2,1)} %refs_3_) | copy-start | bytes 688132
  0.6 18.2 %copy-start.1 = (f32[56]{0:T(128)S(1)}, f32[56]{0:T(128)}, u32[]{:S(2)}) copy-start(f32[56]{0:T(128)} %skip) | copy-start | bytes 676
  3.1 10.1 %collective-permute-start = (bf16[144,512]{1,0:T(8,128)(2,1)S(1)}, bf16[144,512]{1,0:T(8,128)(2,1)S(1)}, u32[]{:S(2)}, u32[]{:S(2)}) collective-permute-start(bf16[144,512]{1,0:T(8,128)(2,1)S(1)} %get-tuple-element.36), channel_id=1, source_target_pairs={{0,4},{4,0},{8,12},{12,8},{16,20},{20,16},{24,28},{28,24},{1,5},{5... | collective-permute-start | bytes 442376 | tf_op jit(solution)/shard_map/ppermute | solution.py:428
  6.1 7.0 %collective-permute-start.1 = (bf16[144,512]{1,0:T(8,128)(2,1)S(1)}, bf16[144,512]{1,0:T(8,128)(2,1)S(1)}, u32[]{:S(2)}, u32[]{:S(2)}) collective-permute-start(bf16[144,512]{1,0:T(8,128)(2,1)S(1)} %get-tuple-element.38), channel_id=1, source_target_pairs={{0,8},{4,12},{8,0},{12,4},{16,24},{20,28},{24,16},{28,20},{1,9},{5... | collective-permute-start | bytes 442376 | tf_op jit(solution)/shard_map/ppermute | solution.py:428
  7.7 7.7 %collective-permute-start.2 = (bf16[144,512]{1,0:T(8,128)(2,1)S(1)}, bf16[144,512]{1,0:T(8,128)(2,1)S(1)}, u32[]{:S(2)}, u32[]{:S(2)}) collective-permute-start(bf16[144,512]{1,0:T(8,128)(2,1)S(1)} %get-tuple-element.39), channel_id=1, source_target_pairs={{0,12},{4,8},{8,4},{12,0},{16,28},{20,24},{24,20},{28,16},{1,13},{... | collective-permute-start | bytes 442376 | tf_op jit(solution)/shard_map/ppermute | solution.py:428
  9.6 11.7 %collective-permute-start.3 = (bf16[144,384]{1,0:T(8,128)(2,1)S(1)}, bf16[144,384]{1,0:T(8,128)(2,1)S(1)}, u32[]{:S(2)}, u32[]{:S(2)}) collective-permute-start(bf16[144,384]{1,0:T(8,128)(2,1)S(1)} %get-tuple-element.45), channel_id=1, source_target_pairs={{0,4},{4,0},{8,12},{12,8},{16,20},{20,16},{24,28},{28,24},{1,5},{5... | collective-permute-start | bytes 331784 | tf_op jit(solution)/shard_map/ppermute | solution.py:428
  11.5 9.7 %collective-permute-start.4 = (bf16[144,384]{1,0:T(8,128)(2,1)S(1)}, bf16[144,384]{1,0:T(8,128)(2,1)S(1)}, u32[]{:S(2)}, u32[]{:S(2)}) collective-permute-start(bf16[144,384]{1,0:T(8,128)(2,1)S(1)} %get-tuple-element.46), channel_id=1, source_target_pairs={{0,8},{4,12},{8,0},{12,4},{16,24},{20,28},{24,16},{28,20},{1,9},{5... | collective-permute-start | bytes 331784 | tf_op jit(solution)/shard_map/ppermute | solution.py:428
  13.1 8.2 %collective-permute-start.5 = (bf16[144,384]{1,0:T(8,128)(2,1)S(1)}, bf16[144,384]{1,0:T(8,128)(2,1)S(1)}, u32[]{:S(2)}, u32[]{:S(2)}) collective-permute-start(bf16[144,384]{1,0:T(8,128)(2,1)S(1)} %get-tuple-element.47), channel_id=1, source_target_pairs={{0,12},{4,8},{8,4},{12,0},{16,28},{20,24},{24,20},{28,16},{1,13},{... | collective-permute-start | bytes 331784 | tf_op jit(solution)/shard_map/ppermute | solution.py:428
  13.1 17.5 %collective-permute-start.12 = (bf16[896,128]{1,0:T(8,128)(2,1)S(1)}, bf16[896,128]{1,0:T(8,128)(2,1)S(1)}, u32[]{:S(2)}, u32[]{:S(2)}) collective-permute-start(bf16[896,128]{1,0:T(8,128)(2,1)S(1)} %copy-done), channel_id=1, source_target_pairs={{0,2},{1,3},{2,0},{3,1},{4,6},{5,7},{6,4},{7,5},{8,10},{9,11},{10,... | collective-permute-start | bytes 688136 | tf_op jit(solution)/shard_map/ppermute | solution.py:428
  16.1 9.8 %collective-permute-start.6 = (bf16[128,512]{1,0:T(8,128)(2,1)S(1)}, bf16[128,512]{1,0:T(8,128)(2,1)S(1)}, u32[]{:S(2)}, u32[]{:S(2)}) collective-permute-start(bf16[128,512]{1,0:T(8,128)(2,1)S(1)} %shard_map.69.refs_0_), channel_id=1, source_target_pairs={{0,16},{4,20},{8,24},{12,28},{16,0},{20,4},{24,8},{28,12},{1,17},{... | collective-permute-start | bytes 393224 | tf_op jit(solution)/shard_map/ppermute | solution.py:428
  22.2 8.4 %collective-permute-start.7 = (bf16[160,384]{1,0:T(8,128)(2,1)S(1)}, bf16[160,384]{1,0:T(8,128)(2,1)S(1)}, u32[]{:S(2)}, u32[]{:S(2)}) collective-permute-start(bf16[160,384]{1,0:T(8,128)(2,1)S(1)} %shard_map.72.refs_1_), channel_id=1, source_target_pairs={{0,16},{4,20},{8,24},{12,28},{16,0},{20,4},{24,8},{28,12},{1,17},{... | collective-permute-start | bytes 368648 | tf_op jit(solution)/shard_map/ppermute | solution.py:428
  26.6 6.8 %collective-permute-start.14 = (bf16[128,512]{1,0:T(8,128)(2,1)S(1)}, bf16[128,512]{1,0:T(8,128)(2,1)S(1)}, u32[]{:S(2)}, u32[]{:S(2)}) collective-permute-start(bf16[128,512]{1,0:T(8,128)(2,1)S(1)} %get-tuple-element.54), channel_id=1, source_target_pairs={{0,4},{4,0},{8,12},{12,8},{16,20},{20,16},{24,28},{28,24},{1,5},{5... | collective-permute-start | bytes 393224 | tf_op jit(solution)/shard_map/ppermute | solution.py:428
  29.1 5.0 %collective-permute-start.15 = (bf16[128,512]{1,0:T(8,128)(2,1)S(1)}, bf16[128,512]{1,0:T(8,128)(2,1)S(1)}, u32[]{:S(2)}, u32[]{:S(2)}) collective-permute-start(bf16[128,512]{1,0:T(8,128)(2,1)S(1)} %get-tuple-element.55), channel_id=1, source_target_pairs={{0,8},{4,12},{8,0},{12,4},{16,24},{20,28},{24,16},{28,20},{1,9},{5... | collective-permute-start | bytes 393224 | tf_op jit(solution)/shard_map/ppermute | solution.py:428
  29.7 5.9 %collective-permute-start.16 = (bf16[128,512]{1,0:T(8,128)(2,1)S(1)}, bf16[128,512]{1,0:T(8,128)(2,1)S(1)}, u32[]{:S(2)}, u32[]{:S(2)}) collective-permute-start(bf16[128,512]{1,0:T(8,128)(2,1)S(1)} %get-tuple-element.56), channel_id=1, source_target_pairs={{0,12},{4,8},{8,4},{12,0},{16,28},{20,24},{24,20},{28,16},{1,13},{... | collective-permute-start | bytes 393224 | tf_op jit(solution)/shard_map/ppermute | solution.py:428
  30.6 8.0 %collective-permute-start.11 = (bf16[896,128]{1,0:T(8,128)(2,1)S(1)}, bf16[896,128]{1,0:T(8,128)(2,1)S(1)}, u32[]{:S(2)}, u32[]{:S(2)}) collective-permute-start(bf16[896,128]{1,0:T(8,128)(2,1)S(1)} %copy-done), channel_id=1, source_target_pairs={{0,1},{1,0},{2,3},{3,2},{4,5},{5,4},{6,7},{7,6},{8,9},{9,8},{10,11... | collective-permute-start | bytes 688136 | tf_op jit(solution)/shard_map/ppermute | solution.py:428
  30.6 9.6 %collective-permute-start.13 = (bf16[896,128]{1,0:T(8,128)(2,1)S(1)}, bf16[896,128]{1,0:T(8,128)(2,1)S(1)}, u32[]{:S(2)}, u32[]{:S(2)}) collective-permute-start(bf16[896,128]{1,0:T(8,128)(2,1)S(1)} %collective-permute-done.12.refs_5_), channel_id=1, source_target_pairs={{0,1},{1,0},{2,3},{3,2},{4,5},{5,4},{6,7},{7,6},{8,9},{9,8},{10,11... | collective-permute-start | bytes 688136 | tf_op jit(solution)/shard_map/ppermute | solution.py:428
  33.4 6.2 %collective-permute-start.9 = (bf16[160,384]{1,0:T(8,128)(2,1)S(1)}, bf16[160,384]{1,0:T(8,128)(2,1)S(1)}, u32[]{:S(2)}, u32[]{:S(2)}) collective-permute-start(bf16[160,384]{1,0:T(8,128)(2,1)S(1)} %get-tuple-element.50), channel_id=1, source_target_pairs={{0,4},{4,0},{8,12},{12,8},{16,20},{20,16},{24,28},{28,24},{1,5},{5... | collective-permute-start | bytes 368648 | tf_op jit(solution)/shard_map/ppermute | solution.py:428
  34.1 6.2 %collective-permute-start.10 = (bf16[160,384]{1,0:T(8,128)(2,1)S(1)}, bf16[160,384]{1,0:T(8,128)(2,1)S(1)}, u32[]{:S(2)}, u32[]{:S(2)}) collective-permute-start(bf16[160,384]{1,0:T(8,128)(2,1)S(1)} %get-tuple-element.51), channel_id=1, source_target_pairs={{0,8},{4,12},{8,0},{12,4},{16,24},{20,28},{24,16},{28,20},{1,9},{5... | collective-permute-start | bytes 368648 | tf_op jit(solution)/shard_map/ppermute | solution.py:428
  35.7 6.1 %collective-permute-start.8 = (bf16[160,384]{1,0:T(8,128)(2,1)S(1)}, bf16[160,384]{1,0:T(8,128)(2,1)S(1)}, u32[]{:S(2)}, u32[]{:S(2)}) collective-permute-start(bf16[160,384]{1,0:T(8,128)(2,1)S(1)} %get-tuple-element.48), channel_id=1, source_target_pairs={{0,12},{4,8},{8,4},{12,0},{16,28},{20,24},{24,20},{28,16},{1,13},{... | collective-permute-start | bytes 368648 | tf_op jit(solution)/shard_map/ppermute | solution.py:428

commit v7 on v5

--- a/solution.py
+++ b/solution.py
@@ -36,8 +36,10 @@
 
 
 def cumulative_by_position(log_decay):
-    upto = (iota((GROUP, GROUP), 1) <= iota((GROUP, GROUP), 0)).astype(F32)
-    return dot(upto, log_decay, ((1,), (1,)), HIGHEST)
+    upto = (iota((GROUP, GROUP), 1) <= iota((GROUP, GROUP), 0)).astype(BF16)
+    high = log_decay.astype(BF16)
+    middle, low = split(log_decay - high.astype(F32))
+    return sum(dot(upto, x, ((1,), (1,))) for x in (low, middle, high))
 
 
 def cumulative_by_head(log_decay):
@@ -524,7 +526,7 @@
         starts[-1] = [jnp.concatenate([x, below], axis=0) for x in starts[-1]]
     starts = [swap_all(x) for x in starts]
 
-    plan = [(tuple(range(group)), k, 0) for k in range(PIECES - 1)]
+    plan = [((0, 3, 1, 2), k, 0) for k in range(PIECES - 1)]
     plan += [(tuple(range(group - 1)), PIECES - 1, 1), ((group - 1,), PIECES - 1, 2)]
     mixed, rest = None, []
     for i, (ms, k, step) in enumerate(plan):

time: 42.7 us -> 42.7 us (level)
  starting transfers between devices: 21 us -> 22.1 us
  waiting for transfers between devices: 6.16 us -> 5.22 us
    ppermute x17, starting transfers between devices: 21 us -> 22.1 us  [swap(): lax.ppermute(x, axis, [(i, i ^ m) for i in range(lax.axis_size(axis))])]
    ppermute x17, waiting for transfers between devices: 6.16 us -> 5.22 us  [swap(): lax.ppermute(x, axis, [(i, i ^ m) for i in range(lax.axis_size(axis))])]
  transfers between devices with their start and end apart: 17 -> 17, of which waited for: 6 -> 5; matrix products, arithmetic and copies ran while one was open for 0% -> 0% of each run, Pallas kernels for 25% -> 25%
where the time goes in v7:
time: 42.7 us; the launch traced here: 42.6 us
  starting transfers between devices  22.1 us (52%)
  Pallas kernels  14.4 us (34%)
  waiting for transfers between devices  5.22 us (12%)
  between operations  0.8 us (2%)
    ppermute x17, starting transfers between devices, swap(): lax.ppermute(x, axis, [(i, i ^ m) for i in range(lax.axis_size(axis))])  22.1 us
    ppermute x17, waiting for transfers between devices, swap(): lax.ppermute(x, axis, [(i, i ^ m) for i in range(lax.axis_size(axis))])  5.22 us
    pallas_call x3, Pallas kernels, local(): call(functools.partial(output_kernel, ms, group, lanes, offsets[k], step,...  4.61 us
    pallas_call x1, Pallas kernels, local(): call(functools.partial(block_kernel, head_dim), [full, full, jax.ShapeDty...  2.42 us
    pallas_call x1, Pallas kernels, local(): call(functools.partial(first_kernel, head_dim, lanes), [piece(widths[0],...  2.25 us
    pallas_call x1, Pallas kernels, local(): call(functools.partial(last_kernel, head_dim, lanes), [piece(widths[1], s...  1.88 us
    pallas_call x2, Pallas kernels, local(): call(functools.partial(starts_kernel, head_dim, group, lanes), [piece(wid...  1.57 us
    pallas_call x1, Pallas kernels, local(): call(functools.partial(totals_kernel, head_dim, group, pair), [piece(widt...  0.97 us
  transfers between devices with their start and end apart: 17, of which 5 were waited for; matrix products, arithmetic and copies ran while one was open for 0% of the time, Pallas kernels for 25%

profile of v7, /device:TPU:0, one launch (start us, length us, event | category | flops | bytes accessed | tf_op | source)
XLA Modules:
  0.0 42.6 jit_solution(9924018341322450796)
XLA Ops:
  0.6 0.0 copy-start
  0.6 0.0 copy-start.1
  0.7 0.1 pad_add_fusion.place
  0.7 2.2 %shard_map.68 = (bf16[136,512]{1,0:T(8,128)(2,1)S(1)}, bf16[136,512]{1,0:T(8,128)(2,1)S(1)}, bf16[136,512]{1,0:T(8,128)(2,1)S(1)}, bf16[136,512]{1,0:T(8,128)(2,...) custom-call(s32[4]{0:T(128)S(1)} %pad_add_fusion.place, ...), custom_call_target="tpu_custom_call" | custom-call | flops 117440512 | bytes 1835008 | tf_op jit(solution)/shard_map/pallas_call | solution.py:438
  3.0 3.0 %collective-permute-start = (bf16[136,512]{1,0:T(8,128)(2,1)S(1)}, bf16[136,512]{1,0:T(8,128)(2,1)S(1)}, u32[]{:S(2)}, u32[]{:S(2)}) collective-permute-start(bf16[136,512]{1,0:T(8,128)(2,1)S(1)} %get-tuple-element.36), channel_id=1, source_target_pairs={{0,4},{4,0},{8,12},{12,8},{16,20},{20,16},{24,28},{28,24},{1,5},{5... | collective-permute-start | bytes 417800 | tf_op jit(solution)/shard_map/ppermute | solution.py:430
  6.0 1.6 %collective-permute-start.1 = (bf16[136,512]{1,0:T(8,128)(2,1)S(1)}, bf16[136,512]{1,0:T(8,128)(2,1)S(1)}, u32[]{:S(2)}, u32[]{:S(2)}) collective-permute-start(bf16[136,512]{1,0:T(8,128)(2,1)S(1)} %get-tuple-element.38), channel_id=1, source_target_pairs={{0,8},{4,12},{8,0},{12,4},{16,24},{20,28},{24,16},{28,20},{1,9},{5... | collective-permute-start | bytes 417800 | tf_op jit(solution)/shard_map/ppermute | solution.py:430
  7.6 0.0 collective-permute-start.2
  7.6 1.9 %shard_map.71 = (bf16[144,384]{1,0:T(8,128)(2,1)S(1)}, bf16[144,384]{1,0:T(8,128)(2,1)S(1)}, bf16[144,384]{1,0:T(8,128)(2,1)S(1)}, bf16[144,384]{1,0:T(8,128)(2,1)S(1)}) custom-call(s32[4]{0:T(128)S(1)} %pad_add_fusion.place, bf16[128,256]{1,0:T(8,128)(2,1)S(1)} %get-tuple-element.32.kq, bf16[128,3584]{1,0:T(8,128)(2,1)S(1)} %get-tuple-element.33.values, ...), custom_call_target="tpu_custom_call" | custom-call | tf_op jit(solution)/shard_map/pallas_call | solution.py:446
  9.5 2.0 %collective-permute-start.3 = (bf16[144,384]{1,0:T(8,128)(2,1)S(1)}, bf16[144,384]{1,0:T(8,128)(2,1)S(1)}, u32[]{:S(2)}, u32[]{:S(2)}) collective-permute-start(bf16[144,384]{1,0:T(8,128)(2,1)S(1)} %get-tuple-element.45), channel_id=1, source_target_pairs={{0,4},{4,0},{8,12},{12,8},{16,20},{20,16},{24,28},{28,24},{1,5},{5... | collective-permute-start | bytes 331784 | tf_op jit(solution)/shard_map/ppermute | solution.py:430
  11.5 1.6 %collective-permute-start.4 = (bf16[144,384]{1,0:T(8,128)(2,1)S(1)}, bf16[144,384]{1,0:T(8,128)(2,1)S(1)}, u32[]{:S(2)}, u32[]{:S(2)}) collective-permute-start(bf16[144,384]{1,0:T(8,128)(2,1)S(1)} %get-tuple-element.46), channel_id=1, source_target_pairs={{0,8},{4,12},{8,0},{12,4},{16,24},{20,28},{24,16},{28,20},{1,9},{5... | collective-permute-start | bytes 331784 | tf_op jit(solution)/shard_map/ppermute | solution.py:430
  13.0 0.0 collective-permute-done.refs_1_.refs_2_
  13.1 0.0 collective-permute-start.5
  13.1 0.0 collective-permute-done.1.refs_2_.refs_3_
  13.1 0.0 copy-done
  13.1 1.9 %collective-permute-start.12 = (bf16[896,128]{1,0:T(8,128)(2,1)S(1)}, bf16[896,128]{1,0:T(8,128)(2,1)S(1)}, u32[]{:S(2)}, u32[]{:S(2)}) collective-permute-start(bf16[896,128]{1,0:T(8,128)(2,1)S(1)} %copy-done), channel_id=1, source_target_pairs={{0,2},{1,3},{2,0},{3,1},{4,6},{5,7},{6,4},{7,5},{8,10},{9,11},{10,... | collective-permute-start | bytes 688136 | tf_op jit(solution)/shard_map/ppermute | solution.py:430
  14.9 0.2 collective-permute-done.2.refs_3_.refs_4_
  15.2 0.7 %shard_map.69.refs_0_ = bf16[128,512]{1,0:T(8,128)(2,1)S(1)} custom-call(s32[4]{0:T(128)S(1)} %pad_add_fusion.place, bf16[136,512]{1,0:T(8,128)(2,1)S(1)} %get-tuple-element.35.refs_0_.refs_1_, bf16[136,512]{1,0:T(8,128)(2,1)S(1)} %collective-permute-done.refs_1_.refs_2_, bf16[136,512]{1,0:T(8,128)(2,1)S(1)} %collective-permute-done.1.refs_2_.refs_3_, ...), custom_call_target="tpu_custom_call" | custom-call | tf_op jit(solution)/shard_map/pallas_call | solution.py:456
  15.8 2.7 %collective-permute-start.6 = (bf16[128,512]{1,0:T(8,128)(2,1)S(1)}, bf16[128,512]{1,0:T(8,128)(2,1)S(1)}, u32[]{:S(2)}, u32[]{:S(2)}) collective-permute-start(bf16[128,512]{1,0:T(8,128)(2,1)S(1)} %shard_map.69.refs_0_), channel_id=1, source_target_pairs={{0,16},{4,20},{8,24},{12,28},{16,0},{20,4},{24,8},{28,12},{1,17},{... | collective-permute-start | bytes 393224 | tf_op jit(solution)/shard_map/ppermute | solution.py:430
  18.5 0.0 copy-done.1
  18.5 2.4 %shard_map.70 = (f32[128,3584]{1,0:T(8,128)S(1)}, f32[128,3584]{1,0:T(8,128)S(1)}, f32[32,128]{1,0:T(8,128)S(1)}) custom-call(bf16[128,256]{1,0:T(8,128)(2,1)S(1)} %get-tuple-element.32.kq, bf16[128,3584]{1,0:T(8,128)(2,1)S(1)} %get-tuple-element.33.values, f32[56,128]{1,0:T(8,128)S(1)} %get-tuple-element.34.log_decay, f32[56]{0:T(128)S(1)} %copy-done.1), custom_call_target="tpu_custom_call" | custom-call | flops 469762048 | bytes 2752512 | tf_op jit(solution)/shard_map/pallas_call | solution.py:463
  20.9 0.0 collective-permute-done.3.refs_5_
  20.9 0.0 collective-permute-done.4.refs_6_
  20.9 0.0 collective-permute-done.5.refs_7_
  21.0 1.0 %shard_map.72.refs_1_ = bf16[160,384]{1,0:T(8,128)(2,1)S(1)} custom-call(s32[4]{0:T(128)S(1)} %pad_add_fusion.place, f32[32,128]{1,0:T(8,128)S(1)} %get-tuple-element.43.sums, bf16[136,512]{1,0:T(8,128)(2,1)S(1)} %get-tuple-element.35.refs_0_.refs_1_, bf16[136,512]{1,0:T(8,128)(2,1)S(1)} %collective-permute-done.refs_1_.refs_2_, ...), custom_call_target="tpu_custom_call" | custom-call | tf_op jit(solution)/shard_map/pallas_call | solution.py:478
  21.9 1.6 %collective-permute-start.7 = (bf16[160,384]{1,0:T(8,128)(2,1)S(1)}, bf16[160,384]{1,0:T(8,128)(2,1)S(1)}, u32[]{:S(2)}, u32[]{:S(2)}) collective-permute-start(bf16[160,384]{1,0:T(8,128)(2,1)S(1)} %shard_map.72.refs_1_), channel_id=1, source_target_pairs={{0,16},{4,20},{8,24},{12,28},{16,0},{20,4},{24,8},{28,12},{1,17},{... | collective-permute-start | bytes 368648 | tf_op jit(solution)/shard_map/ppermute | solution.py:430
  23.5 2.4 %collective-permute-done.6.refs_2_.refs_0_ = bf16[128,512]{1,0:T(8,128)(2,1)S(1)} collective-permute-done((bf16[128,512]{1,0:T(8,128)(2,1)S(1)}, bf16[128,512]{1,0:T(8,128)(2,1)S(1)}, u32[]{:S(2)}, u32[]{:S(2)}) %collective-permute-start.6) | collective-permute-done | bytes 131104 | tf_op jit(solution)/shard_map/ppermute | solution.py:430
  25.9 0.7 %shard_map.74 = (bf16[128,512]{1,0:T(8,128)(2,1)S(1)}, bf16[128,512]{1,0:T(8,128)(2,1)S(1)}, bf16[128,512]{1,0:T(8,128)(2,1)S(1)}, bf16[128,512]{1,0:T(8,128)(2,1)S(1)}) custom-call(s32[4]{0:T(128)S(1)} %pad_add_fusion.place, bf16[128,512]{1,0:T(8,128)(2,1)S(1)} %collective-permute-done.6.refs_2_.refs_0_, ...), custom_call_target="tpu_custom_call" | custom-call | tf_op jit(solution)/shard_map/pallas_call | solution.py:506
  26.6 1.8 %collective-permute-start.14 = (bf16[128,512]{1,0:T(8,128)(2,1)S(1)}, bf16[128,512]{1,0:T(8,128)(2,1)S(1)}, u32[]{:S(2)}, u32[]{:S(2)}) collective-permute-start(bf16[128,512]{1,0:T(8,128)(2,1)S(1)} %get-tuple-element.54), channel_id=1, source_target_pairs={{0,12},{4,8},{8,4},{12,0},{16,28},{20,24},{24,20},{28,16},{1,13},{... | collective-permute-start | bytes 393224 | tf_op jit(solution)/shard_map/ppermute | solution.py:430
  28.5 0.1 collective-permute-start.15
  28.5 1.7 %collective-permute-start.16 = (bf16[128,512]{1,0:T(8,128)(2,1)S(1)}, bf16[128,512]{1,0:T(8,128)(2,1)S(1)}, u32[]{:S(2)}, u32[]{:S(2)}) collective-permute-start(bf16[128,512]{1,0:T(8,128)(2,1)S(1)} %get-tuple-element.56), channel_id=1, source_target_pairs={{0,8},{4,12},{8,0},{12,4},{16,24},{20,28},{24,16},{28,20},{1,9},{5... | collective-permute-start | bytes 393224 | tf_op jit(solution)/shard_map/ppermute | solution.py:430
  30.2 0.0 collective-permute-done.7.refs_3_
  30.2 0.0 collective-permute-start.11
  30.2 0.0 collective-permute-done.12.refs_5_
  30.2 0.5 %collective-permute-start.13 = (bf16[896,128]{1,0:T(8,128)(2,1)S(1)}, bf16[896,128]{1,0:T(8,128)(2,1)S(1)}, u32[]{:S(2)}, u32[]{:S(2)}) collective-permute-start(bf16[896,128]{1,0:T(8,128)(2,1)S(1)} %collective-permute-done.12.refs_5_), channel_id=1, source_target_pairs={{0,1},{1,0},{2,3},{3,2},{4,5},{5,4},{6,7},{7,6},{8,9},{9,8},{10,11... | collective-permute-start | bytes 688136 | tf_op jit(solution)/shard_map/ppermute | solution.py:430
  30.7 0.9 %shard_map.73 = (bf16[152,384]{1,0:T(8,128)(2,1)S(1)}, bf16[152,384]{1,0:T(8,128)(2,1)S(1)}, bf16[152,384]{1,0:T(8,128)(2,1)S(1)}, bf16[152,384]{1,0:T(8,128)(2,1)S(1)}) custom-call(s32[4]{0:T(128)S(1)} %pad_add_fusion.place, bf16[128,512]{1,0:T(8,128)(2,1)S(1)} %shard_map.69.refs_0_, bf16[160,384]{1,0:T(8,128)(2,1)S(1)} %shard_map.72.refs_1_, ...), custom_call_target="tpu_custom_call" | custom-call | tf_op jit(solution)/shard_map/pallas_call | solution.py:506
  31.6 1.0 %collective-permute-done.14.refs_1_ = bf16[128,512]{1,0:T(8,128)(2,1)S(1)} collective-permute-done((bf16[128,512]{1,0:T(8,128)(2,1)S(1)}, bf16[128,512]{1,0:T(8,128)(2,1)S(1)}, u32[]{:S(2)}, u32[]{:S(2)}) %collective-permute-start.14) | collective-permute-done | bytes 131104 | tf_op jit(solution)/shard_map/ppermute | solution.py:430
  32.6 1.7 %collective-permute-start.9 = (bf16[152,384]{1,0:T(8,128)(2,1)S(1)}, bf16[152,384]{1,0:T(8,128)(2,1)S(1)}, u32[]{:S(2)}, u32[]{:S(2)}) collective-permute-start(bf16[152,384]{1,0:T(8,128)(2,1)S(1)} %get-tuple-element.50), channel_id=1, source_target_pairs={{0,4},{4,0},{8,12},{12,8},{16,20},{20,16},{24,28},{28,24},{1,5},{5... | collective-permute-start | bytes 350216 | tf_op jit(solution)/shard_map/ppermute | solution.py:430
  34.3 0.0 collective-permute-done.15.refs_2_
  34.3 0.7 %collective-permute-start.10 = (bf16[152,384]{1,0:T(8,128)(2,1)S(1)}, bf16[152,384]{1,0:T(8,128)(2,1)S(1)}, u32[]{:S(2)}, u32[]{:S(2)}) collective-permute-start(bf16[152,384]{1,0:T(8,128)(2,1)S(1)} %get-tuple-element.51), channel_id=1, source_target_pairs={{0,8},{4,12},{8,0},{12,4},{16,24},{20,28},{24,16},{28,20},{1,9},{5... | collective-permute-start | bytes 350216 | tf_op jit(solution)/shard_map/ppermute | solution.py:430
  35.0 0.0 collective-permute-done.16.refs_3_
  35.0 1.4 %collective-permute-start.8 = (bf16[152,384]{1,0:T(8,128)(2,1)S(1)}, bf16[152,384]{1,0:T(8,128)(2,1)S(1)}, u32[]{:S(2)}, u32[]{:S(2)}) collective-permute-start(bf16[152,384]{1,0:T(8,128)(2,1)S(1)} %get-tuple-element.48), channel_id=1, source_target_pairs={{0,12},{4,8},{8,4},{12,0},{16,28},{20,24},{24,20},{28,16},{1,13},{... | collective-permute-start | bytes 350216 | tf_op jit(solution)/shard_map/ppermute | solution.py:430
  36.4 1.6 %shard_map.75.refs_7_ = bf16[128,3584]{1,0:T(8,128)(2,1)} custom-call(s32[4]{0:T(128)S(1)} %pad_add_fusion.place, bf16[128,256]{1,0:T(8,128)(2,1)S(1)} %get-tuple-element.32.kq, f32[128,3584]{1,0:T(8,128)S(1)} %get-tuple-element.41.local, f32[128,3584]{1,0:T(8,128)S(1)} %get-tuple-element.42.wide_growth, bf16[128,512]{1,0:T(8,128)(2,1)S(1)} %get-tuple-element.53.refs_0_, ...), custom_call_target="tpu_custom_call" | custom-call | tf_op jit(solution)/shard_map/pallas_call | solution.py:538
  37.9 0.0 collective-permute-done.11.refs_4_
  37.9 0.8 %collective-permute-done.9.refs_1_ = bf16[152,384]{1,0:T(8,128)(2,1)S(1)} collective-permute-done((bf16[152,384]{1,0:T(8,128)(2,1)S(1)}, bf16[152,384]{1,0:T(8,128)(2,1)S(1)}, u32[]{:S(2)}, u32[]{:S(2)}) %collective-permute-start.9) | collective-permute-done | bytes 116768 | tf_op jit(solution)/shard_map/ppermute | solution.py:430
  38.7 0.8 %collective-permute-done.10.refs_2_ = bf16[152,384]{1,0:T(8,128)(2,1)S(1)} collective-permute-done((bf16[152,384]{1,0:T(8,128)(2,1)S(1)}, bf16[152,384]{1,0:T(8,128)(2,1)S(1)}, u32[]{:S(2)}, u32[]{:S(2)}) %collective-permute-start.10) | collective-permute-done | bytes 116768 | tf_op jit(solution)/shard_map/ppermute | solution.py:430
  39.5 0.0 collective-permute-done.13.refs_6_
  39.5 1.5 %shard_map.76 = (bf16[128,3584]{1,0:T(8,128)(2,1)}, f32[4,8,896]{2,1,0:T(8,128)S(1)}, bf16[4,896,128]{2,1,0:T(8,128)(2,1)S(1)}) custom-call(s32[4]{0:T(128)S(1)} %pad_add_fusion.place, bf16[128,256]{1,0:T(8,128)(2,1)S(1)} %get-tuple-element.32.kq, f32[128,3584]{1,0:T(8,128)S(1)} %get-tuple-element.41.local, ...), custom_call_target="tpu_custom_call", output_to_operand_aliasing={{0}: (11, {})} | custom-call | tf_op jit(solution)/shard_map/pallas_call | solution.py:538
  41.0 0.0 collective-permute-done.8.refs_0_
  41.0 1.5 %shard_map.77 = (bf16[128,3584]{1,0:T(8,128)(2,1)}, f32[1,128]{1,0:T(1,128)}) custom-call(s32[4]{0:T(128)S(1)} %pad_add_fusion.place, bf16[128,256]{1,0:T(8,128)(2,1)S(1)} %get-tuple-element.32.kq, f32[128,3584]{1,0:T(8,128)S(1)} %get-tuple-element.41.local, f32[128,3584]{1,0:T(8,128)S(1)} %get-tuple-element.42.wide_growth, ...), custom_call_target="tpu_custom_call", output_to_operand_aliasing={{0}: (7, {})} | custom-call | tf_op jit(solution)/shard_map/pallas_call | solution.py:538
Async XLA Ops:
  0.6 12.4 %copy-start = (bf16[896,128]{1,0:T(8,128)(2,1)S(1)}, bf16[896,128]{1,0:T(8,128)(2,1)}, u32[]{:S(2)}) copy-start(bf16[896,128]{1,0:T(8,128)(2,1)} %refs_3_) | copy-start | bytes 688132
  0.6 17.9 %copy-start.1 = (f32[56]{0:T(128)S(1)}, f32[56]{0:T(128)}, u32[]{:S(2)}) copy-start(f32[56]{0:T(128)} %skip) | copy-start | bytes 676
  3.0 10.0 %collective-permute-start = (bf16[136,512]{1,0:T(8,128)(2,1)S(1)}, bf16[136,512]{1,0:T(8,128)(2,1)S(1)}, u32[]{:S(2)}, u32[]{:S(2)}) collective-permute-start(bf16[136,512]{1,0:T(8,128)(2,1)S(1)} %get-tuple-element.36), channel_id=1, source_target_pairs={{0,4},{4,0},{8,12},{12,8},{16,20},{20,16},{24,28},{28,24},{1,5},{5... | collective-permute-start | bytes 417800 | tf_op jit(solution)/shard_map/ppermute | solution.py:430
  6.0 7.0 %collective-permute-start.1 = (bf16[136,512]{1,0:T(8,128)(2,1)S(1)}, bf16[136,512]{1,0:T(8,128)(2,1)S(1)}, u32[]{:S(2)}, u32[]{:S(2)}) collective-permute-start(bf16[136,512]{1,0:T(8,128)(2,1)S(1)} %get-tuple-element.38), channel_id=1, source_target_pairs={{0,8},{4,12},{8,0},{12,4},{16,24},{20,28},{24,16},{28,20},{1,9},{5... | collective-permute-start | bytes 417800 | tf_op jit(solution)/shard_map/ppermute | solution.py:430
  7.6 7.6 %collective-permute-start.2 = (bf16[136,512]{1,0:T(8,128)(2,1)S(1)}, bf16[136,512]{1,0:T(8,128)(2,1)S(1)}, u32[]{:S(2)}, u32[]{:S(2)}) collective-permute-start(bf16[136,512]{1,0:T(8,128)(2,1)S(1)} %get-tuple-element.39), channel_id=1, source_target_pairs={{0,12},{4,8},{8,4},{12,0},{16,28},{20,24},{24,20},{28,16},{1,13},{... | collective-permute-start | bytes 417800 | tf_op jit(solution)/shard_map/ppermute | solution.py:430
  9.5 11.4 %collective-permute-start.3 = (bf16[144,384]{1,0:T(8,128)(2,1)S(1)}, bf16[144,384]{1,0:T(8,128)(2,1)S(1)}, u32[]{:S(2)}, u32[]{:S(2)}) collective-permute-start(bf16[144,384]{1,0:T(8,128)(2,1)S(1)} %get-tuple-element.45), channel_id=1, source_target_pairs={{0,4},{4,0},{8,12},{12,8},{16,20},{20,16},{24,28},{28,24},{1,5},{5... | collective-permute-start | bytes 331784 | tf_op jit(solution)/shard_map/ppermute | solution.py:430
  11.5 9.5 %collective-permute-start.4 = (bf16[144,384]{1,0:T(8,128)(2,1)S(1)}, bf16[144,384]{1,0:T(8,128)(2,1)S(1)}, u32[]{:S(2)}, u32[]{:S(2)}) collective-permute-start(bf16[144,384]{1,0:T(8,128)(2,1)S(1)} %get-tuple-element.46), channel_id=1, source_target_pairs={{0,8},{4,12},{8,0},{12,4},{16,24},{20,28},{24,16},{28,20},{1,9},{5... | collective-permute-start | bytes 331784 | tf_op jit(solution)/shard_map/ppermute | solution.py:430
  13.1 7.9 %collective-permute-start.5 = (bf16[144,384]{1,0:T(8,128)(2,1)S(1)}, bf16[144,384]{1,0:T(8,128)(2,1)S(1)}, u32[]{:S(2)}, u32[]{:S(2)}) collective-permute-start(bf16[144,384]{1,0:T(8,128)(2,1)S(1)} %get-tuple-element.47), channel_id=1, source_target_pairs={{0,12},{4,8},{8,4},{12,0},{16,28},{20,24},{24,20},{28,16},{1,13},{... | collective-permute-start | bytes 331784 | tf_op jit(solution)/shard_map/ppermute | solution.py:430
  13.1 17.1 %collective-permute-start.12 = (bf16[896,128]{1,0:T(8,128)(2,1)S(1)}, bf16[896,128]{1,0:T(8,128)(2,1)S(1)}, u32[]{:S(2)}, u32[]{:S(2)}) collective-permute-start(bf16[896,128]{1,0:T(8,128)(2,1)S(1)} %copy-done), channel_id=1, source_target_pairs={{0,2},{1,3},{2,0},{3,1},{4,6},{5,7},{6,4},{7,5},{8,10},{9,11},{10,... | collective-permute-start | bytes 688136 | tf_op jit(solution)/shard_map/ppermute | solution.py:430
  15.8 10.1 %collective-permute-start.6 = (bf16[128,512]{1,0:T(8,128)(2,1)S(1)}, bf16[128,512]{1,0:T(8,128)(2,1)S(1)}, u32[]{:S(2)}, u32[]{:S(2)}) collective-permute-start(bf16[128,512]{1,0:T(8,128)(2,1)S(1)} %shard_map.69.refs_0_), channel_id=1, source_target_pairs={{0,16},{4,20},{8,24},{12,28},{16,0},{20,4},{24,8},{28,12},{1,17},{... | collective-permute-start | bytes 393224 | tf_op jit(solution)/shard_map/ppermute | solution.py:430
  21.9 8.3 %collective-permute-start.7 = (bf16[160,384]{1,0:T(8,128)(2,1)S(1)}, bf16[160,384]{1,0:T(8,128)(2,1)S(1)}, u32[]{:S(2)}, u32[]{:S(2)}) collective-permute-start(bf16[160,384]{1,0:T(8,128)(2,1)S(1)} %shard_map.72.refs_1_), channel_id=1, source_target_pairs={{0,16},{4,20},{8,24},{12,28},{16,0},{20,4},{24,8},{28,12},{1,17},{... | collective-permute-start | bytes 368648 | tf_op jit(solution)/shard_map/ppermute | solution.py:430
  26.6 6.0 %collective-permute-start.14 = (bf16[128,512]{1,0:T(8,128)(2,1)S(1)}, bf16[128,512]{1,0:T(8,128)(2,1)S(1)}, u32[]{:S(2)}, u32[]{:S(2)}) collective-permute-start(bf16[128,512]{1,0:T(8,128)(2,1)S(1)} %get-tuple-element.54), channel_id=1, source_target_pairs={{0,12},{4,8},{8,4},{12,0},{16,28},{20,24},{24,20},{28,16},{1,13},{... | collective-permute-start | bytes 393224 | tf_op jit(solution)/shard_map/ppermute | solution.py:430
  28.5 5.8 %collective-permute-start.15 = (bf16[128,512]{1,0:T(8,128)(2,1)S(1)}, bf16[128,512]{1,0:T(8,128)(2,1)S(1)}, u32[]{:S(2)}, u32[]{:S(2)}) collective-permute-start(bf16[128,512]{1,0:T(8,128)(2,1)S(1)} %get-tuple-element.55), channel_id=1, source_target_pairs={{0,4},{4,0},{8,12},{12,8},{16,20},{20,16},{24,28},{28,24},{1,5},{5... | collective-permute-start | bytes 393224 | tf_op jit(solution)/shard_map/ppermute | solution.py:430
  28.5 6.5 %collective-permute-start.16 = (bf16[128,512]{1,0:T(8,128)(2,1)S(1)}, bf16[128,512]{1,0:T(8,128)(2,1)S(1)}, u32[]{:S(2)}, u32[]{:S(2)}) collective-permute-start(bf16[128,512]{1,0:T(8,128)(2,1)S(1)} %get-tuple-element.56), channel_id=1, source_target_pairs={{0,8},{4,12},{8,0},{12,4},{16,24},{20,28},{24,16},{28,20},{1,9},{5... | collective-permute-start | bytes 393224 | tf_op jit(solution)/shard_map/ppermute | solution.py:430
  30.2 7.7 %collective-permute-start.11 = (bf16[896,128]{1,0:T(8,128)(2,1)S(1)}, bf16[896,128]{1,0:T(8,128)(2,1)S(1)}, u32[]{:S(2)}, u32[]{:S(2)}) collective-permute-start(bf16[896,128]{1,0:T(8,128)(2,1)S(1)} %copy-done), channel_id=1, source_target_pairs={{0,1},{1,0},{2,3},{3,2},{4,5},{5,4},{6,7},{7,6},{8,9},{9,8},{10,11... | collective-permute-start | bytes 688136 | tf_op jit(solution)/shard_map/ppermute | solution.py:430
  30.2 9.3 %collective-permute-start.13 = (bf16[896,128]{1,0:T(8,128)(2,1)S(1)}, bf16[896,128]{1,0:T(8,128)(2,1)S(1)}, u32[]{:S(2)}, u32[]{:S(2)}) collective-permute-start(bf16[896,128]{1,0:T(8,128)(2,1)S(1)} %collective-permute-done.12.refs_5_), channel_id=1, source_target_pairs={{0,1},{1,0},{2,3},{3,2},{4,5},{5,4},{6,7},{7,6},{8,9},{9,8},{10,11... | collective-permute-start | bytes 688136 | tf_op jit(solution)/shard_map/ppermute | solution.py:430
  32.6 6.1 %collective-permute-start.9 = (bf16[152,384]{1,0:T(8,128)(2,1)S(1)}, bf16[152,384]{1,0:T(8,128)(2,1)S(1)}, u32[]{:S(2)}, u32[]{:S(2)}) collective-permute-start(bf16[152,384]{1,0:T(8,128)(2,1)S(1)} %get-tuple-element.50), channel_id=1, source_target_pairs={{0,4},{4,0},{8,12},{12,8},{16,20},{20,16},{24,28},{28,24},{1,5},{5... | collective-permute-start | bytes 350216 | tf_op jit(solution)/shard_map/ppermute | solution.py:430
  34.3 5.2 %collective-permute-start.10 = (bf16[152,384]{1,0:T(8,128)(2,1)S(1)}, bf16[152,384]{1,0:T(8,128)(2,1)S(1)}, u32[]{:S(2)}, u32[]{:S(2)}) collective-permute-start(bf16[152,384]{1,0:T(8,128)(2,1)S(1)} %get-tuple-element.51), channel_id=1, source_target_pairs={{0,8},{4,12},{8,0},{12,4},{16,24},{20,28},{24,16},{28,20},{1,9},{5... | collective-permute-start | bytes 350216 | tf_op jit(solution)/shard_map/ppermute | solution.py:430
  35.0 6.0 %collective-permute-start.8 = (bf16[152,384]{1,0:T(8,128)(2,1)S(1)}, bf16[152,384]{1,0:T(8,128)(2,1)S(1)}, u32[]{:S(2)}, u32[]{:S(2)}) collective-permute-start(bf16[152,384]{1,0:T(8,128)(2,1)S(1)} %get-tuple-element.48), channel_id=1, source_target_pairs={{0,12},{4,8},{8,4},{12,0},{16,28},{20,24},{24,20},{28,16},{1,13},{... | collective-permute-start | bytes 350216 | tf_op jit(solution)/shard_map/ppermute | solution.py:430

commit v8 on v7

--- a/solution.py
+++ b/solution.py
@@ -497,7 +497,6 @@
                 reach *= 2
             before.append(running.astype(BF16))
 
-    weights = [classifier, swap(classifier, 1, "fsdp"), crossed, swap(crossed, 1, "fsdp")]
     starts = []
     for k, width in enumerate(widths):
         last = k == PIECES - 1
@@ -509,6 +508,9 @@
                 [SMEM] + [VMEM] * (len(operands) + group),
             )(place, *operands, *parts[k])
         )
+        if k == 0:
+            classifier, crossed = lax.optimization_barrier((classifier, crossed, starts))[:2]
+            weights = [classifier, swap(classifier, 1, "fsdp"), crossed, swap(crossed, 1, "fsdp")]
     if not pair:
         whole = call(
             functools.partial(sums_kernel, head_dim, group), row, [VMEM] * (2 * PIECES * group)

time: 42.7 us -> 42.7 us (level)
  starting transfers between devices: 22.1 us -> 21 us
  waiting for transfers between devices: 5.22 us -> 6.23 us
    ppermute x17, starting transfers between devices: 22.1 us -> 21 us  [swap(): lax.ppermute(x, axis, [(i, i ^ m) for i in range(lax.axis_size(axis))])]
    ppermute x17, waiting for transfers between devices: 5.22 us -> 6.23 us  [swap(): lax.ppermute(x, axis, [(i, i ^ m) for i in range(lax.axis_size(axis))])]
  transfers between devices with their start and end apart: 17 -> 17, of which waited for: 5 -> 6; matrix products, arithmetic and copies ran while one was open for 0% -> 0% of each run, Pallas kernels for 25% -> 25%
where the time goes in v8:
time: 42.7 us; the launch traced here: 42.5 us
  starting transfers between devices  21 us (49%)
  Pallas kernels  14.4 us (34%)
  waiting for transfers between devices  6.23 us (15%)
  between operations  0.79 us (2%)
    ppermute x17, starting transfers between devices, swap(): lax.ppermute(x, axis, [(i, i ^ m) for i in range(lax.axis_size(axis))])  21 us
    ppermute x17, waiting for transfers between devices, swap(): lax.ppermute(x, axis, [(i, i ^ m) for i in range(lax.axis_size(axis))])  6.23 us
    pallas_call x3, Pallas kernels, local(): call(functools.partial(output_kernel, ms, group, lanes, offsets[k], step,...  4.6 us
    pallas_call x1, Pallas kernels, local(): call(functools.partial(block_kernel, head_dim), [full, full, jax.ShapeDty...  2.42 us
    pallas_call x1, Pallas kernels, local(): call(functools.partial(first_kernel, head_dim, lanes), [piece(widths[0],...  2.25 us
    pallas_call x1, Pallas kernels, local(): call(functools.partial(last_kernel, head_dim, lanes), [piece(widths[1], s...  1.88 us
    pallas_call x2, Pallas kernels, local(): call(functools.partial(starts_kernel, head_dim, group, lanes), [piece(wid...  1.57 us
    pallas_call x1, Pallas kernels, local(): call(functools.partial(totals_kernel, head_dim, group, pair), [piece(widt...  0.97 us
  transfers between devices with their start and end apart: 17, of which 6 were waited for; matrix products, arithmetic and copies ran while one was open for 0% of the time, Pallas kernels for 25%

profile of v8, /device:TPU:0, one launch (start us, length us, event | category | flops | bytes accessed | tf_op | source)
XLA Modules:
  0.0 42.5 jit_solution(3987411068206386309)
XLA Ops:
  0.6 0.0 copy-start
  0.6 0.0 copy-start.1
  0.7 0.1 pad_add_fusion.place
  0.7 2.2 %shard_map.68 = (bf16[136,512]{1,0:T(8,128)(2,1)S(1)}, bf16[136,512]{1,0:T(8,128)(2,1)S(1)}, bf16[136,512]{1,0:T(8,128)(2,1)S(1)}, bf16[136,512]{1,0:T(8,128)(2,...) custom-call(s32[4]{0:T(128)S(1)} %pad_add_fusion.place, ...), custom_call_target="tpu_custom_call" | custom-call | flops 117440512 | bytes 1835008 | tf_op jit(solution)/shard_map/pallas_call | solution.py:438
  3.0 3.0 %collective-permute-start = (bf16[136,512]{1,0:T(8,128)(2,1)S(1)}, bf16[136,512]{1,0:T(8,128)(2,1)S(1)}, u32[]{:S(2)}, u32[]{:S(2)}) collective-permute-start(bf16[136,512]{1,0:T(8,128)(2,1)S(1)} %get-tuple-element.38), channel_id=1, source_target_pairs={{0,4},{4,0},{8,12},{12,8},{16,20},{20,16},{24,28},{28,24},{1,5},{5... | collective-permute-start | bytes 417800 | tf_op jit(solution)/shard_map/ppermute | solution.py:430
  6.0 1.6 %collective-permute-start.1 = (bf16[136,512]{1,0:T(8,128)(2,1)S(1)}, bf16[136,512]{1,0:T(8,128)(2,1)S(1)}, u32[]{:S(2)}, u32[]{:S(2)}) collective-permute-start(bf16[136,512]{1,0:T(8,128)(2,1)S(1)} %get-tuple-element.40), channel_id=1, source_target_pairs={{0,8},{4,12},{8,0},{12,4},{16,24},{20,28},{24,16},{28,20},{1,9},{5... | collective-permute-start | bytes 417800 | tf_op jit(solution)/shard_map/ppermute | solution.py:430
  7.6 0.0 collective-permute-start.2
  7.6 1.9 %shard_map.71 = (bf16[144,384]{1,0:T(8,128)(2,1)S(1)}, bf16[144,384]{1,0:T(8,128)(2,1)S(1)}, bf16[144,384]{1,0:T(8,128)(2,1)S(1)}, bf16[144,384]{1,0:T(8,128)(2,1)S(1)}) custom-call(s32[4]{0:T(128)S(1)} %pad_add_fusion.place, bf16[128,256]{1,0:T(8,128)(2,1)S(1)} %get-tuple-element.34.kq, bf16[128,3584]{1,0:T(8,128)(2,1)S(1)} %get-tuple-element.35.values, ...), custom_call_target="tpu_custom_call" | custom-call | tf_op jit(solution)/shard_map/pallas_call | solution.py:446
  9.5 2.0 %collective-permute-start.3 = (bf16[144,384]{1,0:T(8,128)(2,1)S(1)}, bf16[144,384]{1,0:T(8,128)(2,1)S(1)}, u32[]{:S(2)}, u32[]{:S(2)}) collective-permute-start(bf16[144,384]{1,0:T(8,128)(2,1)S(1)} %get-tuple-element.47), channel_id=1, source_target_pairs={{0,4},{4,0},{8,12},{12,8},{16,20},{20,16},{24,28},{28,24},{1,5},{5... | collective-permute-start | bytes 331784 | tf_op jit(solution)/shard_map/ppermute | solution.py:430
  11.5 1.6 %collective-permute-start.4 = (bf16[144,384]{1,0:T(8,128)(2,1)S(1)}, bf16[144,384]{1,0:T(8,128)(2,1)S(1)}, u32[]{:S(2)}, u32[]{:S(2)}) collective-permute-start(bf16[144,384]{1,0:T(8,128)(2,1)S(1)} %get-tuple-element.48), channel_id=1, source_target_pairs={{0,8},{4,12},{8,0},{12,4},{16,24},{20,28},{24,16},{28,20},{1,9},{5... | collective-permute-start | bytes 331784 | tf_op jit(solution)/shard_map/ppermute | solution.py:430
  13.0 0.0 collective-permute-done.refs_1_.refs_2_
  13.1 0.0 collective-permute-start.5
  13.1 0.0 collective-permute-done.1.refs_2_.refs_3_
  13.1 0.0 copy-done
  13.1 1.9 %collective-permute-start.11 = (bf16[896,128]{1,0:T(8,128)(2,1)S(1)}, bf16[896,128]{1,0:T(8,128)(2,1)S(1)}, u32[]{:S(2)}, u32[]{:S(2)}) collective-permute-start(bf16[896,128]{1,0:T(8,128)(2,1)S(1)} %copy-done), channel_id=1, source_target_pairs={{0,2},{1,3},{2,0},{3,1},{4,6},{5,7},{6,4},{7,5},{8,10},{9,11},{10,... | collective-permute-start | bytes 688136 | tf_op jit(solution)/shard_map/ppermute | solution.py:430
  14.9 0.2 collective-permute-done.2.refs_3_.refs_4_
  15.2 0.7 %shard_map.69.refs_0_ = bf16[128,512]{1,0:T(8,128)(2,1)S(1)} custom-call(s32[4]{0:T(128)S(1)} %pad_add_fusion.place, bf16[136,512]{1,0:T(8,128)(2,1)S(1)} %get-tuple-element.37.refs_0_.refs_1_, bf16[136,512]{1,0:T(8,128)(2,1)S(1)} %collective-permute-done.refs_1_.refs_2_, bf16[136,512]{1,0:T(8,128)(2,1)S(1)} %collective-permute-done.1.refs_2_.refs_3_, ...), custom_call_target="tpu_custom_call" | custom-call | tf_op jit(solution)/shard_map/pallas_call | solution.py:456
  15.8 2.7 %collective-permute-start.6 = (bf16[128,512]{1,0:T(8,128)(2,1)S(1)}, bf16[128,512]{1,0:T(8,128)(2,1)S(1)}, u32[]{:S(2)}, u32[]{:S(2)}) collective-permute-start(bf16[128,512]{1,0:T(8,128)(2,1)S(1)} %shard_map.69.refs_0_), channel_id=1, source_target_pairs={{0,16},{4,20},{8,24},{12,28},{16,0},{20,4},{24,8},{28,12},{1,17},{... | collective-permute-start | bytes 393224 | tf_op jit(solution)/shard_map/ppermute | solution.py:430
  18.5 0.0 copy-done.1
  18.5 2.4 %shard_map.70 = (f32[128,3584]{1,0:T(8,128)S(1)}, f32[128,3584]{1,0:T(8,128)S(1)}, f32[32,128]{1,0:T(8,128)S(1)}) custom-call(bf16[128,256]{1,0:T(8,128)(2,1)S(1)} %get-tuple-element.34.kq, bf16[128,3584]{1,0:T(8,128)(2,1)S(1)} %get-tuple-element.35.values, f32[56,128]{1,0:T(8,128)S(1)} %get-tuple-element.36.log_decay, f32[56]{0:T(128)S(1)} %copy-done.1), custom_call_target="tpu_custom_call" | custom-call | flops 469762048 | bytes 2752512 | tf_op jit(solution)/shard_map/pallas_call | solution.py:463
  20.9 0.0 collective-permute-done.3.refs_5_
  20.9 0.0 collective-permute-done.4.refs_6_
  20.9 0.0 collective-permute-done.5.refs_7_
  21.0 1.0 %shard_map.72.refs_1_ = bf16[160,384]{1,0:T(8,128)(2,1)S(1)} custom-call(s32[4]{0:T(128)S(1)} %pad_add_fusion.place, f32[32,128]{1,0:T(8,128)S(1)} %get-tuple-element.45.sums, bf16[136,512]{1,0:T(8,128)(2,1)S(1)} %get-tuple-element.37.refs_0_.refs_1_, bf16[136,512]{1,0:T(8,128)(2,1)S(1)} %collective-permute-done.refs_1_.refs_2_, ...), custom_call_target="tpu_custom_call" | custom-call | tf_op jit(solution)/shard_map/pallas_call | solution.py:478
  21.9 1.6 %collective-permute-start.7 = (bf16[160,384]{1,0:T(8,128)(2,1)S(1)}, bf16[160,384]{1,0:T(8,128)(2,1)S(1)}, u32[]{:S(2)}, u32[]{:S(2)}) collective-permute-start(bf16[160,384]{1,0:T(8,128)(2,1)S(1)} %shard_map.72.refs_1_), channel_id=1, source_target_pairs={{0,16},{4,20},{8,24},{12,28},{16,0},{20,4},{24,8},{28,12},{1,17},{... | collective-permute-start | bytes 368648 | tf_op jit(solution)/shard_map/ppermute | solution.py:430
  23.5 2.3 %collective-permute-done.6.refs_2_.refs_0_ = bf16[128,512]{1,0:T(8,128)(2,1)S(1)} collective-permute-done((bf16[128,512]{1,0:T(8,128)(2,1)S(1)}, bf16[128,512]{1,0:T(8,128)(2,1)S(1)}, u32[]{:S(2)}, u32[]{:S(2)}) %collective-permute-start.6) | collective-permute-done | bytes 131104 | tf_op jit(solution)/shard_map/ppermute | solution.py:430
  25.8 0.7 %shard_map.74 = (bf16[128,512]{1,0:T(8,128)(2,1)S(1)}, bf16[128,512]{1,0:T(8,128)(2,1)S(1)}, bf16[128,512]{1,0:T(8,128)(2,1)S(1)}, bf16[128,512]{1,0:T(8,128)(2,1)S(1)}) custom-call(s32[4]{0:T(128)S(1)} %pad_add_fusion.place, bf16[128,512]{1,0:T(8,128)(2,1)S(1)} %collective-permute-done.6.refs_2_.refs_0_, ...), custom_call_target="tpu_custom_call" | custom-call | tf_op jit(solution)/shard_map/pallas_call | solution.py:505
  26.5 1.8 %collective-permute-start.15 = (bf16[128,512]{1,0:T(8,128)(2,1)S(1)}, bf16[128,512]{1,0:T(8,128)(2,1)S(1)}, u32[]{:S(2)}, u32[]{:S(2)}) collective-permute-start(bf16[128,512]{1,0:T(8,128)(2,1)S(1)} %get-tuple-element.56), channel_id=1, source_target_pairs={{0,4},{4,0},{8,12},{12,8},{16,20},{20,16},{24,28},{28,24},{1,5},{5... | collective-permute-start | bytes 393224 | tf_op jit(solution)/shard_map/ppermute | solution.py:430
  28.3 0.7 %collective-permute-start.16 = (bf16[128,512]{1,0:T(8,128)(2,1)S(1)}, bf16[128,512]{1,0:T(8,128)(2,1)S(1)}, u32[]{:S(2)}, u32[]{:S(2)}) collective-permute-start(bf16[128,512]{1,0:T(8,128)(2,1)S(1)} %get-tuple-element.57), channel_id=1, source_target_pairs={{0,8},{4,12},{8,0},{12,4},{16,24},{20,28},{24,16},{28,20},{1,9},{5... | collective-permute-start | bytes 393224 | tf_op jit(solution)/shard_map/ppermute | solution.py:430
  29.1 1.0 %collective-permute-start.14 = (bf16[128,512]{1,0:T(8,128)(2,1)S(1)}, bf16[128,512]{1,0:T(8,128)(2,1)S(1)}, u32[]{:S(2)}, u32[]{:S(2)}) collective-permute-start(bf16[128,512]{1,0:T(8,128)(2,1)S(1)} %get-tuple-element.58), channel_id=1, source_target_pairs={{0,12},{4,8},{8,4},{12,0},{16,28},{20,24},{24,20},{28,16},{1,13},{... | collective-permute-start | bytes 393224 | tf_op jit(solution)/shard_map/ppermute | solution.py:430
  30.1 0.0 collective-permute-done.11.refs_5_
  30.1 0.0 collective-permute-start.12
  30.1 0.0 collective-permute-done.7.refs_3_
  30.1 0.5 %collective-permute-start.13 = (bf16[896,128]{1,0:T(8,128)(2,1)S(1)}, bf16[896,128]{1,0:T(8,128)(2,1)S(1)}, u32[]{:S(2)}, u32[]{:S(2)}) collective-permute-start(bf16[896,128]{1,0:T(8,128)(2,1)S(1)} %collective-permute-done.11.refs_5_), channel_id=1, source_target_pairs={{0,1},{1,0},{2,3},{3,2},{4,5},{5,4},{6,7},{7,6},{8,9},{9,8},{10,11... | collective-permute-start | bytes 688136 | tf_op jit(solution)/shard_map/ppermute | solution.py:430
  30.6 0.9 %shard_map.73 = (bf16[152,384]{1,0:T(8,128)(2,1)S(1)}, bf16[152,384]{1,0:T(8,128)(2,1)S(1)}, bf16[152,384]{1,0:T(8,128)(2,1)S(1)}, bf16[152,384]{1,0:T(8,128)(2,1)S(1)}) custom-call(s32[4]{0:T(128)S(1)} %pad_add_fusion.place, bf16[128,512]{1,0:T(8,128)(2,1)S(1)} %shard_map.69.refs_0_, bf16[160,384]{1,0:T(8,128)(2,1)S(1)} %shard_map.72.refs_1_, ...), custom_call_target="tpu_custom_call" | custom-call | tf_op jit(solution)/shard_map/pallas_call | solution.py:505
  31.5 1.3 %collective-permute-done.15.refs_2_ = bf16[128,512]{1,0:T(8,128)(2,1)S(1)} collective-permute-done((bf16[128,512]{1,0:T(8,128)(2,1)S(1)}, bf16[128,512]{1,0:T(8,128)(2,1)S(1)}, u32[]{:S(2)}, u32[]{:S(2)}) %collective-permute-start.15) | collective-permute-done | bytes 131104 | tf_op jit(solution)/shard_map/ppermute | solution.py:430
  32.8 1.1 %collective-permute-start.9 = (bf16[152,384]{1,0:T(8,128)(2,1)S(1)}, bf16[152,384]{1,0:T(8,128)(2,1)S(1)}, u32[]{:S(2)}, u32[]{:S(2)}) collective-permute-start(bf16[152,384]{1,0:T(8,128)(2,1)S(1)} %get-tuple-element.52), channel_id=1, source_target_pairs={{0,4},{4,0},{8,12},{12,8},{16,20},{20,16},{24,28},{28,24},{1,5},{5... | collective-permute-start | bytes 350216 | tf_op jit(solution)/shard_map/ppermute | solution.py:430
  33.8 0.0 collective-permute-done.16.refs_3_
  33.8 0.3 collective-permute-start.10
  34.1 0.9 %collective-permute-done.14.refs_1_ = bf16[128,512]{1,0:T(8,128)(2,1)S(1)} collective-permute-done((bf16[128,512]{1,0:T(8,128)(2,1)S(1)}, bf16[128,512]{1,0:T(8,128)(2,1)S(1)}, u32[]{:S(2)}, u32[]{:S(2)}) %collective-permute-start.14) | collective-permute-done | bytes 131104 | tf_op jit(solution)/shard_map/ppermute | solution.py:430
  35.0 1.3 %collective-permute-start.8 = (bf16[152,384]{1,0:T(8,128)(2,1)S(1)}, bf16[152,384]{1,0:T(8,128)(2,1)S(1)}, u32[]{:S(2)}, u32[]{:S(2)}) collective-permute-start(bf16[152,384]{1,0:T(8,128)(2,1)S(1)} %get-tuple-element.50), channel_id=1, source_target_pairs={{0,12},{4,8},{8,4},{12,0},{16,28},{20,24},{24,20},{28,16},{1,13},{... | collective-permute-start | bytes 350216 | tf_op jit(solution)/shard_map/ppermute | solution.py:430
  36.3 1.5 %shard_map.75.refs_7_ = bf16[128,3584]{1,0:T(8,128)(2,1)} custom-call(s32[4]{0:T(128)S(1)} %pad_add_fusion.place, bf16[128,256]{1,0:T(8,128)(2,1)S(1)} %get-tuple-element.34.kq, f32[128,3584]{1,0:T(8,128)S(1)} %get-tuple-element.43.local, f32[128,3584]{1,0:T(8,128)S(1)} %get-tuple-element.44.wide_growth, bf16[128,512]{1,0:T(8,128)(2,1)S(1)} %get-tuple-element.55.refs_0_, ...), custom_call_target="tpu_custom_call" | custom-call | tf_op jit(solution)/shard_map/pallas_call | solution.py:540
  37.9 0.9 %collective-permute-done.9.refs_1_ = bf16[152,384]{1,0:T(8,128)(2,1)S(1)} collective-permute-done((bf16[152,384]{1,0:T(8,128)(2,1)S(1)}, bf16[152,384]{1,0:T(8,128)(2,1)S(1)}, u32[]{:S(2)}, u32[]{:S(2)}) %collective-permute-start.9) | collective-permute-done | bytes 116768 | tf_op jit(solution)/shard_map/ppermute | solution.py:430
  38.8 0.6 %collective-permute-done.10.refs_2_ = bf16[152,384]{1,0:T(8,128)(2,1)S(1)} collective-permute-done((bf16[152,384]{1,0:T(8,128)(2,1)S(1)}, bf16[152,384]{1,0:T(8,128)(2,1)S(1)}, u32[]{:S(2)}, u32[]{:S(2)}) %collective-permute-start.10) | collective-permute-done | bytes 116768 | tf_op jit(solution)/shard_map/ppermute | solution.py:430
  39.4 0.0 collective-permute-done.12.refs_4_
  39.4 0.0 collective-permute-done.13.refs_6_
  39.4 1.5 %shard_map.76 = (bf16[128,3584]{1,0:T(8,128)(2,1)}, f32[4,8,896]{2,1,0:T(8,128)S(1)}, bf16[4,896,128]{2,1,0:T(8,128)(2,1)S(1)}) custom-call(s32[4]{0:T(128)S(1)} %pad_add_fusion.place, bf16[128,256]{1,0:T(8,128)(2,1)S(1)} %get-tuple-element.34.kq, f32[128,3584]{1,0:T(8,128)S(1)} %get-tuple-element.43.local, ...), custom_call_target="tpu_custom_call", output_to_operand_aliasing={{0}: (11, {})} | custom-call | tf_op jit(solution)/shard_map/pallas_call | solution.py:540
  41.0 0.0 collective-permute-done.8.refs_0_
  41.0 1.5 %shard_map.77 = (bf16[128,3584]{1,0:T(8,128)(2,1)}, f32[1,128]{1,0:T(1,128)}) custom-call(s32[4]{0:T(128)S(1)} %pad_add_fusion.place, bf16[128,256]{1,0:T(8,128)(2,1)S(1)} %get-tuple-element.34.kq, f32[128,3584]{1,0:T(8,128)S(1)} %get-tuple-element.43.local, f32[128,3584]{1,0:T(8,128)S(1)} %get-tuple-element.44.wide_growth, ...), custom_call_target="tpu_custom_call", output_to_operand_aliasing={{0}: (7, {})} | custom-call | tf_op jit(solution)/shard_map/pallas_call | solution.py:540
Async XLA Ops:
  0.6 12.4 %copy-start = (bf16[896,128]{1,0:T(8,128)(2,1)S(1)}, bf16[896,128]{1,0:T(8,128)(2,1)}, u32[]{:S(2)}) copy-start(bf16[896,128]{1,0:T(8,128)(2,1)} %refs_3_) | copy-start | bytes 688132
  0.6 17.9 %copy-start.1 = (f32[56]{0:T(128)S(1)}, f32[56]{0:T(128)}, u32[]{:S(2)}) copy-start(f32[56]{0:T(128)} %skip) | copy-start | bytes 676
  3.0 10.0 %collective-permute-start = (bf16[136,512]{1,0:T(8,128)(2,1)S(1)}, bf16[136,512]{1,0:T(8,128)(2,1)S(1)}, u32[]{:S(2)}, u32[]{:S(2)}) collective-permute-start(bf16[136,512]{1,0:T(8,128)(2,1)S(1)} %get-tuple-element.38), channel_id=1, source_target_pairs={{0,4},{4,0},{8,12},{12,8},{16,20},{20,16},{24,28},{28,24},{1,5},{5... | collective-permute-start | bytes 417800 | tf_op jit(solution)/shard_map/ppermute | solution.py:430
  6.0 7.0 %collective-permute-start.1 = (bf16[136,512]{1,0:T(8,128)(2,1)S(1)}, bf16[136,512]{1,0:T(8,128)(2,1)S(1)}, u32[]{:S(2)}, u32[]{:S(2)}) collective-permute-start(bf16[136,512]{1,0:T(8,128)(2,1)S(1)} %get-tuple-element.40), channel_id=1, source_target_pairs={{0,8},{4,12},{8,0},{12,4},{16,24},{20,28},{24,16},{28,20},{1,9},{5... | collective-permute-start | bytes 417800 | tf_op jit(solution)/shard_map/ppermute | solution.py:430
  7.6 7.6 %collective-permute-start.2 = (bf16[136,512]{1,0:T(8,128)(2,1)S(1)}, bf16[136,512]{1,0:T(8,128)(2,1)S(1)}, u32[]{:S(2)}, u32[]{:S(2)}) collective-permute-start(bf16[136,512]{1,0:T(8,128)(2,1)S(1)} %get-tuple-element.41), channel_id=1, source_target_pairs={{0,12},{4,8},{8,4},{12,0},{16,28},{20,24},{24,20},{28,16},{1,13},{... | collective-permute-start | bytes 417800 | tf_op jit(solution)/shard_map/ppermute | solution.py:430
  9.5 11.4 %collective-permute-start.3 = (bf16[144,384]{1,0:T(8,128)(2,1)S(1)}, bf16[144,384]{1,0:T(8,128)(2,1)S(1)}, u32[]{:S(2)}, u32[]{:S(2)}) collective-permute-start(bf16[144,384]{1,0:T(8,128)(2,1)S(1)} %get-tuple-element.47), channel_id=1, source_target_pairs={{0,4},{4,0},{8,12},{12,8},{16,20},{20,16},{24,28},{28,24},{1,5},{5... | collective-permute-start | bytes 331784 | tf_op jit(solution)/shard_map/ppermute | solution.py:430
  11.5 9.5 %collective-permute-start.4 = (bf16[144,384]{1,0:T(8,128)(2,1)S(1)}, bf16[144,384]{1,0:T(8,128)(2,1)S(1)}, u32[]{:S(2)}, u32[]{:S(2)}) collective-permute-start(bf16[144,384]{1,0:T(8,128)(2,1)S(1)} %get-tuple-element.48), channel_id=1, source_target_pairs={{0,8},{4,12},{8,0},{12,4},{16,24},{20,28},{24,16},{28,20},{1,9},{5... | collective-permute-start | bytes 331784 | tf_op jit(solution)/shard_map/ppermute | solution.py:430
  13.1 7.9 %collective-permute-start.5 = (bf16[144,384]{1,0:T(8,128)(2,1)S(1)}, bf16[144,384]{1,0:T(8,128)(2,1)S(1)}, u32[]{:S(2)}, u32[]{:S(2)}) collective-permute-start(bf16[144,384]{1,0:T(8,128)(2,1)S(1)} %get-tuple-element.49), channel_id=1, source_target_pairs={{0,12},{4,8},{8,4},{12,0},{16,28},{20,24},{24,20},{28,16},{1,13},{... | collective-permute-start | bytes 331784 | tf_op jit(solution)/shard_map/ppermute | solution.py:430
  13.1 17.0 %collective-permute-start.11 = (bf16[896,128]{1,0:T(8,128)(2,1)S(1)}, bf16[896,128]{1,0:T(8,128)(2,1)S(1)}, u32[]{:S(2)}, u32[]{:S(2)}) collective-permute-start(bf16[896,128]{1,0:T(8,128)(2,1)S(1)} %copy-done), channel_id=1, source_target_pairs={{0,2},{1,3},{2,0},{3,1},{4,6},{5,7},{6,4},{7,5},{8,10},{9,11},{10,... | collective-permute-start | bytes 688136 | tf_op jit(solution)/shard_map/ppermute | solution.py:430
  15.8 10.0 %collective-permute-start.6 = (bf16[128,512]{1,0:T(8,128)(2,1)S(1)}, bf16[128,512]{1,0:T(8,128)(2,1)S(1)}, u32[]{:S(2)}, u32[]{:S(2)}) collective-permute-start(bf16[128,512]{1,0:T(8,128)(2,1)S(1)} %shard_map.69.refs_0_), channel_id=1, source_target_pairs={{0,16},{4,20},{8,24},{12,28},{16,0},{20,4},{24,8},{28,12},{1,17},{... | collective-permute-start | bytes 393224 | tf_op jit(solution)/shard_map/ppermute | solution.py:430
  21.9 8.2 %collective-permute-start.7 = (bf16[160,384]{1,0:T(8,128)(2,1)S(1)}, bf16[160,384]{1,0:T(8,128)(2,1)S(1)}, u32[]{:S(2)}, u32[]{:S(2)}) collective-permute-start(bf16[160,384]{1,0:T(8,128)(2,1)S(1)} %shard_map.72.refs_1_), channel_id=1, source_target_pairs={{0,16},{4,20},{8,24},{12,28},{16,0},{20,4},{24,8},{28,12},{1,17},{... | collective-permute-start | bytes 368648 | tf_op jit(solution)/shard_map/ppermute | solution.py:430
  26.5 6.2 %collective-permute-start.15 = (bf16[128,512]{1,0:T(8,128)(2,1)S(1)}, bf16[128,512]{1,0:T(8,128)(2,1)S(1)}, u32[]{:S(2)}, u32[]{:S(2)}) collective-permute-start(bf16[128,512]{1,0:T(8,128)(2,1)S(1)} %get-tuple-element.56), channel_id=1, source_target_pairs={{0,4},{4,0},{8,12},{12,8},{16,20},{20,16},{24,28},{28,24},{1,5},{5... | collective-permute-start | bytes 393224 | tf_op jit(solution)/shard_map/ppermute | solution.py:430
  28.3 5.5 %collective-permute-start.16 = (bf16[128,512]{1,0:T(8,128)(2,1)S(1)}, bf16[128,512]{1,0:T(8,128)(2,1)S(1)}, u32[]{:S(2)}, u32[]{:S(2)}) collective-permute-start(bf16[128,512]{1,0:T(8,128)(2,1)S(1)} %get-tuple-element.57), channel_id=1, source_target_pairs={{0,8},{4,12},{8,0},{12,4},{16,24},{20,28},{24,16},{28,20},{1,9},{5... | collective-permute-start | bytes 393224 | tf_op jit(solution)/shard_map/ppermute | solution.py:430
  29.1 5.9 %collective-permute-start.14 = (bf16[128,512]{1,0:T(8,128)(2,1)S(1)}, bf16[128,512]{1,0:T(8,128)(2,1)S(1)}, u32[]{:S(2)}, u32[]{:S(2)}) collective-permute-start(bf16[128,512]{1,0:T(8,128)(2,1)S(1)} %get-tuple-element.58), channel_id=1, source_target_pairs={{0,12},{4,8},{8,4},{12,0},{16,28},{20,24},{24,20},{28,16},{1,13},{... | collective-permute-start | bytes 393224 | tf_op jit(solution)/shard_map/ppermute | solution.py:430
  30.1 9.4 %collective-permute-start.12 = (bf16[896,128]{1,0:T(8,128)(2,1)S(1)}, bf16[896,128]{1,0:T(8,128)(2,1)S(1)}, u32[]{:S(2)}, u32[]{:S(2)}) collective-permute-start(bf16[896,128]{1,0:T(8,128)(2,1)S(1)} %copy-done), channel_id=1, source_target_pairs={{0,1},{1,0},{2,3},{3,2},{4,5},{5,4},{6,7},{7,6},{8,9},{9,8},{10,11... | collective-permute-start | bytes 688136 | tf_op jit(solution)/shard_map/ppermute | solution.py:430
  30.1 9.3 %collective-permute-start.13 = (bf16[896,128]{1,0:T(8,128)(2,1)S(1)}, bf16[896,128]{1,0:T(8,128)(2,1)S(1)}, u32[]{:S(2)}, u32[]{:S(2)}) collective-permute-start(bf16[896,128]{1,0:T(8,128)(2,1)S(1)} %collective-permute-done.11.refs_5_), channel_id=1, source_target_pairs={{0,1},{1,0},{2,3},{3,2},{4,5},{5,4},{6,7},{7,6},{8,9},{9,8},{10,11... | collective-permute-start | bytes 688136 | tf_op jit(solution)/shard_map/ppermute | solution.py:430
  32.8 6.0 %collective-permute-start.9 = (bf16[152,384]{1,0:T(8,128)(2,1)S(1)}, bf16[152,384]{1,0:T(8,128)(2,1)S(1)}, u32[]{:S(2)}, u32[]{:S(2)}) collective-permute-start(bf16[152,384]{1,0:T(8,128)(2,1)S(1)} %get-tuple-element.52), channel_id=1, source_target_pairs={{0,4},{4,0},{8,12},{12,8},{16,20},{20,16},{24,28},{28,24},{1,5},{5... | collective-permute-start | bytes 350216 | tf_op jit(solution)/shard_map/ppermute | solution.py:430
  33.8 5.6 %collective-permute-start.10 = (bf16[152,384]{1,0:T(8,128)(2,1)S(1)}, bf16[152,384]{1,0:T(8,128)(2,1)S(1)}, u32[]{:S(2)}, u32[]{:S(2)}) collective-permute-start(bf16[152,384]{1,0:T(8,128)(2,1)S(1)} %get-tuple-element.53), channel_id=1, source_target_pairs={{0,8},{4,12},{8,0},{12,4},{16,24},{20,28},{24,16},{28,20},{1,9},{5... | collective-permute-start | bytes 350216 | tf_op jit(solution)/shard_map/ppermute | solution.py:430
  35.0 6.0 %collective-permute-start.8 = (bf16[152,384]{1,0:T(8,128)(2,1)S(1)}, bf16[152,384]{1,0:T(8,128)(2,1)S(1)}, u32[]{:S(2)}, u32[]{:S(2)}) collective-permute-start(bf16[152,384]{1,0:T(8,128)(2,1)S(1)} %get-tuple-element.50), channel_id=1, source_target_pairs={{0,12},{4,8},{8,4},{12,0},{16,28},{20,24},{24,20},{28,16},{1,13},{... | collective-permute-start | bytes 350216 | tf_op jit(solution)/shard_map/ppermute | solution.py:430
